TPU v7x, 256 devices: a whole 4x4x8 slice. The times are simulated.
256 devices in a mesh: section: 16 (over x_lo, y, core), dp: 16 (over x_hi, z).
Axes of the slice: x: 4 (x_hi: 2, x_lo: 2; x = x_hi * 2 + x_lo), y: 4, z: 8, core: 2. Of those that a mesh axis runs over, the one named last changes fastest.
Arguments:
- inputs: bfloat16 [2, 8, 128, 12288], P(None, None, 'dp'), may hold values from -6 to 6
- down_proj: bfloat16 [16, 24, 12288], P('section'), may hold values from -0.0546875 to 0.0546875
- up_proj: bfloat16 [16, 24, 12288], P('section'), may hold values from -1.25 to 1.25
Outputs:
- grad_down_proj: float32 [16, 24, 12288], P('section', None, 'dp')
- grad_up_proj: float32 [16, 24, 12288], P('section', None, 'dp')
All inputs are finite; a program needn't handle non-finite values.
Results may differ from a plain program's by a relative error of at most 0.0075.
Values may be sent and summed in bfloat16 or wider, within the bound.
No kernel may reach another device: no remote copies, remote signals or barrier semaphores. Data moves between devices by JAX's collectives and lax.ppermute only.
A program may use at most 64 MiB of HBM per device.

v0:
```python
import jax
import jax.numpy as jnp
from jax import lax
from jax.sharding import PartitionSpec as P

EPS = 1e-05


def swapped(block, axis, stride):
    count = lax.axis_size(axis)
    route = []
    for low in range(count):
        high = low | 1 << stride
        if high != low and high < count:
            route += [(low, high), (high, low)]
    return lax.ppermute(block, axis, route)


def passed_along(block, axis, distance):
    devices = range(lax.axis_size(axis))
    route = [(i - distance, i) for i in devices if i - distance in devices]
    return lax.ppermute(block, axis, route)


def contract_features(first_operand, second_operand):
    return lax.dot_general(
        first_operand, second_operand, (((1,), (1,)), ((), ())), preferred_element_type=jnp.float32
    )


def contract_rows(first_operand, second_operand):
    return lax.dot_general(
        first_operand, second_operand, (((0,), (0,)), ((), ())), preferred_element_type=jnp.float32
    )


def layer_forward(hidden, proj_down, proj_up):
    hidden_f = hidden.astype(jnp.float32)
    inv_rms = lax.rsqrt(jnp.mean(hidden_f * hidden_f, axis=-1, keepdims=True) + EPS)
    normed = (hidden_f * inv_rms).astype(jnp.bfloat16)
    pre_act = contract_features(normed, proj_down)
    gated_act = jax.nn.silu(pre_act).astype(jnp.bfloat16)
    return (hidden_f + jnp.dot(gated_act, proj_up, preferred_element_type=jnp.float32)).astype(
        jnp.bfloat16
    )


def layer_gradients(hidden, gradient, proj_down, proj_up):
    hidden_f = hidden.astype(jnp.float32)
    inv_rms = lax.rsqrt(jnp.mean(hidden_f * hidden_f, axis=-1, keepdims=True) + EPS)
    normed = (hidden_f * inv_rms).astype(jnp.bfloat16)
    pre_act = contract_features(normed, proj_down)
    gated_act = jax.nn.silu(pre_act).astype(jnp.bfloat16)
    grad_gated = contract_features(gradient, proj_up)
    sigmoid_val = jax.nn.sigmoid(pre_act)
    grad_pre = (grad_gated * sigmoid_val * (1.0 + pre_act * (1.0 - sigmoid_val))).astype(
        jnp.bfloat16
    )
    grad_normed = jnp.dot(grad_pre, proj_down, preferred_element_type=jnp.float32)
    feature_count = hidden_f.shape[-1]
    inner_sum = jnp.sum(grad_normed * hidden_f, axis=-1, keepdims=True)
    grad_hidden = (
        inv_rms * grad_normed - hidden_f * (inv_rms * inv_rms * inv_rms) * inner_sum / feature_count
    )
    grad_in = (gradient.astype(jnp.float32) + grad_hidden).astype(jnp.bfloat16)
    return (grad_in, grad_pre, normed, gated_act)


def store_slot(buffer, pipe_index, slot, live_flag, value):
    return buffer.at[pipe_index, slot].set(jnp.where(live_flag, value, buffer[pipe_index, slot]))


def shards(inputs, down_proj, up_proj):
    sections = lax.axis_size("section")
    position = lax.axis_index("section")
    members = lax.axis_size("dp")
    levels = sections.bit_length() - 1
    micro_count = inputs.shape[1]
    row_count = inputs.shape[2]
    feature_count = inputs.shape[3]
    normalizer = float(micro_count * row_count * members)
    own_down = down_proj[0]
    own_up = up_proj[0]
    rank_count = own_down.shape[0]
    mirror_down, mirror_up = (own_down, own_up)
    for bit_level in range(levels):
        mirror_down, mirror_up = swapped((mirror_down, mirror_up), "section", bit_level)
    is_first = position == 0
    is_last = position == sections - 1
    ticks = sections + micro_count - 1
    zero_rows = jnp.zeros((row_count, feature_count), jnp.bfloat16)
    zero_narrow = jnp.zeros((row_count, rank_count), jnp.bfloat16)
    saved_rows = jnp.zeros((2, micro_count, row_count, feature_count), jnp.bfloat16)
    targets = jnp.zeros((2, micro_count, row_count, feature_count), jnp.bfloat16)
    pre_store = jnp.zeros((2, micro_count, row_count, rank_count), jnp.bfloat16)
    gated_store = jnp.zeros((2, micro_count, row_count, rank_count), jnp.bfloat16)

    def forward_tick(tick_index, loop_state):
        recv_down, recv_up, saved_rows, targets = loop_state
        batch_down = tick_index - position
        batch_up = tick_index - (sections - 1 - position)
        live_down = (batch_down >= 0) & (batch_down < micro_count)
        live_up = (batch_up >= 0) & (batch_up < micro_count)
        index_down = jnp.clip(batch_down, 0, micro_count - 1)
        index_up = jnp.clip(batch_up, 0, micro_count - 1)
        source_down = inputs[0, index_down]
        source_up = inputs[1, index_up]
        hidden_down = jnp.where(is_first, source_down, recv_down)
        hidden_up = jnp.where(is_last, source_up, recv_up)
        saved_rows = store_slot(saved_rows, 0, index_down, live_down, hidden_down)
        saved_rows = store_slot(saved_rows, 1, index_up, live_up, hidden_up)
        out_down = lax.cond(
            live_down, lambda: layer_forward(hidden_down, own_down, own_up), lambda: zero_rows
        )
        out_up = lax.cond(
            live_up, lambda: layer_forward(hidden_up, mirror_down, mirror_up), lambda: zero_rows
        )
        start_down = (
            (out_down.astype(jnp.float32) - source_down.astype(jnp.float32)) / normalizer
        ).astype(jnp.bfloat16)
        start_up = (
            (out_up.astype(jnp.float32) - source_up.astype(jnp.float32)) / normalizer
        ).astype(jnp.bfloat16)
        targets = store_slot(targets, 0, index_down, live_down & is_last, start_down)
        targets = store_slot(targets, 1, index_up, live_up & is_first, start_up)
        sent_down = passed_along(out_down, "section", 1)
        sent_up = passed_along(out_up, "section", -1)
        return (sent_down, sent_up, saved_rows, targets)

    forward_state = lax.fori_loop(
        0, ticks, forward_tick, (zero_rows, zero_rows, saved_rows, targets)
    )
    saved_rows = forward_state[2]
    targets = forward_state[3]
    empty_result = (zero_rows, zero_narrow, zero_rows, zero_narrow)

    def backward_tick(tick_index, loop_state):
        recv_down, recv_up, saved_rows, targets, pre_store, gated_store = loop_state
        batch_down = tick_index - (sections - 1 - position)
        batch_up = tick_index - position
        live_down = (batch_down >= 0) & (batch_down < micro_count)
        live_up = (batch_up >= 0) & (batch_up < micro_count)
        index_down = jnp.clip(batch_down, 0, micro_count - 1)
        index_up = jnp.clip(batch_up, 0, micro_count - 1)
        grad_down = jnp.where(is_last, targets[0, index_down], recv_down)
        grad_up = jnp.where(is_first, targets[1, index_up], recv_up)
        stored_down = saved_rows[0, index_down]
        stored_up = saved_rows[1, index_up]
        result_down = lax.cond(
            live_down,
            lambda: layer_gradients(stored_down, grad_down, own_down, own_up),
            lambda: empty_result,
        )
        result_up = lax.cond(
            live_up,
            lambda: layer_gradients(stored_up, grad_up, mirror_down, mirror_up),
            lambda: empty_result,
        )
        saved_rows = store_slot(saved_rows, 0, index_down, live_down, result_down[2])
        saved_rows = store_slot(saved_rows, 1, index_up, live_up, result_up[2])
        targets = store_slot(targets, 0, index_down, live_down, grad_down)
        targets = store_slot(targets, 1, index_up, live_up, grad_up)
        pre_store = store_slot(pre_store, 0, index_down, live_down, result_down[1])
        pre_store = store_slot(pre_store, 1, index_up, live_up, result_up[1])
        gated_store = store_slot(gated_store, 0, index_down, live_down, result_down[3])
        gated_store = store_slot(gated_store, 1, index_up, live_up, result_up[3])
        sent_down = passed_along(result_down[0], "section", -1)
        sent_up = passed_along(result_up[0], "section", 1)
        return (sent_down, sent_up, saved_rows, targets, pre_store, gated_store)

    backward_state = lax.fori_loop(
        0, ticks, backward_tick, (zero_rows, zero_rows, saved_rows, targets, pre_store, gated_store)
    )
    normed_all = backward_state[2].reshape(2, micro_count * row_count, feature_count)
    grads_all = backward_state[3].reshape(2, micro_count * row_count, feature_count)
    pre_all = backward_state[4].reshape(2, micro_count * row_count, rank_count)
    gated_all = backward_state[5].reshape(2, micro_count * row_count, rank_count)
    own_a = contract_rows(pre_all[0], normed_all[0])
    own_b = contract_rows(gated_all[0], grads_all[0])
    mirror_a = contract_rows(pre_all[1], normed_all[1])
    mirror_b = contract_rows(gated_all[1], grads_all[1])
    back_a, back_b = (mirror_a, mirror_b)
    for bit_level in range(levels):
        back_a, back_b = swapped((back_a, back_b), "section", bit_level)
    total_a = own_a + back_a
    total_b = own_b + back_b
    result_a, result_b = (
        lax.psum_scatter(total_a, "dp", scatter_dimension=1, tiled=True),
        lax.psum_scatter(total_b, "dp", scatter_dimension=1, tiled=True),
    )
    return (result_a[None], result_b[None])


def solution(mesh):
    placed = (P(None, None, "dp", None), P("section", None, None), P("section", None, None))
    return jax.shard_map(
        shards,
        mesh=mesh,
        in_specs=placed,
        out_specs=(P("section", None, "dp"), P("section", None, "dp")),
        check_vma=False,
    )
```

profile of v0, /device:TPU:1, one launch (start us, length us, event | category | flops | bytes accessed | tf_op | source)
XLA Modules:
  0.0 1990.6 jit_solution(656532622570240700)
XLA Ops:
  13.8 13.1 collective-permute-done.9
  28.1 11.5 collective-permute-done.5
  40.7 12.2 collective-permute-done.10
  54.1 11.4 collective-permute-done.6
  66.8 12.5 collective-permute-done.7
  83.3 466.2 %while.56 = (s32[]{:T(128)}, bf16[8,12288]{1,0:T(8,128)(2,1)S(1)}, bf16[8,12288]{1,0:T(8,128)(2,1)S(1)}, bf16[2,8,8,12288]{3,2,1,0:T(8,128)(2,1)}, bf16[2,8,8,12...) while((s32[]{:T(128)}, bf16[8,12288]{1,0:T(8,128)(2,1)S(1)}, ...), condition=%wide.region_9.10_spmd, body=%wide.region_0.9_spmd.sunk | while | flops 22611928 | bytes 11409169 | solution.py:130
  338.3 15.5 collective-permute-start
  552.1 912.9 %while.57 = (s32[]{:T(128)}, bf16[8,12288]{1,0:T(8,128)(2,1)}, bf16[8,12288]{1,0:T(8,128)(2,1)}, bf16[2,8,8,12288]{3,2,1,0:T(8,128)(2,1)}, bf16[2,8,8,12288]{3,2...) while((s32[]{:T(128)}, bf16[8,12288]{1,0:T(8,128)(2,1)}, ...), condition=%wide.region_21.22_spmd, body=%wide.region_10.21_spmd.sunk | while | flops 32840548 | bytes 27554488 | solution.py:171
  710.7 9.6 conditional.11
  908.4 11.2 collective-permute-start.3
  1047.5 15.5 collective-permute-start.3
  1099.0 11.6 collective-permute-start.3
  1142.6 11.6 collective-permute-start.3
  1227.1 11.6 collective-permute-start.3
  1311.7 11.6 collective-permute-start.3
  1396.2 11.6 collective-permute-start.3
  1472.0 25.2 %collective-permute-done.17 = f32[24,12288]{1,0:T(8,128)S(1)} collective-permute-done((f32[24,12288]{1,0:T(8,128)S(1)}, f32[24,12288]{1,0:T(8,128)S(1)}, u32[]{:S(2)}, u32[]{:S(2)}) %collective-permute-start.17) | collective-permute-done | bytes 1179680 | tf_op jit(solution)/shard_map/ppermute | solution.py:16
  1497.4 27.8 %collective-permute-done.18 = f32[24,12288]{1,0:T(8,128)S(1)} collective-permute-done((f32[24,12288]{1,0:T(8,128)S(1)}, f32[24,12288]{1,0:T(8,128)S(1)}, u32[]{:S(2)}, u32[]{:S(2)}) %collective-permute-start.18) | collective-permute-done | bytes 1179680 | tf_op jit(solution)/shard_map/ppermute | solution.py:16
  1525.2 20.3 %collective-permute-start.19 = (f32[24,12288]{1,0:T(8,128)S(1)}, f32[24,12288]{1,0:T(8,128)S(1)}, u32[]{:S(2)}, u32[]{:S(2)}) collective-permute-start(f32[24,12288]{1,0:T(8,128)S(1)} %collective-permute-done.18), channel_id=1, source_target_pairs={{0,128},{128,0},{16,144},{144,16},{32,160},{160,32},{48,176},{176,... | collective-permute-start | bytes 3538952 | tf_op jit(solution)/shard_map/ppermute | solution.py:16
  1551.6 18.1 collective-permute-done.19
  1576.2 21.7 %collective-permute-start.15 = (f32[24,12288]{1,0:T(8,128)S(1)}, f32[24,12288]{1,0:T(8,128)S(1)}, u32[]{:S(2)}, u32[]{:S(2)}) collective-permute-start(f32[24,12288]{1,0:T(8,128)S(1)} %collective-permute-done.14), channel_id=1, source_target_pairs={{0,128},{128,0},{16,144},{144,16},{32,160},{160,32},{48,176},{176,... | collective-permute-start | bytes 3538952 | tf_op jit(solution)/shard_map/ppermute | solution.py:16
  1597.9 24.3 %collective-permute-done.15 = f32[24,12288]{1,0:T(8,128)S(1)} collective-permute-done((f32[24,12288]{1,0:T(8,128)S(1)}, f32[24,12288]{1,0:T(8,128)S(1)}, u32[]{:S(2)}, u32[]{:S(2)}) %collective-permute-start.15) | collective-permute-done | bytes 1179680 | tf_op jit(solution)/shard_map/ppermute | solution.py:16
  1625.1 151.7 %reduce-scatter.5.cloned.1.call-done = f32[24,768]{1,0:T(8,128)} async-done(((f32[24,12288]{1,0:T(8,128)}), f32[24,768]{1,0:T(8,128)}) %reduce-scatter.5.cloned.1.call-update) | async-done | bytes 73744 | tf_op jit(solution)/shard_map/reduce_scatter | solution.py:189
  1776.7 207.0 %reduce-scatter.3.cloned.1.call-done = f32[24,768]{1,0:T(8,128)} async-done(((f32[24,12288]{1,0:T(8,128)}), f32[24,768]{1,0:T(8,128)}) %reduce-scatter.3.cloned.1.call-update) | async-done | bytes 73744 | tf_op jit(solution)/shard_map/reduce_scatter | solution.py:188
  (1225 shorter events, 1534.2 us)
Async XLA Ops:
  7.2 1769.6 %reduce-scatter.5.cloned.1.call-start = ((), (), s32[]{:S(2)}) async-start(), calls=%async_computation.3 | async-start | bytes 1253376 | tf_op jit(solution)/shard_map/reduce_scatter | solution.py:189
  13.2 26.3 %collective-permute-start.5 = (bf16[24,12288]{1,0:T(8,128)(2,1)S(1)}, bf16[24,12288]{1,0:T(8,128)(2,1)S(1)}, u32[]{:S(2)}, u32[]{:S(2)}) collective-permute-start(bf16[24,12288]{1,0:T(8,128)(2,1)S(1)} %collective-permute-done.4), channel_id=1, source_target_pairs={{0,32},{32,0},{16,48},{48,16},{64,96},{96,64},{80,112},{112,80},{1... | collective-permute-start | bytes 1769480 | tf_op jit(solution)/shard_map/ppermute | solution.py:16
  26.9 26.0 %collective-permute-start.10 = (bf16[24,12288]{1,0:T(8,128)(2,1)S(1)}, bf16[24,12288]{1,0:T(8,128)(2,1)S(1)}, u32[]{:S(2)}, u32[]{:S(2)}) collective-permute-start(bf16[24,12288]{1,0:T(8,128)(2,1)S(1)} %collective-permute-done.9), channel_id=1, source_target_pairs={{0,64},{64,0},{16,80},{80,16},{32,96},{96,32},{48,112},{112,48},{1... | collective-permute-start | bytes 1769480 | tf_op jit(solution)/shard_map/ppermute | solution.py:16
  39.6 26.0 %collective-permute-start.6 = (bf16[24,12288]{1,0:T(8,128)(2,1)S(1)}, bf16[24,12288]{1,0:T(8,128)(2,1)S(1)}, u32[]{:S(2)}, u32[]{:S(2)}) collective-permute-start(bf16[24,12288]{1,0:T(8,128)(2,1)S(1)} %collective-permute-done.5), channel_id=1, source_target_pairs={{0,64},{64,0},{16,80},{80,16},{32,96},{96,32},{48,112},{112,48},{1... | collective-permute-start | bytes 1769480 | tf_op jit(solution)/shard_map/ppermute | solution.py:16
  561.1 26.5 %collective-permute-start.3 = (bf16[8,12288]{1,0:T(8,128)(2,1)}, bf16[8,12288]{1,0:T(8,128)(2,1)}, u32[]{:S(2)}, u32[]{:S(2)}) collective-permute-start(bf16[8,12288]{1,0:T(8,128)(2,1)} %get-tuple-element.1236), channel_id=1, source_target_pairs={{0,16},{16,32},{32,48},{48,64},{64,80},{80,96},{96,112},{112,128},... | collective-permute-start | bytes 589832 | tf_op jit(solution)/shard_map/while/body/eval_jaxpr/ppermute | solution.py:22
  908.4 28.7 %collective-permute-start.3 = (bf16[8,12288]{1,0:T(8,128)(2,1)}, bf16[8,12288]{1,0:T(8,128)(2,1)}, u32[]{:S(2)}, u32[]{:S(2)}) collective-permute-start(bf16[8,12288]{1,0:T(8,128)(2,1)} %get-tuple-element.1236), channel_id=1, source_target_pairs={{0,16},{16,32},{32,48},{48,64},{64,80},{80,96},{96,112},{112,128},... | collective-permute-start | bytes 589832 | tf_op jit(solution)/shard_map/while/body/eval_jaxpr/ppermute | solution.py:22
  977.7 25.7 %collective-permute-start.3 = (bf16[8,12288]{1,0:T(8,128)(2,1)}, bf16[8,12288]{1,0:T(8,128)(2,1)}, u32[]{:S(2)}, u32[]{:S(2)}) collective-permute-start(bf16[8,12288]{1,0:T(8,128)(2,1)} %get-tuple-element.1236), channel_id=1, source_target_pairs={{0,16},{16,32},{32,48},{48,64},{64,80},{80,96},{96,112},{112,128},... | collective-permute-start | bytes 589832 | tf_op jit(solution)/shard_map/while/body/eval_jaxpr/ppermute | solution.py:22
  1047.5 33.0 %collective-permute-start.3 = (bf16[8,12288]{1,0:T(8,128)(2,1)}, bf16[8,12288]{1,0:T(8,128)(2,1)}, u32[]{:S(2)}, u32[]{:S(2)}) collective-permute-start(bf16[8,12288]{1,0:T(8,128)(2,1)} %get-tuple-element.1236), channel_id=1, source_target_pairs={{0,16},{16,32},{32,48},{48,64},{64,80},{80,96},{96,112},{112,128},... | collective-permute-start | bytes 589832 | tf_op jit(solution)/shard_map/while/body/eval_jaxpr/ppermute | solution.py:22
  1099.0 34.6 %collective-permute-start.3 = (bf16[8,12288]{1,0:T(8,128)(2,1)}, bf16[8,12288]{1,0:T(8,128)(2,1)}, u32[]{:S(2)}, u32[]{:S(2)}) collective-permute-start(bf16[8,12288]{1,0:T(8,128)(2,1)} %get-tuple-element.1236), channel_id=1, source_target_pairs={{0,16},{16,32},{32,48},{48,64},{64,80},{80,96},{96,112},{112,128},... | collective-permute-start | bytes 589832 | tf_op jit(solution)/shard_map/while/body/eval_jaxpr/ppermute | solution.py:22
  1142.6 34.5 %collective-permute-start.3 = (bf16[8,12288]{1,0:T(8,128)(2,1)}, bf16[8,12288]{1,0:T(8,128)(2,1)}, u32[]{:S(2)}, u32[]{:S(2)}) collective-permute-start(bf16[8,12288]{1,0:T(8,128)(2,1)} %get-tuple-element.1236), channel_id=1, source_target_pairs={{0,16},{16,32},{32,48},{48,64},{64,80},{80,96},{96,112},{112,128},... | collective-permute-start | bytes 589832 | tf_op jit(solution)/shard_map/while/body/eval_jaxpr/ppermute | solution.py:22
  1186.1 32.0 %collective-permute-start.3 = (bf16[8,12288]{1,0:T(8,128)(2,1)}, bf16[8,12288]{1,0:T(8,128)(2,1)}, u32[]{:S(2)}, u32[]{:S(2)}) collective-permute-start(bf16[8,12288]{1,0:T(8,128)(2,1)} %get-tuple-element.1236), channel_id=1, source_target_pairs={{0,16},{16,32},{32,48},{48,64},{64,80},{80,96},{96,112},{112,128},... | collective-permute-start | bytes 589832 | tf_op jit(solution)/shard_map/while/body/eval_jaxpr/ppermute | solution.py:22
  1227.1 34.5 %collective-permute-start.3 = (bf16[8,12288]{1,0:T(8,128)(2,1)}, bf16[8,12288]{1,0:T(8,128)(2,1)}, u32[]{:S(2)}, u32[]{:S(2)}) collective-permute-start(bf16[8,12288]{1,0:T(8,128)(2,1)} %get-tuple-element.1236), channel_id=1, source_target_pairs={{0,16},{16,32},{32,48},{48,64},{64,80},{80,96},{96,112},{112,128},... | collective-permute-start | bytes 589832 | tf_op jit(solution)/shard_map/while/body/eval_jaxpr/ppermute | solution.py:22
  1270.6 32.0 %collective-permute-start.3 = (bf16[8,12288]{1,0:T(8,128)(2,1)}, bf16[8,12288]{1,0:T(8,128)(2,1)}, u32[]{:S(2)}, u32[]{:S(2)}) collective-permute-start(bf16[8,12288]{1,0:T(8,128)(2,1)} %get-tuple-element.1236), channel_id=1, source_target_pairs={{0,16},{16,32},{32,48},{48,64},{64,80},{80,96},{96,112},{112,128},... | collective-permute-start | bytes 589832 | tf_op jit(solution)/shard_map/while/body/eval_jaxpr/ppermute | solution.py:22
  1311.7 34.6 %collective-permute-start.3 = (bf16[8,12288]{1,0:T(8,128)(2,1)}, bf16[8,12288]{1,0:T(8,128)(2,1)}, u32[]{:S(2)}, u32[]{:S(2)}) collective-permute-start(bf16[8,12288]{1,0:T(8,128)(2,1)} %get-tuple-element.1236), channel_id=1, source_target_pairs={{0,16},{16,32},{32,48},{48,64},{64,80},{80,96},{96,112},{112,128},... | collective-permute-start | bytes 589832 | tf_op jit(solution)/shard_map/while/body/eval_jaxpr/ppermute | solution.py:22
  1355.2 31.9 %collective-permute-start.3 = (bf16[8,12288]{1,0:T(8,128)(2,1)}, bf16[8,12288]{1,0:T(8,128)(2,1)}, u32[]{:S(2)}, u32[]{:S(2)}) collective-permute-start(bf16[8,12288]{1,0:T(8,128)(2,1)} %get-tuple-element.1236), channel_id=1, source_target_pairs={{0,16},{16,32},{32,48},{48,64},{64,80},{80,96},{96,112},{112,128},... | collective-permute-start | bytes 589832 | tf_op jit(solution)/shard_map/while/body/eval_jaxpr/ppermute | solution.py:22
  1396.2 34.5 %collective-permute-start.3 = (bf16[8,12288]{1,0:T(8,128)(2,1)}, bf16[8,12288]{1,0:T(8,128)(2,1)}, u32[]{:S(2)}, u32[]{:S(2)}) collective-permute-start(bf16[8,12288]{1,0:T(8,128)(2,1)} %get-tuple-element.1236), channel_id=1, source_target_pairs={{0,16},{16,32},{32,48},{48,64},{64,80},{80,96},{96,112},{112,128},... | collective-permute-start | bytes 589832 | tf_op jit(solution)/shard_map/while/body/eval_jaxpr/ppermute | solution.py:22
  1469.7 27.4 %collective-permute-start.17 = (f32[24,12288]{1,0:T(8,128)S(1)}, f32[24,12288]{1,0:T(8,128)S(1)}, u32[]{:S(2)}, u32[]{:S(2)}) collective-permute-start(f32[24,12288]{1,0:T(8,128)S(1)} %collective-permute-done.16), channel_id=1, source_target_pairs={{0,32},{32,0},{16,48},{48,16},{64,96},{96,64},{80,112},{112,80},{1... | collective-permute-start | bytes 3538952 | tf_op jit(solution)/shard_map/ppermute | solution.py:16
  1471.6 25.6 %collective-permute-start.12 = (f32[24,12288]{1,0:T(8,128)S(1)}, f32[24,12288]{1,0:T(8,128)S(1)}, u32[]{:S(2)}, u32[]{:S(2)}) collective-permute-start(f32[24,12288]{1,0:T(8,128)S(1)} %convolution_bitcast_fusion.2), channel_id=1, source_target_pairs={{0,16},{16,0},{32,48},{48,32},{64,80},{80,64},{96,112},{112,96},{1... | collective-permute-start | bytes 3538952 | tf_op jit(solution)/shard_map/ppermute | solution.py:16
  1497.2 28.0 %collective-permute-start.18 = (f32[24,12288]{1,0:T(8,128)S(1)}, f32[24,12288]{1,0:T(8,128)S(1)}, u32[]{:S(2)}, u32[]{:S(2)}) collective-permute-start(f32[24,12288]{1,0:T(8,128)S(1)} %collective-permute-done.17), channel_id=1, source_target_pairs={{0,64},{64,0},{16,80},{80,16},{32,96},{96,32},{48,112},{112,48},{1... | collective-permute-start | bytes 3538952 | tf_op jit(solution)/shard_map/ppermute | solution.py:16
  1497.2 51.1 %collective-permute-start.13 = (f32[24,12288]{1,0:T(8,128)S(1)}, f32[24,12288]{1,0:T(8,128)S(1)}, u32[]{:S(2)}, u32[]{:S(2)}) collective-permute-start(f32[24,12288]{1,0:T(8,128)S(1)} %collective-permute-done.12), channel_id=1, source_target_pairs={{0,32},{32,0},{16,48},{48,16},{64,96},{96,64},{80,112},{112,80},{1... | collective-permute-start | bytes 3538952 | tf_op jit(solution)/shard_map/ppermute | solution.py:16
  1525.2 44.5 %collective-permute-start.19 = (f32[24,12288]{1,0:T(8,128)S(1)}, f32[24,12288]{1,0:T(8,128)S(1)}, u32[]{:S(2)}, u32[]{:S(2)}) collective-permute-start(f32[24,12288]{1,0:T(8,128)S(1)} %collective-permute-done.18), channel_id=1, source_target_pairs={{0,128},{128,0},{16,144},{144,16},{32,160},{160,32},{48,176},{176,... | collective-permute-start | bytes 3538952 | tf_op jit(solution)/shard_map/ppermute | solution.py:16
  1548.3 27.9 %collective-permute-start.14 = (f32[24,12288]{1,0:T(8,128)S(1)}, f32[24,12288]{1,0:T(8,128)S(1)}, u32[]{:S(2)}, u32[]{:S(2)}) collective-permute-start(f32[24,12288]{1,0:T(8,128)S(1)} %collective-permute-done.13), channel_id=1, source_target_pairs={{0,64},{64,0},{16,80},{80,16},{32,96},{96,32},{48,112},{112,48},{1... | collective-permute-start | bytes 3538952 | tf_op jit(solution)/shard_map/ppermute | solution.py:16
  1572.5 411.2 %reduce-scatter.3.cloned.1.call-start = ((), (), s32[]{:S(2)}) async-start(), calls=%async_computation.2 | async-start | bytes 1253376 | tf_op jit(solution)/shard_map/reduce_scatter | solution.py:188
  1576.2 46.0 %collective-permute-start.15 = (f32[24,12288]{1,0:T(8,128)S(1)}, f32[24,12288]{1,0:T(8,128)S(1)}, u32[]{:S(2)}, u32[]{:S(2)}) collective-permute-start(f32[24,12288]{1,0:T(8,128)S(1)} %collective-permute-done.14), channel_id=1, source_target_pairs={{0,128},{128,0},{16,144},{144,16},{32,160},{160,32},{48,176},{176,... | collective-permute-start | bytes 3538952 | tf_op jit(solution)/shard_map/ppermute | solution.py:16
  (89 other events, 1387.8 us)
Sparse Core Ops, SparseCore 0:
  1572.6 204.0 reduce-scatter.4
  1781.6 202.0 reduce-scatter.2
where the time goes:
time: 2010 us; the launch traced here: 1990 us
  waiting for transfers between devices  541 us (27%)
  other arithmetic  532 us (26%)
  starting transfers between devices  438 us (22%)
  local copies, waits for them, and re-layouts  344 us (17%)
  matrix products  118 us (6%)
    scatter x230, other arithmetic, store_slot(): buffer.at[pipe_index, slot]  441 us
    ppermute x92, starting transfers between devices, passed_along(): return lax.ppermute(block, axis, route)  383 us
    reduce_scatter x1, waiting for transfers between devices, shards(): lax.psum_scatter(total_a, 'dp', scatter_dimension=1, tiled=True)  207 us
    ppermute x16, waiting for transfers between devices, swapped(): return lax.ppermute(block, axis, route)  168 us
    reduce_scatter x1, waiting for transfers between devices, shards(): lax.psum_scatter(total_b, 'dp', scatter_dimension=1, tiled=True)  152 us
    dynamic_slice x207, local copies, waits for them, and re-layouts, store_slot(): buffer[pipe_index, slot]  150 us
    while x46, local copies, waits for them, and re-layouts  82.2 us
    ppermute x16, starting transfers between devices, swapped(): return lax.ppermute(block, axis, route)  55 us
  transfers between devices with their start and end apart: 110, of which 18 were waited for; matrix products, arithmetic and copies ran while one was open for 25% of the time, Pallas kernels for 0%

commit v1 on v0

v1 whole, which is shorter than its diff:
```python
import jax
import jax.numpy as jnp
from jax import lax
from jax.experimental import pallas as pl
from jax.experimental.pallas import tpu as pltpu
from jax.sharding import PartitionSpec as P

EPS = 1e-05
LANES = 128
F32 = jnp.float32
BF16 = jnp.bfloat16


def split(value):
    high = value.astype(BF16)
    return high, (value - high.astype(F32)).astype(BF16)


def dot_nn(left, right):
    return lax.dot_general(left, right, (((1,), (0,)), ((), ())), preferred_element_type=F32)


def dot_nt(left, right):
    return lax.dot_general(left, right, (((1,), (1,)), ((), ())), preferred_element_type=F32)


def params():
    return pltpu.CompilerParams(vmem_limit_bytes=48 * 1024 * 1024)


def project_kernel(x_ref, down_ref, up_ref, both_ref, square_ref, acc_ref, sum_ref):
    step = pl.program_id(0)

    @pl.when(step == 0)
    def _():
        acc_ref[...] = jnp.zeros_like(acc_ref)
        sum_ref[...] = jnp.zeros_like(sum_ref)

    rows = x_ref[...]
    rank = down_ref.shape[0]
    acc_ref[0:rank] += dot_nt(down_ref[...], rows)
    acc_ref[rank : 2 * rank] += dot_nt(up_ref[...], rows)
    wide = rows.astype(F32)
    total = sum_ref[...]
    for tile in range(wide.shape[1] // LANES):
        part = wide[:, tile * LANES : (tile + 1) * LANES]
        total += part * part
    sum_ref[...] = total

    @pl.when(step == pl.num_programs(0) - 1)
    def _():
        high, low = split(acc_ref[...])
        both_ref[...] = jnp.concatenate([high, low], axis=1)
        square_ref[...] = jnp.sum(sum_ref[...].T, axis=0, keepdims=True)


def project(rows, down, up):
    count, features = rows.shape
    rank = down.shape[0]
    width = features // 8
    return pl.pallas_call(
        project_kernel,
        grid=(8,),
        in_specs=[
            pl.BlockSpec((count, width), lambda c: (0, c)),
            pl.BlockSpec((rank, width), lambda c: (0, c)),
            pl.BlockSpec((rank, width), lambda c: (0, c)),
        ],
        out_specs=[
            pl.BlockSpec((2 * rank, 2 * LANES), lambda c: (0, 0)),
            pl.BlockSpec((1, LANES), lambda c: (0, 0)),
        ],
        out_shape=[
            jax.ShapeDtypeStruct((2 * rank, 2 * LANES), BF16),
            jax.ShapeDtypeStruct((1, LANES), F32),
        ],
        scratch_shapes=[pltpu.VMEM((2 * rank, LANES), F32), pltpu.VMEM((LANES, LANES), F32)],
        compiler_params=params(),
    )(rows, down, up)


def pair_kernel(own_ref, other_ref, out_ref, pad_ref):
    rank = own_ref.shape[0]
    pad_ref[...] = jnp.zeros_like(pad_ref)
    pad_ref[:, 0:rank] = dot_nt(own_ref[...], other_ref[...])
    packed = pad_ref[0:8]
    for group in range(1, rank // 8):
        packed += pltpu.roll(pad_ref[8 * group : 8 * group + 8], rank * group, 1)
    for copy in range(out_ref.shape[0]):
        out_ref[copy] = packed


def pair_products(own, other, copies):
    rank = own.shape[0]
    return pl.pallas_call(
        pair_kernel,
        out_shape=jax.ShapeDtypeStruct((copies, 8, LANES), F32),
        scratch_shapes=[pltpu.VMEM((rank, LANES), F32)],
        compiler_params=params(),
    )(own, other)


def order_kernel(rank, blocks, in_ref, out_ref):
    position = lax.axis_index("section")
    lane = lax.broadcasted_iota(jnp.int32, (8, LANES), 1)
    tiles = rank * blocks // LANES
    pieces = [in_ref[position ^ t] for t in range(blocks)]
    for group in range(rank // 8):
        turned = [pltpu.roll(pieces[t], (rank * (t - group)) % LANES, 1) for t in range(blocks)]
        for tile in range(tiles):
            place = (lane + tile * LANES) // rank
            value = jnp.zeros((8, LANES), F32)
            for t in range(blocks):
                if rank * t < (tile + 1) * LANES and rank * (t + 1) > tile * LANES:
                    value = jnp.where(place == t, turned[t], value)
            for copy in range(out_ref.shape[0]):
                out_ref[copy, tile * rank + 8 * group : tile * rank + 8 * group + 8] = value


def order_blocks(gathered, rank, copies):
    blocks = gathered.shape[0]

    def kernel(in_ref, out_ref):
        order_kernel(rank, blocks, in_ref, out_ref)

    rows = rank * blocks // LANES * rank
    return pl.pallas_call(
        kernel,
        out_shape=jax.ShapeDtypeStruct((copies, rows, LANES), F32),
        compiler_params=params(),
    )(gathered)


def chain_kernel(rank, blocks, features, normalizer, grid_ref, proj_ref, square_ref, out_ref, *rest):
    plain_ref, turned_ref, act_ref, scaled_ref, grad_ref, skip_ref = rest
    size = rank * blocks
    tiles = size // LANES
    whole = jnp.concatenate(
        [
            jnp.concatenate(
                [grid_ref[b, tile * rank : (tile + 1) * rank] for tile in range(tiles)], axis=1
            )
            for b in range(blocks)
        ],
        axis=0,
    )
    for ref, value in ((plain_ref, whole), (turned_ref, whole.T)):
        high, low = split(value)
        for tile in range(tiles):
            ref[:, 2 * tile * LANES : (2 * tile + 1) * LANES] = high[:, tile * LANES : (tile + 1) * LANES]
            ref[:, (2 * tile + 1) * LANES : (2 * tile + 2) * LANES] = low[
                :, tile * LANES : (tile + 1) * LANES
            ]

    def span(b):
        first = rank * b // LANES
        last = (rank * b + rank - 1) // LANES
        return first, last

    def columns(ref, b, start, stop):
        first, last = span(b)
        return ref[start:stop, 2 * first * LANES : 2 * (last + 1) * LANES]

    def placed(b, value):
        first, last = span(b)
        before = rank * b - first * LANES
        after = (last + 1) * LANES - rank * (b + 1)
        parts = []
        if before:
            parts.append(jnp.zeros((before, LANES), F32))
        parts.append(value)
        if after:
            parts.append(jnp.zeros((after, LANES), F32))
        wide = jnp.concatenate(parts, axis=0).astype(BF16)
        doubled = []
        for tile in range(last - first + 1):
            doubled += [wide[tile * LANES : (tile + 1) * LANES]] * 2
        return jnp.concatenate(doubled, axis=0)

    narrow, hidden = [], []
    for b in range(blocks):
        pair = proj_ref[b].astype(F32)
        joined = pair[:, 0:LANES] + pair[:, LANES : 2 * LANES]
        narrow.append(joined[0:rank])
        hidden.append(joined[rank : 2 * rank])
    initial = list(hidden)
    square = square_ref[...]
    inverses, acts, pres, slopes, ends = [], [], [], [], []
    for b in range(blocks):
        inverse = lax.rsqrt(square / features + EPS)
        pre = narrow[b] * inverse
        sigmoid = 1.0 / (1.0 + jnp.exp(-pre))
        act = (pre * sigmoid).astype(BF16).astype(F32)
        act_ref[rank * b : rank * (b + 1)] = act
        inverses.append(inverse)
        acts.append(act)
        pres.append(pre)
        slopes.append(sigmoid * (1.0 + pre * (1.0 - sigmoid)))
        right = placed(b, act)
        if b + 1 < blocks:
            start = rank * (b + 1) // 16 * 16
            update = dot_nn(columns(turned_ref, b, start, size), right)
            for k in range(b + 1, blocks):
                narrow[k] = narrow[k] + update[rank * k - start : rank * (k + 1) - start]
        start = rank * b // 16 * 16
        update = dot_nn(columns(plain_ref, b, start, size), right)
        own = update[rank * b - start : rank * (b + 1) - start]
        for k in range(b + 1, blocks):
            hidden[k] = hidden[k] + update[rank * k - start : rank * (k + 1) - start]
        square = square + jnp.sum(act * (2.0 * hidden[b] + own), axis=0, keepdims=True)
        ends.append(hidden[b] + own)

    back = [jnp.zeros((rank, LANES), F32) for _ in range(blocks)]
    decay = jnp.zeros((1, LANES), F32)
    for k in reversed(range(blocks)):
        weight = 1.0 / normalizer - decay
        scaled = acts[k] * weight
        scaled_ref[rank * k : rank * (k + 1)] = scaled
        skip_ref[rank * k : rank * (k + 1)] = -decay * acts[k]
        incoming = ends[k] * weight - initial[k] / normalizer + back[k]
        grad = (incoming * slopes[k] * inverses[k]).astype(BF16).astype(F32)
        grad_ref[rank * k : rank * (k + 1)] = grad
        decay = decay + inverses[k] / features * jnp.sum(grad * pres[k], axis=0, keepdims=True)
        if k:
            stop = -(-rank * k // 16) * 16
            coarse = scaled.astype(BF16).astype(F32)
            fine = scaled - coarse
            update = (
                dot_nn(columns(turned_ref, k, 0, stop), placed(k, coarse))
                + dot_nn(columns(turned_ref, k, 0, stop), placed(k, fine))
                + dot_nn(columns(plain_ref, k, 0, stop), placed(k, grad))
            )
            for b in range(k):
                back[b] = back[b] + update[rank * b : rank * (b + 1)]

    position = lax.axis_index("section")
    mine = pl.ds(pl.multiple_of(position * rank, 8), rank)
    own_act = act_ref[mine].astype(BF16)
    own_high, own_low = split(scaled_ref[mine])
    own_grad = grad_ref[mine].astype(BF16)
    all_act = act_ref[...].astype(BF16)
    all_high, all_low = split(scaled_ref[...])
    all_grad = grad_ref[...].astype(BF16)
    place = lax.broadcasted_iota(jnp.int32, (rank, size), 1) // rank
    later = dot_nt(own_act, all_high) + dot_nt(own_act, all_low)
    earlier = dot_nt(own_high, all_act) + dot_nt(own_low, all_act)
    both_up = jnp.where(place >= position, later, earlier)
    crossed = jnp.where(
        place < position,
        dot_nt(own_grad, all_act),
        jnp.where(place > position, dot_nt(own_act, all_grad), 0.0),
    )
    pieces = [grad_ref[mine], skip_ref[mine]]
    for value in (both_up, crossed):
        pieces += [value[:, tile * LANES : (tile + 1) * LANES] for tile in range(tiles)]
    payload = jnp.concatenate(pieces, axis=0).astype(BF16)
    for copy in range(out_ref.shape[0]):
        out_ref[copy] = payload


def run_chain(grid, gathered, square, rank, features, normalizer, copies):
    blocks = grid.shape[0]
    size = rank * blocks
    rows = 2 * rank + 2 * (size // LANES) * rank

    def kernel(*refs):
        chain_kernel(rank, blocks, features, normalizer, *refs)

    last = gathered.shape[2] // (2 * LANES) - 1
    narrow = pltpu.VMEM((size, LANES), F32)
    return pl.pallas_call(
        kernel,
        grid=(1,),
        in_specs=[
            pl.BlockSpec(grid.shape, lambda i: (0, 0, 0)),
            pl.BlockSpec((blocks, 2 * rank, 2 * LANES), lambda i: (0, 0, last)),
            pl.BlockSpec((1, LANES), lambda i: (0, 0)),
        ],
        out_specs=pl.BlockSpec((copies, rows, LANES), lambda i: (0, 0, 0)),
        out_shape=jax.ShapeDtypeStruct((copies, rows, LANES), BF16),
        scratch_shapes=[
            pltpu.VMEM((size, 2 * size), BF16),
            pltpu.VMEM((size, 2 * size), BF16),
            narrow,
            narrow,
            narrow,
            narrow,
        ],
        compiler_params=params(),
    )(grid, gathered, square)


def finish_kernel(rank, blocks, parts_ref, rows_ref, weights_ref, down_ref, up_ref):
    size = rank * blocks
    tiles = size // LANES
    members = parts_ref.shape[0]
    position = lax.axis_index("section")
    total = None
    left = []
    for member in range(members):
        piece = parts_ref[member]
        left.append(piece[0 : 2 * rank])
        sums = piece.astype(F32)[2 * rank :]
        total = sums if total is None else total + sums

    def unfold(first):
        return jnp.concatenate(
            [total[(first + tile) * rank : (first + tile + 1) * rank] for tile in range(tiles)], axis=1
        )

    both_up, crossed = unfold(0), unfold(tiles)
    place = lax.broadcasted_iota(jnp.int32, (rank, size), 1) // rank
    below = jnp.where(place < position, crossed, 0.0)
    above = jnp.where(place > position, crossed, 0.0)
    weights = [weights_ref[b].astype(F32) for b in range(blocks)]
    all_down = jnp.concatenate([w[0:rank] for w in weights], axis=0).astype(BF16)
    all_up = jnp.concatenate([w[rank : 2 * rank] for w in weights], axis=0).astype(BF16)
    result = jnp.zeros((2 * rank, rows_ref.shape[2]), F32)
    for member in range(members):
        result += dot_nn(left[member], rows_ref[member])
    high, low = split(jnp.concatenate([below, both_up], axis=0))
    result += dot_nn(high, all_up) + dot_nn(low, all_up)
    high, low = split(above)
    cross = dot_nn(high, all_down) + dot_nn(low, all_down)
    down_ref[0] = result[0:rank]
    up_ref[0] = result[rank : 2 * rank] + cross


def finish(parts, rows, gathered, rank):
    blocks = gathered.shape[0]
    width = rows.shape[2]

    def kernel(*refs):
        finish_kernel(rank, blocks, *refs)

    shape = jax.ShapeDtypeStruct((1, rank, width), F32)
    out = pl.BlockSpec((1, rank, width), lambda i: (0, 0, 0))
    return pl.pallas_call(
        kernel,
        grid=(1,),
        in_specs=[
            pl.BlockSpec(parts.shape, lambda i: (0, 0, 0)),
            pl.BlockSpec(rows.shape, lambda i: (0, 0, 0)),
            pl.BlockSpec((blocks, 2 * rank, width), lambda i: (0, 0, 0)),
        ],
        out_specs=[out, out],
        out_shape=[shape, shape],
        compiler_params=params(),
    )(parts, rows, gathered)


def shards(inputs, down_proj, up_proj):
    sections = lax.axis_size("section")
    members = lax.axis_size("dp")
    position = lax.axis_index("section")
    member = lax.axis_index("dp")
    own_down, own_up = down_proj[0], up_proj[0]
    rank, features = own_down.shape
    width = features // members
    pipes, micro, count = inputs.shape[:3]
    normalizer = float(micro * count * members)
    all_rows = inputs.reshape(pipes * micro * count, features)

    route = [
        ((s ^ d) * members + d, s * members + d) for s in range(sections) for d in range(members)
    ]
    outgoing = jnp.where((position ^ member) >= position, own_up, own_down)
    other = lax.ppermute(outgoing, ("section", "dp"), route)

    share = lax.dynamic_index_in_dim(
        inputs.reshape(sections, count, features), position, 0, keepdims=False
    )
    share = share.reshape(count, members, width).transpose(1, 0, 2)
    share = lax.all_to_all(share, "dp", 0, 0)
    slices = lax.all_gather(share, "section")
    slices = slices.transpose(1, 0, 2, 3).reshape(members, sections * count, width)

    both, square = project(all_rows, own_down, own_up)
    own_slice = jnp.concatenate(
        [lax.dynamic_slice_in_dim(w, member * width, width, 1) for w in (own_down, own_up)], axis=0
    )
    gathered = lax.all_gather(jnp.concatenate([own_slice, both], axis=1), "section")

    products = lax.all_to_all(pair_products(own_up, other, members), "dp", 0, 0)
    grid = lax.all_to_all(order_blocks(products, rank, sections), "section", 0, 0)
    parts = run_chain(grid, gathered, square, rank, features, normalizer, members)
    parts = lax.all_to_all(parts, "dp", 0, 0)
    return finish(parts, slices, gathered, rank)


def solution(mesh):
    placed = (P(None, None, "dp", None), P("section", None, None), P("section", None, None))
    return jax.shard_map(
        shards,
        mesh=mesh,
        in_specs=placed,
        out_specs=(P("section", None, "dp"), P("section", None, "dp")),
        check_vma=False,
    )
```

time: 2010 us -> 142 us (0.07)
  other arithmetic: 532 us -> 0.71 us
  waiting for transfers between devices: 541 us -> 18.9 us
  starting transfers between devices: 438 us -> 5.07 us
  local copies, waits for them, and re-layouts: 344 us -> 10.8 us
  matrix products: 118 us -> 0 us
  blocking collectives: 0 us -> 76.8 us
    scatter x230 -> x0, other arithmetic: 441 us -> none  [store_slot(): buffer.at[pipe_index, slot]]
    ppermute x108 -> x1, starting transfers between devices: 438 us -> 0.7 us  [shards(): other = lax.ppermute(outgoing, ('section', 'dp'), route)]
    reduce_scatter x2 -> x0, waiting for transfers between devices: 359 us -> none  [the longest x1 207 us: shards(): lax.psum_scatter(total_a, 'dp', scatter_dimension=1, tiled=True)]
    ppermute x108 -> x1, waiting for transfers between devices: 182 us -> 0.01 us  [shards(): other = lax.ppermute(outgoing, ('section', 'dp'), route)]
    dynamic_slice x230 -> x2, local copies, waits for them, and re-layouts: 172 us -> 1.74 us  [the longest x1 0.94 us: shards(): lax.dynamic_index_in_dim(inputs.reshape(sections, count, features), posit...]
    dot_general x68 -> x0, matrix products: 118 us -> none  [the longest x32 54.7 us: contract_features(): lax.dot_general(first_operand, second_operand, (((1,), (1,)), ((), ())),...]
    while x46 -> x0, local copies, waits for them, and re-layouts: 82.2 us -> none
    all_to_all x0 -> x3, blocking collectives: none -> 76.8 us  [the longest x1 36.5 us: shards(): products = lax.all_to_all(pair_products(own_up, other, members), 'dp', 0, 0)]
  transfers between devices with their start and end apart: 110 -> 4, of which waited for: 18 -> 2; matrix products, arithmetic and copies ran while one was open for 25% -> 2% of each run, Pallas kernels for 0% -> 6%
where the time goes in v1:
time: 142 us; the launch traced here: 140 us
  blocking collectives  76.8 us (54%)
  waiting for transfers between devices  18.9 us (13%)
  between operations  14.1 us (10%)
  Pallas kernels  13.9 us (10%)
  local copies, waits for them, and re-layouts  10.8 us (8%)
  starting transfers between devices  5.07 us (4%)
    all_to_all x1, blocking collectives, shards(): products = lax.all_to_all(pair_products(own_up, other, members), 'dp', 0, 0)  36.5 us
    all_to_all x1, blocking collectives, shards(): share = lax.all_to_all(share, 'dp', 0, 0)  20.5 us
    all_to_all x1, blocking collectives, shards(): lax.all_to_all(order_blocks(products, rank, sections), 'section', 0, 0)  19.7 us
    all_to_all x1, waiting for transfers between devices, shards(): parts = lax.all_to_all(parts, 'dp', 0, 0)  12.6 us
    pallas_call x1, Pallas kernels, run_chain(): pl.pallas_call(kernel, grid=(1,), in_specs=[pl.BlockSpec(grid.shape, lamb...  7.31 us
    unnamed x14, local copies, waits for them, and re-layouts  6.87 us
    all_gather x1, waiting for transfers between devices, shards(): slices = lax.all_gather(share, 'section')  6.22 us
    all_to_all x1, starting transfers between devices, shards(): parts = lax.all_to_all(parts, 'dp', 0, 0)  4.29 us
  transfers between devices with their start and end apart: 4, of which 2 were waited for; matrix products, arithmetic and copies ran while one was open for 2% of the time, Pallas kernels for 6%

profile of v1, /device:TPU:1, one launch (start us, length us, event | category | flops | bytes accessed | tf_op | source)
XLA Modules:
  0.0 140.2 jit_solution(15395240382391002497)
XLA Ops:
  7.2 0.0 all-gather.5.cloned.1.call-start
  7.2 0.8 dynamic-slice_bitcast_fusion
  8.0 1.1 copy-done.2
  9.1 1.9 %copy-done.4 = bf16[2,8,8,12288]{3,2,1,0:T(8,128)(2,1)S(1)} copy-done((bf16[2,8,8,12288]{3,2,1,0:T(8,128)(2,1)S(1)}, bf16[2,8,8,12288]{3,2,1,0:T(8,128)(2,1)}, u32[]{:S(2)}) %copy-start.4) | copy-done | bytes 3145752
  11.0 1.1 copy-done.5
  12.0 3.3 %shard_map.52 = (bf16[48,256]{1,0:T(8,128)(2,1)S(1)}, f32[1,128]{1,0:T(1,128)S(1)}) custom-call(bf16[128,12288]{1,0:T(8,128)(2,1)S(1)} %bitcast.26, bf16[24,12288]{1,0:T(8,128)(2,1)S(1)} %bitcast.27, bf16[24,12288]{1,0:T(8,128)(2,1)S(1)} %bitcast.23), custom_call_target="tpu_custom_call" | custom-call | tf_op jit(solution)/shard_map/pallas_call | solution.py:61
  15.4 0.6 pad_maximum_fusion
  16.1 0.0 all-gather.7.cloned.1.call-start
  16.1 0.9 constant_dynamic-slice_fusion
  17.1 20.5 %all_to_all.20 = bf16[16,8,768]{2,1,0:T(8,128)(2,1)} all-to-all(bf16[16,8,768]{2,1,0:T(8,128)(2,1)S(1)} %bitcast.29), channel_id=1, replica_groups=mesh['section'=16,'dp'=16] {'dp'}, dimensions={0} | all-to-all | bytes 393216 | tf_op jit(solution)/shard_map/all_to_all | solution.py:374
  37.6 0.1 broadcast_select_fusion
  37.7 0.7 collective-permute-start
  38.4 0.4 shard_map.50
  38.8 36.5 %all_to_all.21.in_ref = f32[16,8,128]{2,1,0:T(8,128)S(1)} all-to-all(f32[16,8,128]{2,1,0:T(8,128)S(1)} %shard_map.50), channel_id=1, replica_groups=mesh['section'=16,'dp'=16] {'dp'}, dimensions={0} | all-to-all | bytes 131072 | tf_op jit(solution)/shard_map/all_to_all | solution.py:384
  75.4 0.1 shard_map.51
  75.5 19.7 %all_to_all.22.refs_0_ = f32[16,72,128]{2,1,0:T(8,128)S(1)} all-to-all(f32[16,72,128]{2,1,0:T(8,128)S(1)} %shard_map.51), channel_id=1, replica_groups=mesh['section'=16,'dp'=16] {'section'}, dimensions={0} | all-to-all | bytes 1179648 | tf_op jit(solution)/shard_map/all_to_all | solution.py:385
  95.2 1.4 %copy-done = bf16[768,1024]{1,0:T(8,128)(2,1)S(1)} copy-done((bf16[768,1024]{1,0:T(8,128)(2,1)S(1)}, bf16[768,1024]{1,0:T(8,128)(2,1)}, u32[]{:S(2)}) %copy-start) | copy-done | bytes 1572888
  96.6 7.3 %shard_map.53 = bf16[16,192,128]{2,1,0:T(8,128)(2,1)} custom-call(f32[16,72,128]{2,1,0:T(8,128)S(1)} %all_to_all.22.refs_0_, bf16[16,48,1024]{2,1,0:T(8,128)(2,1)S(1)} %bitcast.21, f32[1,128]{1,0:T(1,128)S(1)} %get-tuple-element.5.refs_2_), custom_call_target="tpu_custom_call" | custom-call | tf_op jit(solution)/shard_map/pallas_call | solution.py:271
  104.0 4.3 %all-to-all-start.2 = ((bf16[16,192,128]{2,1,0:T(8,128)(2,1)}), bf16[16,192,128]{2,1,0:T(8,128)(2,1)}, u32[]{:S(2)}, u32[]{:S(2)}) async-start(bf16[16,192,128]{2,1,0:T(8,128)(2,1)} %shard_map.53), calls=%async_computation.2 | async-start | bytes 1572864 | tf_op jit(solution)/shard_map/all_to_all | solution.py:387
  108.3 6.2 %all-gather.7.cloned.1.call-done = bf16[256,8,768]{2,1,0:T(8,128)(2,1)} async-done(((bf16[16,8,768]{2,1,0:T(8,128)(2,1)}), bf16[256,8,768]{2,1,0:T(8,128)(2,1)}) %all-gather.7.cloned.1.call-update) | async-done | bytes 3145744 | tf_op jit(solution)/shard_map/all_gather | solution.py:375
  114.5 2.2 %copy.8 = bf16[16,16,8,768]{3,2,1,0:T(8,128)(2,1)S(1)} copy(bf16[16,16,8,768]{3,2,0,1:T(8,128)(2,1)} %bitcast.28) | data formatting | bytes 6291456 | tf_op jit(solution)/shard_map/transpose | solution.py:376
  116.7 12.6 %all-to-all-done.2.refs_0_ = bf16[16,192,128]{2,1,0:T(8,128)(2,1)} async-done(((bf16[16,192,128]{2,1,0:T(8,128)(2,1)}), bf16[16,192,128]{2,1,0:T(8,128)(2,1)}, u32[]{:S(2)}, u32[]{:S(2)}) %all-to-all-start.2) | async-done | bytes 786464 | tf_op jit(solution)/shard_map/all_to_all | solution.py:387
  129.3 1.4 %copy-done.1 = bf16[768,1024]{1,0:T(8,128)(2,1)S(1)} copy-done((bf16[768,1024]{1,0:T(8,128)(2,1)S(1)}, bf16[768,1024]{1,0:T(8,128)(2,1)}, u32[]{:S(2)}) %copy-start.1) | copy-done | bytes 1572888
  130.7 2.7 %shard_map.54 = (f32[1,24,768]{2,1,0:T(8,128)}, f32[1,24,768]{2,1,0:T(8,128)}) custom-call(bf16[16,192,128]{2,1,0:T(8,128)(2,1)} %all-to-all-done.2.refs_0_, bf16[16,128,768]{2,1,0:T(8,128)(2,1)S(1)} %bitcast.20, bf16[16,48,1024]{2,1,0:T(8,128)(2,1)S(1)} %bitcast.22), custom_call_target="tpu_custom_call" | custom-call | tf_op jit(solution)/shard_map/pallas_call | solution.py:338
  (13 shorter events, 0.1 us)
Async XLA Ops:
  7.2 88.0 %all-gather.5.cloned.1.call-start = ((), (), s32[]{:S(2)}) async-start(), calls=%async_computation.4 | async-start | bytes 1671168 | tf_op jit(solution)/shard_map/all_gather | solution.py:382
  8.0 1.1 copy-start.2
  9.1 1.9 %copy-start.4 = (bf16[2,8,8,12288]{3,2,1,0:T(8,128)(2,1)S(1)}, bf16[2,8,8,12288]{3,2,1,0:T(8,128)(2,1)}, u32[]{:S(2)}) copy-start(bf16[2,8,8,12288]{3,2,1,0:T(8,128)(2,1)} %param.3) | copy-start | bytes 9437188
  11.0 1.1 copy-start.5
  12.0 25.6 %copy-start.3 = (bf16[1,24,12288]{2,1,0:T(8,128)(2,1)S(1)}, bf16[1,24,12288]{2,1,0:T(8,128)(2,1)}, u32[]{:S(2)}) copy-start(bf16[1,24,12288]{2,1,0:T(8,128)(2,1)} %param.5) | copy-start | bytes 1769476
  12.0 25.6 %copy-start.6 = (bf16[1,24,12288]{2,1,0:T(8,128)(2,1)S(1)}, bf16[1,24,12288]{2,1,0:T(8,128)(2,1)}, u32[]{:S(2)}) copy-start(bf16[1,24,12288]{2,1,0:T(8,128)(2,1)} %param.4) | copy-start | bytes 1769476
  16.1 98.4 %all-gather.7.cloned.1.call-start = ((), (), s32[]{:S(2)}) async-start(), calls=%async_computation.5 | async-start | bytes 3342336 | tf_op jit(solution)/shard_map/all_gather | solution.py:375
  37.7 0.7 collective-permute-start
  95.2 1.4 %copy-start = (bf16[768,1024]{1,0:T(8,128)(2,1)S(1)}, bf16[768,1024]{1,0:T(8,128)(2,1)}, u32[]{:S(2)}) copy-start(bf16[768,1024]{1,0:T(8,128)(2,1)} %all-gather.5.cloned.1.call-done) | copy-start | bytes 4718596
  104.0 25.4 %all-to-all-start.2 = ((bf16[16,192,128]{2,1,0:T(8,128)(2,1)}), bf16[16,192,128]{2,1,0:T(8,128)(2,1)}, u32[]{:S(2)}, u32[]{:S(2)}) async-start(bf16[16,192,128]{2,1,0:T(8,128)(2,1)} %shard_map.53), calls=%async_computation.2 | async-start | bytes 1572864 | tf_op jit(solution)/shard_map/all_to_all | solution.py:387
  129.3 1.4 %copy-start.1 = (bf16[768,1024]{1,0:T(8,128)(2,1)S(1)}, bf16[768,1024]{1,0:T(8,128)(2,1)}, u32[]{:S(2)}) copy-start(bf16[768,1024]{1,0:T(8,128)(2,1)} %all-gather.5.cloned.1.call-done) | copy-start | bytes 4718596
Sparse Core Ops, SparseCore 0:
  16.2 40.0 all-gather.4
  58.1 56.3 all-gather.6

commit v2 on v1

v2 whole, which is shorter than its diff:
```python
import jax
import jax.numpy as jnp
from jax import lax
from jax.experimental import pallas as pl
from jax.experimental.pallas import tpu as pltpu
from jax.sharding import PartitionSpec as P

EPS = 1e-05
LANES = 128
F32 = jnp.float32
BF16 = jnp.bfloat16


def split(value):
    high = value.astype(BF16)
    return high, (value - high.astype(F32)).astype(BF16)


def dot_nn(left, right):
    return lax.dot_general(left, right, (((1,), (0,)), ((), ())), preferred_element_type=F32)


def dot_nt(left, right):
    return lax.dot_general(left, right, (((1,), (1,)), ((), ())), preferred_element_type=F32)


def params(megabytes=12):
    return pltpu.CompilerParams(vmem_limit_bytes=megabytes * 1024 * 1024)


def project_kernel(x_ref, down_ref, up_ref, both_ref, square_ref):
    rank, features = down_ref.shape
    width = 1536
    down = jnp.zeros((rank, LANES), F32)
    up = jnp.zeros((rank, LANES), F32)
    total = jnp.zeros((LANES, LANES), F32)
    for start in range(0, features, width):
        rows = x_ref[:, start : start + width]
        down += dot_nt(down_ref[:, start : start + width], rows)
        up += dot_nt(up_ref[:, start : start + width], rows)
        wide = rows.astype(F32)
        for tile in range(0, wide.shape[1], LANES):
            part = wide[:, tile : tile + LANES]
            total += part * part
    both_ref[0:rank] = down
    both_ref[rank : 2 * rank] = up
    square_ref[...] = jnp.sum(total.T, axis=0, keepdims=True)


def project(rows, down, up):
    rank = down.shape[0]
    return pl.pallas_call(
        project_kernel,
        out_shape=[
            jax.ShapeDtypeStruct((2 * rank, LANES), F32),
            jax.ShapeDtypeStruct((1, LANES), F32),
        ],
        compiler_params=params(),
    )(rows, down, up)


def pair_kernel(own_ref, other_ref, share_ref, out_ref, pad_ref):
    rank, features = own_ref.shape
    members = out_ref.shape[0]
    pad_ref[...] = jnp.zeros_like(pad_ref)
    pad_ref[:, 0:rank] = dot_nt(own_ref[...], other_ref[...])
    packed = pad_ref[0:8]
    for group in range(1, rank // 8):
        packed += pltpu.roll(pad_ref[8 * group : 8 * group + 8], rank * group, 1)
    head = jnp.concatenate([packed, jnp.zeros_like(packed)], axis=0)
    tiles = features // members // LANES
    for member in range(members):
        parts = [head]
        for tile in range(member * tiles, (member + 1) * tiles):
            parts.append(share_ref[:, tile * LANES : (tile + 1) * LANES].astype(F32))
        out_ref[member] = jnp.concatenate(parts, axis=0).astype(BF16)


def pair_products(own, other, share, members):
    rank, features = own.shape
    rows = 16 + 8 * (features // members // LANES)
    return pl.pallas_call(
        pair_kernel,
        out_shape=jax.ShapeDtypeStruct((members, rows, LANES), BF16),
        scratch_shapes=[pltpu.VMEM((rank, LANES), F32)],
        compiler_params=params(),
    )(own, other, share)


def partner(position, member, sections):
    return position ^ member ^ ((sections // 2 + sections // 4) * (position & 1))


def partner_of(position, member, sections):
    mixed = position ^ member
    return mixed ^ ((sections // 2 + sections // 4) * (mixed & 1))


def order_kernel(rank, blocks, in_ref, both_ref, weight_ref, out_ref, share_ref, work_ref):
    position = lax.axis_index("section")
    lane = lax.broadcasted_iota(jnp.int32, (8, LANES), 1)
    tiles = rank * blocks // LANES
    pieces = [in_ref[partner(position, t, blocks)].astype(F32)[0:8] for t in range(blocks)]
    bands = []
    for member in range(in_ref.shape[0]):
        piece = in_ref[member].astype(F32)
        band = [piece[row : row + 8] for row in range(16, piece.shape[0], 8)]
        bands.append(jnp.concatenate(band, axis=1))
    rows = 8 * in_ref.shape[0]
    share_ref[0:rows] = jnp.concatenate(bands, axis=0).astype(BF16)
    share_ref[rows:] = weight_ref[...]
    for group in range(rank // 8):
        turned = [pltpu.roll(pieces[t], (rank * (t - group)) % LANES, 1) for t in range(blocks)]
        for tile in range(tiles):
            place = (lane + tile * LANES) // rank
            value = jnp.zeros((8, LANES), F32)
            for t in range(blocks):
                if rank * t < (tile + 1) * LANES and rank * (t + 1) > tile * LANES:
                    value = jnp.where(place == t, turned[t], value)
            work_ref[tile * rank + 8 * group : tile * rank + 8 * group + 8] = value
    work_ref[tiles * rank : (tiles + 2) * rank] = both_ref[...]
    filled = (tiles + 2) * rank
    if filled < work_ref.shape[0]:
        work_ref[filled:] = jnp.zeros((work_ref.shape[0] - filled, LANES), F32)
    payload = work_ref[...].astype(BF16)
    for copy in range(out_ref.shape[0]):
        out_ref[copy] = payload


def order_blocks(gathered, both, weight, rank, copies):
    blocks = gathered.shape[0]

    def kernel(*refs):
        order_kernel(rank, blocks, *refs)

    rows = -(-(rank * blocks // LANES + 2) * rank // 16) * 16
    members, height = gathered.shape[:2]
    return pl.pallas_call(
        kernel,
        out_shape=[
            jax.ShapeDtypeStruct((copies, rows, LANES), BF16),
            jax.ShapeDtypeStruct((8 * members + 2 * rank, (height - 16) // 8 * LANES), BF16),
        ],
        scratch_shapes=[pltpu.VMEM((rows, LANES), F32)],
        compiler_params=params(),
    )(gathered, both, weight)


def chain_kernel(rank, blocks, features, normalizer, grid_ref, square_ref, out_ref, *rest):
    plain_ref, turned_ref, act_ref, scaled_ref, grad_ref, skip_ref = rest
    size = rank * blocks
    tiles = size // LANES
    received = [grid_ref[b].astype(F32) for b in range(blocks)]
    whole = jnp.concatenate(
        [
            jnp.concatenate(
                [piece[tile * rank : (tile + 1) * rank] for tile in range(tiles)], axis=1
            )
            for piece in received
        ],
        axis=0,
    )
    plain_ref[...] = whole.astype(BF16)
    turned_ref[...] = whole.T.astype(BF16)

    def span(b):
        first = rank * b // LANES
        last = (rank * b + rank - 1) // LANES
        return first, last

    def columns(ref, b, start, stop):
        first, last = span(b)
        return ref[start:stop, first * LANES : (last + 1) * LANES]

    def placed(b, value):
        first, last = span(b)
        before = rank * b - first * LANES
        after = (last + 1) * LANES - rank * (b + 1)
        parts = []
        if before:
            parts.append(jnp.zeros((before, LANES), F32))
        parts.append(value)
        if after:
            parts.append(jnp.zeros((after, LANES), F32))
        return jnp.concatenate(parts, axis=0).astype(BF16)

    narrow, hidden = [], []
    for piece in received:
        narrow.append(piece[tiles * rank : (tiles + 1) * rank])
        hidden.append(piece[(tiles + 1) * rank : (tiles + 2) * rank])
    initial = list(hidden)
    square = square_ref[...]
    inverses, acts, pres, slopes, ends = [], [], [], [], []
    for b in range(blocks):
        inverse = lax.rsqrt(square / features + EPS)
        pre = narrow[b] * inverse
        sigmoid = 1.0 / (1.0 + jnp.exp(-pre))
        act = (pre * sigmoid).astype(BF16).astype(F32)
        act_ref[rank * b : rank * (b + 1)] = act
        inverses.append(inverse)
        acts.append(act)
        pres.append(pre)
        slopes.append(sigmoid * (1.0 + pre * (1.0 - sigmoid)))
        right = placed(b, act)
        if b + 1 < blocks:
            start = rank * (b + 1) // 16 * 16
            update = dot_nn(columns(turned_ref, b, start, size), right)
            for k in range(b + 1, blocks):
                narrow[k] = narrow[k] + update[rank * k - start : rank * (k + 1) - start]
        start = rank * b // 16 * 16
        update = dot_nn(columns(plain_ref, b, start, size), right)
        own = update[rank * b - start : rank * (b + 1) - start]
        for k in range(b + 1, blocks):
            hidden[k] = hidden[k] + update[rank * k - start : rank * (k + 1) - start]
        square = square + jnp.sum(act * (2.0 * hidden[b] + own), axis=0, keepdims=True)
        ends.append(hidden[b] + own)

    back = [jnp.zeros((rank, LANES), F32) for _ in range(blocks)]
    decay = jnp.zeros((1, LANES), F32)
    for k in reversed(range(blocks)):
        weight = 1.0 / normalizer - decay
        scaled = acts[k] * weight
        scaled_ref[rank * k : rank * (k + 1)] = scaled
        skip_ref[rank * k : rank * (k + 1)] = -decay * acts[k]
        incoming = ends[k] * weight - initial[k] / normalizer + back[k]
        grad = (incoming * slopes[k] * inverses[k]).astype(BF16).astype(F32)
        grad_ref[rank * k : rank * (k + 1)] = grad
        decay = decay + inverses[k] / features * jnp.sum(grad * pres[k], axis=0, keepdims=True)
        if k:
            stop = -(-rank * k // 16) * 16
            coarse = scaled.astype(BF16).astype(F32)
            fine = scaled - coarse
            update = (
                dot_nn(columns(turned_ref, k, 0, stop), placed(k, coarse))
                + dot_nn(columns(turned_ref, k, 0, stop), placed(k, fine))
                + dot_nn(columns(plain_ref, k, 0, stop), placed(k, grad))
            )
            for b in range(k):
                back[b] = back[b] + update[rank * b : rank * (b + 1)]

    position = lax.axis_index("section")
    mine = pl.ds(pl.multiple_of(position * rank, 8), rank)
    own_act = act_ref[mine].astype(BF16)
    own_high, own_low = split(scaled_ref[mine])
    own_grad = grad_ref[mine].astype(BF16)
    all_act = act_ref[...].astype(BF16)
    all_high, all_low = split(scaled_ref[...])
    all_grad = grad_ref[...].astype(BF16)
    place = lax.broadcasted_iota(jnp.int32, (rank, size), 1) // rank
    later = dot_nt(own_act, all_high) + dot_nt(own_act, all_low)
    earlier = dot_nt(own_high, all_act) + dot_nt(own_low, all_act)
    both_up = jnp.where(place >= position, later, earlier)
    crossed = jnp.where(
        place < position,
        dot_nt(own_grad, all_act),
        jnp.where(place > position, dot_nt(own_act, all_grad), 0.0),
    )
    groups = LANES // 8
    source = lax.broadcasted_iota(jnp.int32, (LANES, LANES), 0)
    target = lax.broadcasted_iota(jnp.int32, (LANES, LANES), 1)
    moved = source == target ^ (position * (LANES // groups))
    rows = jnp.concatenate([grad_ref[mine], skip_ref[mine]], axis=0).astype(BF16)
    rows = dot_nn(rows, jnp.where(moved, 1.0, 0.0).astype(BF16))
    source = lax.broadcasted_iota(jnp.int32, (size, size), 0)
    target = lax.broadcasted_iota(jnp.int32, (size, size), 1)
    block = target // rank
    moved = source == target + rank * ((block ^ position) - block)
    sums = jnp.concatenate([both_up, crossed], axis=0).astype(BF16)
    sums = dot_nn(sums, jnp.where(moved, 1.0, 0.0).astype(BF16))
    pieces = [rows]
    for value in (sums[0:rank], sums[rank : 2 * rank]):
        pieces += [value[:, tile * LANES : (tile + 1) * LANES] for tile in range(tiles)]
    payload = jnp.concatenate(pieces, axis=0).astype(BF16)
    for copy in range(out_ref.shape[0]):
        out_ref[copy] = payload


def run_chain(grid, square, rank, features, normalizer, copies):
    blocks = grid.shape[0]
    size = rank * blocks
    rows = 2 * rank + 2 * (size // LANES) * rank

    def kernel(*refs):
        chain_kernel(rank, blocks, features, normalizer, *refs)

    narrow = pltpu.VMEM((size, LANES), F32)
    square_matrix = pltpu.VMEM((size, size), BF16)
    return pl.pallas_call(
        kernel,
        out_shape=jax.ShapeDtypeStruct((copies, rows, LANES), BF16),
        scratch_shapes=[square_matrix, square_matrix, narrow, narrow, narrow, narrow],
        compiler_params=params(),
    )(grid, square)


def finish_kernel(rank, blocks, parts_ref, *refs):
    down_ref, up_ref, held_ref, copied = refs[blocks:]
    copies = [
        pltpu.make_async_copy(ref, held_ref.at[i], copied.at[i])
        for i, ref in enumerate(refs[:blocks])
    ]
    for copy in copies:
        copy.start()
    size = rank * blocks
    tiles = size // LANES
    members = parts_ref.shape[0]
    position = lax.axis_index("section")
    total = None
    left = []
    for member in range(members):
        piece = parts_ref[member]
        piece = piece.astype(F32)
        left.append(piece[0 : 2 * rank])
        sums = piece[2 * rank :]
        total = sums if total is None else total + sums

    lane = lax.broadcasted_iota(jnp.int32, (2 * rank, LANES), 1)
    width = LANES // members
    stride = 1
    while stride < members:
        upper = (lane // width) & stride != 0
        for low in range(members):
            if low & stride == 0:
                first, second = left[low], left[low | stride]
                left[low] = jnp.where(upper, pltpu.roll(second, stride * width, 1), first)
                left[low | stride] = jnp.where(
                    upper, second, pltpu.roll(first, LANES - stride * width, 1)
                )
        stride *= 2

    def unfold(first):
        return jnp.concatenate(
            [total[(first + tile) * rank : (first + tile + 1) * rank] for tile in range(tiles)], axis=1
        )

    both_up, crossed = unfold(0), unfold(tiles)
    place = (lax.broadcasted_iota(jnp.int32, (rank, size), 1) // rank) ^ position
    below = jnp.where(place < position, crossed, 0.0)
    above = jnp.where(place > position, crossed, 0.0)
    rows = 8 * members
    result = jnp.zeros((2 * rank, held_ref.shape[2]), F32)
    weights = []
    for i in range(blocks):
        copies[i].wait()
        result += dot_nn(left[i].astype(BF16), held_ref[i, 0:rows])
        weights.append(held_ref[i, rows:].astype(F32))
    all_down = jnp.concatenate([w[0:rank] for w in weights], axis=0).astype(BF16)
    all_up = jnp.concatenate([w[rank : 2 * rank] for w in weights], axis=0).astype(BF16)
    high, low = split(jnp.concatenate([below, both_up], axis=0))
    result += dot_nn(high, all_up) + dot_nn(low, all_up)
    high, low = split(above)
    cross = dot_nn(high, all_down) + dot_nn(low, all_down)
    down_ref[0] = result[0:rank]
    up_ref[0] = result[rank : 2 * rank] + cross


def finish(parts, slices, rank):
    blocks = len(slices)
    width = slices[0].shape[1]

    def kernel(*refs):
        finish_kernel(rank, blocks, *refs)

    shape = jax.ShapeDtypeStruct((1, rank, width), F32)
    vmem = pl.BlockSpec(memory_space=pltpu.VMEM)
    return pl.pallas_call(
        kernel,
        in_specs=[vmem] + [pl.BlockSpec(memory_space=pl.ANY)] * blocks,
        out_specs=[vmem, vmem],
        out_shape=[shape, shape],
        scratch_shapes=[
            pltpu.VMEM((blocks,) + slices[0].shape, BF16),
            pltpu.SemaphoreType.DMA((blocks,)),
        ],
        compiler_params=params(60),
    )(parts, *slices)


def swapped(value, distance, count):
    return lax.ppermute(value, "section", [(i, i ^ distance) for i in range(count)])


def shards(inputs, down_proj, up_proj):
    sections = lax.axis_size("section")
    members = lax.axis_size("dp")
    position = lax.axis_index("section")
    member = lax.axis_index("dp")
    own_down, own_up = down_proj[0], up_proj[0]
    rank, features = own_down.shape
    width = features // members
    pipes, micro, count = inputs.shape[:3]
    normalizer = float(micro * count * members)
    all_rows = inputs.reshape(pipes * micro * count, features)

    route = [
        (partner(s, d, sections) * members + d, s * members + d)
        for s in range(sections)
        for d in range(members)
    ]
    receiver = partner_of(position, member, sections)
    outgoing = jnp.where(receiver >= position, own_up, own_down)
    other = lax.ppermute(outgoing, ("section", "dp"), route)

    share = lax.dynamic_index_in_dim(
        inputs.reshape(sections, count, features), position, 0, keepdims=False
    )
    weight = jnp.concatenate(
        [lax.dynamic_slice_in_dim(w, member * width, width, 1) for w in (own_down, own_up)], axis=0
    )
    both, square = project(all_rows, own_down, own_up)
    other, share, weight, both, square = lax.optimization_barrier(
        (other, share, weight, both, square)
    )

    products = lax.all_to_all(pair_products(own_up, other, share, members), "dp", 0, 0)
    grid, share = order_blocks(products, both, weight, rank, sections)
    grid = lax.all_to_all(grid, "section", 0, 0)
    grid, share = lax.optimization_barrier((grid, share))

    half = sections // 2
    slices = {0: share}
    for distance in (2, half - 2, half, *range(4, half - 2, 2)):
        slices[distance] = swapped(share, distance, sections)
    parts = run_chain(grid, square, rank, features, normalizer, members)
    parts, slices = lax.optimization_barrier((parts, slices))
    for distance in range(2, half, 2):
        slices[half + distance] = swapped(slices[half], distance, sections)
    for distance in range(0, sections, 2):
        slices[distance + 1] = swapped(slices[distance], 1, sections)
    parts = lax.all_to_all(parts, "dp", 0, 0)
    return finish(parts, [slices[d] for d in range(sections)], rank)


def solution(mesh):
    placed = (P(None, None, "dp", None), P("section", None, None), P("section", None, None))
    return jax.shard_map(
        shards,
        mesh=mesh,
        in_specs=placed,
        out_specs=(P("section", None, "dp"), P("section", None, "dp")),
        check_vma=False,
    )
```

time: 142 us -> 101 us (0.71); the launches traced: 140 us -> 101 us
  blocking collectives: 76.8 us -> 37.2 us
  starting transfers between devices: 5.07 us -> 24.2 us
  between operations: 14.1 us -> 0.99 us
  local copies, waits for them, and re-layouts: 10.8 us -> 6.94 us
  waiting for transfers between devices: 18.9 us -> 15.8 us
    all_to_all x3 -> x2, blocking collectives: 76.8 us -> 37.2 us  [the longest x1 19.6 us: shards(): lax.all_to_all(pair_products(own_up, other, share, members), 'dp', 0, 0)]
    ppermute x0 -> x15, waiting for transfers between devices: none -> 15.7 us  [swapped(): lax.ppermute(value, 'section', [(i, i ^ distance) for i in range(count)])]
    ppermute x0 -> x15, starting transfers between devices: none -> 13 us  [swapped(): lax.ppermute(value, 'section', [(i, i ^ distance) for i in range(count)])]
    all_to_all x1, waiting for transfers between devices: 12.6 us -> 0.01 us  [shards(): parts = lax.all_to_all(parts, 'dp', 0, 0)]
    all_gather x2 -> x0, waiting for transfers between devices: 6.22 us -> none  [the longest x1 6.22 us: shards(): slices = lax.all_gather(share, 'section')]
    ppermute x1, starting transfers between devices: 0.7 us -> 6.58 us  [shards(): other = lax.ppermute(outgoing, ('section', 'dp'), route)]
    transpose x1 -> x0, local copies, waits for them, and re-layouts: 2.2 us -> none  [shards(): slices.transpose(1, 0, 2, 3).reshape(members, sections * count, width)]
    unnamed x14 -> x38, local copies, waits for them, and re-layouts: 6.87 us -> 5.98 us
  transfers between devices with their start and end apart: 4 -> 17, of which waited for: 2 -> 5; matrix products, arithmetic and copies ran while one was open for 2% -> 1% of each run, Pallas kernels for 6% -> 9%
where the time goes in v2:
time: 101 us
  blocking collectives  37.2 us (37%)
  starting transfers between devices  24.2 us (24%)
  waiting for transfers between devices  15.8 us (16%)
  Pallas kernels  14.4 us (14%)
  local copies, waits for them, and re-layouts  6.94 us (7%)
  other arithmetic  1.32 us (1%)
    all_to_all x1, blocking collectives, shards(): lax.all_to_all(pair_products(own_up, other, share, members), 'dp', 0, 0)  19.6 us
    all_to_all x1, blocking collectives, shards(): grid = lax.all_to_all(grid, 'section', 0, 0)  17.5 us
    ppermute x15, waiting for transfers between devices, swapped(): lax.ppermute(value, 'section', [(i, i ^ distance) for i in range(count)])  15.7 us
    ppermute x15, starting transfers between devices, swapped(): lax.ppermute(value, 'section', [(i, i ^ distance) for i in range(count)])  13 us
    pallas_call x1, Pallas kernels, run_chain(): pl.pallas_call(kernel, out_shape=jax.ShapeDtypeStruct((copies, rows, LANE...  6.86 us
    ppermute x1, starting transfers between devices, shards(): other = lax.ppermute(outgoing, ('section', 'dp'), route)  6.58 us
    unnamed x38, local copies, waits for them, and re-layouts  5.98 us
    pallas_call x1, Pallas kernels, finish(): pl.pallas_call(kernel, in_specs=[vmem] + [pl.BlockSpec(memory_space=pl.AN...  4.77 us
  transfers between devices with their start and end apart: 17, of which 5 were waited for; matrix products, arithmetic and copies ran while one was open for 1% of the time, Pallas kernels for 9%

profile of v2, /device:TPU:1, one launch (start us, length us, event | category | flops | bytes accessed | tf_op | source)
XLA Modules:
  0.0 100.8 jit_solution(1224144263414374486)
XLA Ops:
  0.6 1.3 %broadcast_select_fusion = bf16[24,12288]{1,0:T(8,128)(2,1)S(1)} fusion(pred[]{:T(512)S(6)} %ge.3, bf16[1,24,12288]{2,1,0:T(8,128)(2,1)} %param.4, bf16[1,24,12288]{2,1,0:T(8,128)(2,1)} %param.5), kind=kLoop, calls=%fused_computation | loop fusion | flops 294912 | bytes 1769473 | tf_op jit(solution)/shard_map/jit(_where)/select_n | solution.py:401
  2.0 6.6 %collective-permute-start = (bf16[24,12288]{1,0:T(8,128)(2,1)S(1)}, bf16[24,12288]{1,0:T(8,128)(2,1)S(1)}, u32[]{:S(2)}, u32[]{:S(2)}) collective-permute-start(bf16[24,12288]{1,0:T(8,128)(2,1)S(1)} %broadcast_select_fusion), channel_id=1, source_target_pairs={{0,0},{17,1},{34,2},{51,3},{68,4},{85,5},{102,6},{119,7},{136,8},{... | collective-permute-start | bytes 1769480 | tf_op jit(solution)/shard_map/ppermute | solution.py:402
  8.5 0.9 dynamic-slice_bitcast_fusion.share_ref
  9.5 1.1 %copy-done = bf16[1,24,12288]{2,1,0:T(8,128)(2,1)S(1)} copy-done((bf16[1,24,12288]{2,1,0:T(8,128)(2,1)S(1)}, bf16[1,24,12288]{2,1,0:T(8,128)(2,1)}, u32[]{:S(2)}) %copy-start) | copy-done | bytes 589848
  10.6 1.9 %copy-done.1 = bf16[2,8,8,12288]{3,2,1,0:T(8,128)(2,1)S(1)} copy-done((bf16[2,8,8,12288]{3,2,1,0:T(8,128)(2,1)S(1)}, bf16[2,8,8,12288]{3,2,1,0:T(8,128)(2,1)}, u32[]{:S(2)}) %copy-start.1) | copy-done | bytes 3145752
  12.4 1.1 %copy-done.2 = bf16[1,24,12288]{2,1,0:T(8,128)(2,1)S(1)} copy-done((bf16[1,24,12288]{2,1,0:T(8,128)(2,1)S(1)}, bf16[1,24,12288]{2,1,0:T(8,128)(2,1)}, u32[]{:S(2)}) %copy-start.2) | copy-done | bytes 589848
  13.5 2.2 %shard_map.50 = (f32[48,128]{1,0:T(8,128)S(1)}, f32[1,128]{1,0:T(1,128)S(1)}) custom-call(bf16[128,12288]{1,0:T(8,128)(2,1)S(1)} %bitcast.15, bf16[24,12288]{1,0:T(8,128)(2,1)S(1)} %bitcast.16, bf16[24,12288]{1,0:T(8,128)(2,1)S(1)} %bitcast.12), custom_call_target="tpu_custom_call" | custom-call | tf_op jit(solution)/shard_map/pallas_call | solution.py:52
  16.2 19.6 %all_to_all.15.refs_0_ = bf16[16,64,128]{2,1,0:T(8,128)(2,1)S(1)} all-to-all(bf16[16,64,128]{2,1,0:T(8,128)(2,1)S(1)} %shard_map.51), channel_id=1, replica_groups=mesh['section'=16,'dp'=16] {'dp'}, dimensions={0} | all-to-all | bytes 524288 | tf_op jit(solution)/shard_map/all_to_all | solution.py:415
  36.0 17.5 %all_to_all.16.refs_0_ = bf16[16,128,128]{2,1,0:T(8,128)(2,1)S(1)} all-to-all(bf16[16,128,128]{2,1,0:T(8,128)(2,1)S(1)} %get-tuple-element.25), channel_id=1, replica_groups=mesh['section'=16,'dp'=16] {'section'}, dimensions={0} | all-to-all | bytes 1048576 | tf_op jit(solution)/shard_map/all_to_all | solution.py:417
  53.6 0.7 collective-permute-start.4
  54.3 1.2 %collective-permute-start.3 = (bf16[176,768]{1,0:T(8,128)(2,1)S(1)}, bf16[176,768]{1,0:T(8,128)(2,1)S(1)}, u32[]{:S(2)}, u32[]{:S(2)}) collective-permute-start(bf16[176,768]{1,0:T(8,128)(2,1)S(1)} %get-tuple-element.31.refs_1_), channel_id=1, source_target_pairs={{0,96},{16,112},{32,64},{48,80},{64,32},{80,48},{96,0},{112,16},{1... | collective-permute-start | bytes 811016 | tf_op jit(solution)/shard_map/ppermute | solution.py:380
  55.5 0.7 collective-permute-start.2
  56.2 1.3 %collective-permute-start.1 = (bf16[176,768]{1,0:T(8,128)(2,1)S(1)}, bf16[176,768]{1,0:T(8,128)(2,1)S(1)}, u32[]{:S(2)}, u32[]{:S(2)}) collective-permute-start(bf16[176,768]{1,0:T(8,128)(2,1)S(1)} %get-tuple-element.31.refs_1_), channel_id=1, source_target_pairs={{0,32},{16,48},{32,0},{48,16},{64,96},{80,112},{96,64},{112,80},{1... | collective-permute-start | bytes 811016 | tf_op jit(solution)/shard_map/ppermute | solution.py:380
  57.6 6.9 %shard_map.53 = bf16[16,192,128]{2,1,0:T(8,128)(2,1)} custom-call(bf16[16,128,128]{2,1,0:T(8,128)(2,1)S(1)} %all_to_all.16.refs_0_, f32[1,128]{1,0:T(1,128)S(1)} %get-tuple-element.28.refs_1_), custom_call_target="tpu_custom_call" | custom-call | tf_op jit(solution)/shard_map/pallas_call | solution.py:288
  64.4 3.9 %collective-permute-done.3.refs_7_ = bf16[176,768]{1,0:T(8,128)(2,1)S(1)} collective-permute-done((bf16[176,768]{1,0:T(8,128)(2,1)S(1)}, bf16[176,768]{1,0:T(8,128)(2,1)S(1)}, u32[]{:S(2)}, u32[]{:S(2)}) %collective-permute-start.3) | collective-permute-done | bytes 270368 | tf_op jit(solution)/shard_map/ppermute | solution.py:380
  68.7 4.6 %all-to-all-start.2 = ((bf16[16,192,128]{2,1,0:T(8,128)(2,1)}), bf16[16,192,128]{2,1,0:T(8,128)(2,1)S(1)}, u32[]{:S(2)}, u32[]{:S(2)}) async-start(bf16[16,192,128]{2,1,0:T(8,128)(2,1)} %shard_map.53), calls=%async_computation.2 | async-start | bytes 1572864 | tf_op jit(solution)/shard_map/all_to_all | solution.py:430
  73.4 2.5 %collective-permute-start.5 = (bf16[176,768]{1,0:T(8,128)(2,1)S(1)}, bf16[176,768]{1,0:T(8,128)(2,1)S(1)}, u32[]{:S(2)}, u32[]{:S(2)}) collective-permute-start(bf16[176,768]{1,0:T(8,128)(2,1)S(1)} %get-tuple-element.31.refs_1_), channel_id=1, source_target_pairs={{0,16},{16,0},{32,48},{48,32},{64,80},{80,64},{96,112},{112,96},{1... | collective-permute-start | bytes 811016 | tf_op jit(solution)/shard_map/ppermute | solution.py:380
  76.4 1.2 %collective-permute-start.14 = (bf16[176,768]{1,0:T(8,128)(2,1)S(1)}, bf16[176,768]{1,0:T(8,128)(2,1)S(1)}, u32[]{:S(2)}, u32[]{:S(2)}) collective-permute-start(bf16[176,768]{1,0:T(8,128)(2,1)S(1)} %collective-permute-done.4.refs_9_), channel_id=1, source_target_pairs={{0,96},{16,112},{32,64},{48,80},{64,32},{80,48},{96,0},{112,16},{1... | collective-permute-start | bytes 811016 | tf_op jit(solution)/shard_map/ppermute | solution.py:380
  78.3 1.3 %collective-permute-start.10 = (bf16[176,768]{1,0:T(8,128)(2,1)S(1)}, bf16[176,768]{1,0:T(8,128)(2,1)S(1)}, u32[]{:S(2)}, u32[]{:S(2)}) collective-permute-start(bf16[176,768]{1,0:T(8,128)(2,1)S(1)} %collective-permute-done.4.refs_9_), channel_id=1, source_target_pairs={{0,32},{16,48},{32,0},{48,16},{64,96},{80,112},{96,64},{112,80},{1... | collective-permute-start | bytes 811016 | tf_op jit(solution)/shard_map/ppermute | solution.py:380
  79.7 0.9 collective-permute-start.9
  80.9 10.5 %collective-permute-done.14.refs_15_ = bf16[176,768]{1,0:T(8,128)(2,1)S(1)} collective-permute-done((bf16[176,768]{1,0:T(8,128)(2,1)S(1)}, bf16[176,768]{1,0:T(8,128)(2,1)S(1)}, u32[]{:S(2)}, u32[]{:S(2)}) %collective-permute-start.14) | collective-permute-done | bytes 270368 | tf_op jit(solution)/shard_map/ppermute | solution.py:380
  91.4 0.9 collective-permute-start.15
  95.0 0.9 copy-done.4
  95.9 4.8 %shard_map.54 = (f32[1,24,768]{2,1,0:T(8,128)}, f32[1,24,768]{2,1,0:T(8,128)}) custom-call(bf16[16,192,128]{2,1,0:T(8,128)(2,1)} %copy-done.4, bf16[176,768]{1,0:T(8,128)(2,1)} %copy-done.3, bf16[176,768]{1,0:T(8,128)(2,1)} %copy-done.9, bf16[176,768]{1,0:T(8,128)(2,1)} %copy-done.8, bf16[176,768]{1,0:T(8,128)(2,1)} %copy-done.10, ...), custom_call_target="tpu_custom_call" | custom-call | tf_op jit(solution)/shard_map/pallas_call | solution.py:366
  (59 shorter events, 5.2 us)
Async XLA Ops:
  2.0 13.8 %collective-permute-start = (bf16[24,12288]{1,0:T(8,128)(2,1)S(1)}, bf16[24,12288]{1,0:T(8,128)(2,1)S(1)}, u32[]{:S(2)}, u32[]{:S(2)}) collective-permute-start(bf16[24,12288]{1,0:T(8,128)(2,1)S(1)} %broadcast_select_fusion), channel_id=1, source_target_pairs={{0,0},{17,1},{34,2},{51,3},{68,4},{85,5},{102,6},{119,7},{136,8},{... | collective-permute-start | bytes 1769480 | tf_op jit(solution)/shard_map/ppermute | solution.py:402
  36.0 58.9 %copy-start.3 = (bf16[176,768]{1,0:T(8,128)(2,1)}, bf16[176,768]{1,0:T(8,128)(2,1)S(1)}, u32[]{:S(2)}) copy-start(bf16[176,768]{1,0:T(8,128)(2,1)S(1)} %get-tuple-element.31.refs_1_) | copy-start | bytes 811012
  53.6 10.9 %collective-permute-start.4 = (bf16[176,768]{1,0:T(8,128)(2,1)S(1)}, bf16[176,768]{1,0:T(8,128)(2,1)S(1)}, u32[]{:S(2)}, u32[]{:S(2)}) collective-permute-start(bf16[176,768]{1,0:T(8,128)(2,1)S(1)} %get-tuple-element.31.refs_1_), channel_id=1, source_target_pairs={{0,128},{16,144},{32,160},{48,176},{64,192},{80,208},{96,224},{112... | collective-permute-start | bytes 811016 | tf_op jit(solution)/shard_map/ppermute | solution.py:380
  54.3 14.0 %collective-permute-start.3 = (bf16[176,768]{1,0:T(8,128)(2,1)S(1)}, bf16[176,768]{1,0:T(8,128)(2,1)S(1)}, u32[]{:S(2)}, u32[]{:S(2)}) collective-permute-start(bf16[176,768]{1,0:T(8,128)(2,1)S(1)} %get-tuple-element.31.refs_1_), channel_id=1, source_target_pairs={{0,96},{16,112},{32,64},{48,80},{64,32},{80,48},{96,0},{112,16},{1... | collective-permute-start | bytes 811016 | tf_op jit(solution)/shard_map/ppermute | solution.py:380
  55.5 12.8 %collective-permute-start.2 = (bf16[176,768]{1,0:T(8,128)(2,1)S(1)}, bf16[176,768]{1,0:T(8,128)(2,1)S(1)}, u32[]{:S(2)}, u32[]{:S(2)}) collective-permute-start(bf16[176,768]{1,0:T(8,128)(2,1)S(1)} %get-tuple-element.31.refs_1_), channel_id=1, source_target_pairs={{0,64},{16,80},{32,96},{48,112},{64,0},{80,16},{96,32},{112,48},{1... | collective-permute-start | bytes 811016 | tf_op jit(solution)/shard_map/ppermute | solution.py:380
  56.2 12.5 %collective-permute-start.1 = (bf16[176,768]{1,0:T(8,128)(2,1)S(1)}, bf16[176,768]{1,0:T(8,128)(2,1)S(1)}, u32[]{:S(2)}, u32[]{:S(2)}) collective-permute-start(bf16[176,768]{1,0:T(8,128)(2,1)S(1)} %get-tuple-element.31.refs_1_), channel_id=1, source_target_pairs={{0,32},{16,48},{32,0},{48,16},{64,96},{80,112},{96,64},{112,80},{1... | collective-permute-start | bytes 811016 | tf_op jit(solution)/shard_map/ppermute | solution.py:380
  64.4 30.5 %copy-start.5 = (bf16[176,768]{1,0:T(8,128)(2,1)}, bf16[176,768]{1,0:T(8,128)(2,1)S(1)}, u32[]{:S(2)}) copy-start(bf16[176,768]{1,0:T(8,128)(2,1)S(1)} %collective-permute-done.4.refs_9_) | copy-start | bytes 811012
  68.3 26.6 %copy-start.6 = (bf16[176,768]{1,0:T(8,128)(2,1)}, bf16[176,768]{1,0:T(8,128)(2,1)S(1)}, u32[]{:S(2)}) copy-start(bf16[176,768]{1,0:T(8,128)(2,1)S(1)} %collective-permute-done.3.refs_7_) | copy-start | bytes 811012
  68.3 26.6 %copy-start.7 = (bf16[176,768]{1,0:T(8,128)(2,1)}, bf16[176,768]{1,0:T(8,128)(2,1)S(1)}, u32[]{:S(2)}) copy-start(bf16[176,768]{1,0:T(8,128)(2,1)S(1)} %collective-permute-done.2.refs_5_) | copy-start | bytes 811012
  68.7 26.3 %copy-start.8 = (bf16[176,768]{1,0:T(8,128)(2,1)}, bf16[176,768]{1,0:T(8,128)(2,1)S(1)}, u32[]{:S(2)}) copy-start(bf16[176,768]{1,0:T(8,128)(2,1)S(1)} %collective-permute-done.1.refs_3_) | copy-start | bytes 811012
  68.7 26.2 %all-to-all-start.2 = ((bf16[16,192,128]{2,1,0:T(8,128)(2,1)}), bf16[16,192,128]{2,1,0:T(8,128)(2,1)S(1)}, u32[]{:S(2)}, u32[]{:S(2)}) async-start(bf16[16,192,128]{2,1,0:T(8,128)(2,1)} %shard_map.53), calls=%async_computation.2 | async-start | bytes 1572864 | tf_op jit(solution)/shard_map/all_to_all | solution.py:430
  73.4 4.9 %collective-permute-start.5 = (bf16[176,768]{1,0:T(8,128)(2,1)S(1)}, bf16[176,768]{1,0:T(8,128)(2,1)S(1)}, u32[]{:S(2)}, u32[]{:S(2)}) collective-permute-start(bf16[176,768]{1,0:T(8,128)(2,1)S(1)} %get-tuple-element.31.refs_1_), channel_id=1, source_target_pairs={{0,16},{16,0},{32,48},{48,32},{64,80},{80,64},{96,112},{112,96},{1... | collective-permute-start | bytes 811016 | tf_op jit(solution)/shard_map/ppermute | solution.py:380
  75.9 3.8 %collective-permute-start.6 = (bf16[176,768]{1,0:T(8,128)(2,1)S(1)}, bf16[176,768]{1,0:T(8,128)(2,1)S(1)}, u32[]{:S(2)}, u32[]{:S(2)}) collective-permute-start(bf16[176,768]{1,0:T(8,128)(2,1)S(1)} %collective-permute-done.1.refs_3_), channel_id=1, source_target_pairs={{0,16},{16,0},{32,48},{48,32},{64,80},{80,64},{96,112},{112,96},{1... | collective-permute-start | bytes 811016 | tf_op jit(solution)/shard_map/ppermute | solution.py:380
  76.0 4.6 %collective-permute-start.7 = (bf16[176,768]{1,0:T(8,128)(2,1)S(1)}, bf16[176,768]{1,0:T(8,128)(2,1)S(1)}, u32[]{:S(2)}, u32[]{:S(2)}) collective-permute-start(bf16[176,768]{1,0:T(8,128)(2,1)S(1)} %collective-permute-done.2.refs_5_), channel_id=1, source_target_pairs={{0,16},{16,0},{32,48},{48,32},{64,80},{80,64},{96,112},{112,96},{1... | collective-permute-start | bytes 811016 | tf_op jit(solution)/shard_map/ppermute | solution.py:380
  76.4 15.0 %collective-permute-start.14 = (bf16[176,768]{1,0:T(8,128)(2,1)S(1)}, bf16[176,768]{1,0:T(8,128)(2,1)S(1)}, u32[]{:S(2)}, u32[]{:S(2)}) collective-permute-start(bf16[176,768]{1,0:T(8,128)(2,1)S(1)} %collective-permute-done.4.refs_9_), channel_id=1, source_target_pairs={{0,96},{16,112},{32,64},{48,80},{64,32},{80,48},{96,0},{112,16},{1... | collective-permute-start | bytes 811016 | tf_op jit(solution)/shard_map/ppermute | solution.py:380
  77.6 14.7 %collective-permute-start.12 = (bf16[176,768]{1,0:T(8,128)(2,1)S(1)}, bf16[176,768]{1,0:T(8,128)(2,1)S(1)}, u32[]{:S(2)}, u32[]{:S(2)}) collective-permute-start(bf16[176,768]{1,0:T(8,128)(2,1)S(1)} %collective-permute-done.4.refs_9_), channel_id=1, source_target_pairs={{0,64},{16,80},{32,96},{48,112},{64,0},{80,16},{96,32},{112,48},{1... | collective-permute-start | bytes 811016 | tf_op jit(solution)/shard_map/ppermute | solution.py:380
  78.3 16.7 %copy-start.9 = (bf16[176,768]{1,0:T(8,128)(2,1)}, bf16[176,768]{1,0:T(8,128)(2,1)S(1)}, u32[]{:S(2)}) copy-start(bf16[176,768]{1,0:T(8,128)(2,1)S(1)} %collective-permute-done.5.refs_2_) | copy-start | bytes 811012
  78.3 14.1 %collective-permute-start.10 = (bf16[176,768]{1,0:T(8,128)(2,1)S(1)}, bf16[176,768]{1,0:T(8,128)(2,1)S(1)}, u32[]{:S(2)}, u32[]{:S(2)}) collective-permute-start(bf16[176,768]{1,0:T(8,128)(2,1)S(1)} %collective-permute-done.4.refs_9_), channel_id=1, source_target_pairs={{0,32},{16,48},{32,0},{48,16},{64,96},{80,112},{96,64},{112,80},{1... | collective-permute-start | bytes 811016 | tf_op jit(solution)/shard_map/ppermute | solution.py:380
  79.7 15.3 %copy-start.10 = (bf16[176,768]{1,0:T(8,128)(2,1)}, bf16[176,768]{1,0:T(8,128)(2,1)S(1)}, u32[]{:S(2)}) copy-start(bf16[176,768]{1,0:T(8,128)(2,1)S(1)} %collective-permute-done.6.refs_4_) | copy-start | bytes 811012
  79.7 13.3 %collective-permute-start.9 = (bf16[176,768]{1,0:T(8,128)(2,1)S(1)}, bf16[176,768]{1,0:T(8,128)(2,1)S(1)}, u32[]{:S(2)}, u32[]{:S(2)}) collective-permute-start(bf16[176,768]{1,0:T(8,128)(2,1)S(1)} %collective-permute-done.4.refs_9_), channel_id=1, source_target_pairs={{0,16},{16,0},{32,48},{48,32},{64,80},{80,64},{96,112},{112,96},{1... | collective-permute-start | bytes 811016 | tf_op jit(solution)/shard_map/ppermute | solution.py:380
  80.6 12.3 %collective-permute-start.8 = (bf16[176,768]{1,0:T(8,128)(2,1)S(1)}, bf16[176,768]{1,0:T(8,128)(2,1)S(1)}, u32[]{:S(2)}, u32[]{:S(2)}) collective-permute-start(bf16[176,768]{1,0:T(8,128)(2,1)S(1)} %collective-permute-done.3.refs_7_), channel_id=1, source_target_pairs={{0,16},{16,0},{32,48},{48,32},{64,80},{80,64},{96,112},{112,96},{1... | collective-permute-start | bytes 811016 | tf_op jit(solution)/shard_map/ppermute | solution.py:380
  91.4 2.0 %collective-permute-start.15 = (bf16[176,768]{1,0:T(8,128)(2,1)S(1)}, bf16[176,768]{1,0:T(8,128)(2,1)S(1)}, u32[]{:S(2)}, u32[]{:S(2)}) collective-permute-start(bf16[176,768]{1,0:T(8,128)(2,1)S(1)} %collective-permute-done.14.refs_15_), channel_id=1, source_target_pairs={{0,16},{16,0},{32,48},{48,32},{64,80},{80,64},{96,112},{112,96},{1... | collective-permute-start | bytes 811016 | tf_op jit(solution)/shard_map/ppermute | solution.py:380
  92.3 1.6 %collective-permute-start.13 = (bf16[176,768]{1,0:T(8,128)(2,1)S(1)}, bf16[176,768]{1,0:T(8,128)(2,1)S(1)}, u32[]{:S(2)}, u32[]{:S(2)}) collective-permute-start(bf16[176,768]{1,0:T(8,128)(2,1)S(1)} %collective-permute-done.12.refs_13_), channel_id=1, source_target_pairs={{0,16},{16,0},{32,48},{48,32},{64,80},{80,64},{96,112},{112,96},{1... | collective-permute-start | bytes 811016 | tf_op jit(solution)/shard_map/ppermute | solution.py:380
  92.4 2.5 %collective-permute-start.11 = (bf16[176,768]{1,0:T(8,128)(2,1)S(1)}, bf16[176,768]{1,0:T(8,128)(2,1)}, u32[]{:S(2)}, u32[]{:S(2)}) collective-permute-start(bf16[176,768]{1,0:T(8,128)(2,1)S(1)} %collective-permute-done.10.refs_11_), channel_id=1, source_target_pairs={{0,16},{16,0},{32,48},{48,32},{64,80},{80,64},{96,112},{112,96},{1... | collective-permute-start | bytes 811016 | tf_op jit(solution)/shard_map/ppermute | solution.py:380
  (12 other events, 30.3 us)

commit v3 on v2

--- a/solution.py
+++ b/solution.py
@@ -270,12 +270,10 @@
     pieces = [rows]
     for value in (sums[0:rank], sums[rank : 2 * rank]):
         pieces += [value[:, tile * LANES : (tile + 1) * LANES] for tile in range(tiles)]
-    payload = jnp.concatenate(pieces, axis=0).astype(BF16)
-    for copy in range(out_ref.shape[0]):
-        out_ref[copy] = payload
-
-
-def run_chain(grid, square, rank, features, normalizer, copies):
+    out_ref[...] = jnp.concatenate(pieces, axis=0).astype(BF16)
+
+
+def run_chain(grid, square, rank, features, normalizer):
     blocks = grid.shape[0]
     size = rank * blocks
     rows = 2 * rank + 2 * (size // LANES) * rank
@@ -287,10 +285,32 @@
     square_matrix = pltpu.VMEM((size, size), BF16)
     return pl.pallas_call(
         kernel,
-        out_shape=jax.ShapeDtypeStruct((copies, rows, LANES), BF16),
+        out_shape=jax.ShapeDtypeStruct((rows, LANES), BF16),
         scratch_shapes=[square_matrix, square_matrix, narrow, narrow, narrow, narrow],
         compiler_params=params(),
     )(grid, square)
+
+
+def combine_kernel(rank, own_ref, other_ref, out_ref):
+    own, other = own_ref[...], other_ref[...]
+    both = own.astype(F32) + other.astype(F32)
+    payload = jnp.concatenate(
+        [own[0 : 2 * rank], other[0 : 2 * rank], both[2 * rank :].astype(BF16)], axis=0
+    )
+    for copy in range(out_ref.shape[0]):
+        out_ref[copy] = payload
+
+
+def combine(own, other, rank, copies):
+    def kernel(*refs):
+        combine_kernel(rank, *refs)
+
+    rows = own.shape[0] + 2 * rank
+    return pl.pallas_call(
+        kernel,
+        out_shape=jax.ShapeDtypeStruct((copies, rows, LANES), BF16),
+        compiler_params=params(),
+    )(own, other)
 
 
 def finish_kernel(rank, blocks, parts_ref, *refs):
@@ -303,30 +323,12 @@
         copy.start()
     size = rank * blocks
     tiles = size // LANES
-    members = parts_ref.shape[0]
+    near = parts_ref.shape[0]
     position = lax.axis_index("section")
-    total = None
-    left = []
-    for member in range(members):
-        piece = parts_ref[member]
-        piece = piece.astype(F32)
-        left.append(piece[0 : 2 * rank])
-        sums = piece[2 * rank :]
-        total = sums if total is None else total + sums
-
-    lane = lax.broadcasted_iota(jnp.int32, (2 * rank, LANES), 1)
-    width = LANES // members
-    stride = 1
-    while stride < members:
-        upper = (lane // width) & stride != 0
-        for low in range(members):
-            if low & stride == 0:
-                first, second = left[low], left[low | stride]
-                left[low] = jnp.where(upper, pltpu.roll(second, stride * width, 1), first)
-                left[low | stride] = jnp.where(
-                    upper, second, pltpu.roll(first, LANES - stride * width, 1)
-                )
-        stride *= 2
+    own_half = lax.axis_index("dp") // near
+    total = parts_ref[0, 4 * rank :].astype(F32)
+    for member in range(1, near):
+        total += parts_ref[member, 4 * rank :].astype(F32)
 
     def unfold(first):
         return jnp.concatenate(
@@ -337,15 +339,22 @@
     place = (lax.broadcasted_iota(jnp.int32, (rank, size), 1) // rank) ^ position
     below = jnp.where(place < position, crossed, 0.0)
     above = jnp.where(place > position, crossed, 0.0)
-    rows = 8 * members
+    for copy in copies:
+        copy.wait()
+    wide = [held_ref[i].astype(F32) for i in range(blocks)]
+
+    def stacked(first, count):
+        return jnp.concatenate([piece[first : first + count] for piece in wide], axis=0).astype(BF16)
+
     result = jnp.zeros((2 * rank, held_ref.shape[2]), F32)
-    weights = []
-    for i in range(blocks):
-        copies[i].wait()
-        result += dot_nn(left[i].astype(BF16), held_ref[i, 0:rows])
-        weights.append(held_ref[i, rows:].astype(F32))
-    all_down = jnp.concatenate([w[0:rank] for w in weights], axis=0).astype(BF16)
-    all_up = jnp.concatenate([w[rank : 2 * rank] for w in weights], axis=0).astype(BF16)
+    for half in range(2):
+        start = pl.multiple_of((own_half ^ half) * 2 * rank, 16)
+        for member in range(near):
+            left = parts_ref[member, pl.ds(start, 2 * rank)]
+            result += dot_nn(left, stacked(8 * (half * near + member), 8))
+    rows = 16 * near
+    all_down = stacked(rows, rank)
+    all_up = stacked(rows + rank, rank)
     high, low = split(jnp.concatenate([below, both_up], axis=0))
     result += dot_nn(high, all_up) + dot_nn(low, all_up)
     high, low = split(above)
@@ -376,8 +385,12 @@
     )(parts, *slices)
 
 
+def moved(value, axis, distance, count):
+    return lax.ppermute(value, axis, [(i, i ^ distance) for i in range(count)])
+
+
 def swapped(value, distance, count):
-    return lax.ppermute(value, "section", [(i, i ^ distance) for i in range(count)])
+    return moved(value, "section", distance, count)
 
 
 def shards(inputs, down_proj, up_proj):
@@ -415,19 +428,25 @@
     products = lax.all_to_all(pair_products(own_up, other, share, members), "dp", 0, 0)
     grid, share = order_blocks(products, both, weight, rank, sections)
     grid = lax.all_to_all(grid, "section", 0, 0)
-    grid, share = lax.optimization_barrier((grid, share))
 
     half = sections // 2
     slices = {0: share}
-    for distance in (2, half - 2, half, *range(4, half - 2, 2)):
+    for distance in (2, half - 2, half):
         slices[distance] = swapped(share, distance, sections)
-    parts = run_chain(grid, square, rank, features, normalizer, members)
+    parts = run_chain(grid, square, rank, features, normalizer)
     parts, slices = lax.optimization_barrier((parts, slices))
-    for distance in range(2, half, 2):
-        slices[half + distance] = swapped(slices[half], distance, sections)
+    for distance in range(4, half - 2, 2):
+        slices[distance] = swapped(share, distance, sections)
+    last = half - 2
+    slices[half + last] = swapped(slices[half], last, sections)
+    for distance in range(2, last, 2):
+        slices[half + distance] = swapped(slices[distance], half, sections)
     for distance in range(0, sections, 2):
         slices[distance + 1] = swapped(slices[distance], 1, sections)
-    parts = lax.all_to_all(parts, "dp", 0, 0)
+    line = members // 2
+    parts = combine(parts, moved(parts, "dp", line, members), rank, line)
+    groups = [list(range(start, start + line)) for start in (0, line)]
+    parts = lax.all_to_all(parts, "dp", 0, 0, axis_index_groups=groups)
     return finish(parts, [slices[d] for d in range(sections)], rank)
 
 

time: 101 us -> 94.8 us (0.939)
  blocking collectives: 37.2 us -> 19.6 us
  starting transfers between devices: 24.2 us -> 40.5 us
  waiting for transfers between devices: 15.8 us -> 9.98 us
    all_to_all x1 -> x0, blocking collectives: 17.5 us -> none  [shards(): grid = lax.all_to_all(grid, 'section', 0, 0)]
    ppermute x15 -> x16, waiting for transfers between devices: 15.7 us -> 5.13 us  [moved(): return lax.ppermute(value, axis, [(i, i ^ distance) for i in range(count)])]
    ppermute x15 -> x16, starting transfers between devices: 13 us -> 22.1 us  [moved(): return lax.ppermute(value, axis, [(i, i ^ distance) for i in range(count)])]
    all_to_all x1 -> x2, starting transfers between devices: 4.65 us -> 11.8 us  [the longest x1 7.95 us: shards(): grid = lax.all_to_all(grid, 'section', 0, 0)]
    all_to_all x1 -> x2, waiting for transfers between devices: 0.01 us -> 4.83 us  [the longest x1 4.83 us: shards(): grid = lax.all_to_all(grid, 'section', 0, 0)]
    pallas_call x1 -> x2, Pallas kernels: 6.86 us -> 6.78 us  [the longest x1 5.94 us: run_chain(): pl.pallas_call(kernel, out_shape=jax.ShapeDtypeStruct((rows, LANES), BF16...]
  transfers between devices with their start and end apart: 17 -> 19, of which waited for: 5 -> 5; matrix products, arithmetic and copies ran while one was open for 1% -> 1% of each run, Pallas kernels for 9% -> 10%
where the time goes in v3:
time: 94.8 us; the launch traced here: 94.2 us
  starting transfers between devices  40.5 us (43%)
  blocking collectives  19.6 us (21%)
  Pallas kernels  15.3 us (16%)
  waiting for transfers between devices  9.98 us (11%)
  local copies, waits for them, and re-layouts  6.52 us (7%)
  other arithmetic  1.32 us (1%)
  between operations  1.02 us (1%)
    ppermute x16, starting transfers between devices, moved(): return lax.ppermute(value, axis, [(i, i ^ distance) for i in range(count)])  22.1 us
    all_to_all x1, blocking collectives, shards(): lax.all_to_all(pair_products(own_up, other, share, members), 'dp', 0, 0)  19.6 us
    all_to_all x1, starting transfers between devices, shards(): grid = lax.all_to_all(grid, 'section', 0, 0)  7.95 us
    ppermute x1, starting transfers between devices, shards(): other = lax.ppermute(outgoing, ('section', 'dp'), route)  6.58 us
    pallas_call x1, Pallas kernels, run_chain(): pl.pallas_call(kernel, out_shape=jax.ShapeDtypeStruct((rows, LANES), BF16...  5.94 us
    unnamed x38, local copies, waits for them, and re-layouts  5.55 us
    ppermute x16, waiting for transfers between devices, moved(): return lax.ppermute(value, axis, [(i, i ^ distance) for i in range(count)])  5.13 us
    pallas_call x1, Pallas kernels, finish(): pl.pallas_call(kernel, in_specs=[vmem] + [pl.BlockSpec(memory_space=pl.AN...  4.89 us
  transfers between devices with their start and end apart: 19, of which 5 were waited for; matrix products, arithmetic and copies ran while one was open for 1% of the time, Pallas kernels for 10%

profile of v3, /device:TPU:1, one launch (start us, length us, event | category | flops | bytes accessed | tf_op | source)
XLA Modules:
  0.0 94.2 jit_solution(8453629251573714778)
XLA Ops:
  0.6 1.3 %broadcast_select_fusion = bf16[24,12288]{1,0:T(8,128)(2,1)S(1)} fusion(pred[]{:T(512)S(6)} %ge.3, bf16[1,24,12288]{2,1,0:T(8,128)(2,1)} %param.4, bf16[1,24,12288]{2,1,0:T(8,128)(2,1)} %param.5), kind=kLoop, calls=%fused_computation | loop fusion | flops 294912 | bytes 1769473 | tf_op jit(solution)/shard_map/jit(_where)/select_n | solution.py:414
  2.0 6.6 %collective-permute-start = (bf16[24,12288]{1,0:T(8,128)(2,1)S(1)}, bf16[24,12288]{1,0:T(8,128)(2,1)S(1)}, u32[]{:S(2)}, u32[]{:S(2)}) collective-permute-start(bf16[24,12288]{1,0:T(8,128)(2,1)S(1)} %broadcast_select_fusion), channel_id=1, source_target_pairs={{0,0},{17,1},{34,2},{51,3},{68,4},{85,5},{102,6},{119,7},{136,8},{... | collective-permute-start | bytes 1769480 | tf_op jit(solution)/shard_map/ppermute | solution.py:415
  8.5 0.9 %dynamic-slice_bitcast_fusion.share_ref = bf16[8,12288]{1,0:T(8,128)(2,1)S(1)} fusion(bf16[16,8,12288]{2,1,0:T(8,128)(2,1)} %bitcast.14, s32[]{:T(128)S(6)} %select_n.18), kind=kLoop, calls=%fused_computation.1 | loop fusion | bytes 393220 | tf_op jit(solution)/shard_map/jit(dynamic_index_in_dim)/squeeze | solution.py:417
  9.5 1.1 %copy-done = bf16[1,24,12288]{2,1,0:T(8,128)(2,1)S(1)} copy-done((bf16[1,24,12288]{2,1,0:T(8,128)(2,1)S(1)}, bf16[1,24,12288]{2,1,0:T(8,128)(2,1)}, u32[]{:S(2)}) %copy-start) | copy-done | bytes 589848
  10.6 1.9 %copy-done.1 = bf16[2,8,8,12288]{3,2,1,0:T(8,128)(2,1)S(1)} copy-done((bf16[2,8,8,12288]{3,2,1,0:T(8,128)(2,1)S(1)}, bf16[2,8,8,12288]{3,2,1,0:T(8,128)(2,1)}, u32[]{:S(2)}) %copy-start.1) | copy-done | bytes 3145752
  12.4 1.1 %copy-done.2 = bf16[1,24,12288]{2,1,0:T(8,128)(2,1)S(1)} copy-done((bf16[1,24,12288]{2,1,0:T(8,128)(2,1)S(1)}, bf16[1,24,12288]{2,1,0:T(8,128)(2,1)}, u32[]{:S(2)}) %copy-start.2) | copy-done | bytes 589848
  13.5 2.2 %shard_map.50 = (f32[48,128]{1,0:T(8,128)S(1)}, f32[1,128]{1,0:T(1,128)S(1)}) custom-call(bf16[128,12288]{1,0:T(8,128)(2,1)S(1)} %bitcast.15, bf16[24,12288]{1,0:T(8,128)(2,1)S(1)} %bitcast.16, bf16[24,12288]{1,0:T(8,128)(2,1)S(1)} %bitcast.12), custom_call_target="tpu_custom_call" | custom-call | tf_op jit(solution)/shard_map/pallas_call | solution.py:52
  16.2 19.6 %all_to_all.15.refs_0_ = bf16[16,64,128]{2,1,0:T(8,128)(2,1)S(1)} all-to-all(bf16[16,64,128]{2,1,0:T(8,128)(2,1)S(1)} %shard_map.51), channel_id=1, replica_groups=mesh['section'=16,'dp'=16] {'dp'}, dimensions={0} | all-to-all | bytes 524288 | tf_op jit(solution)/shard_map/all_to_all | solution.py:428
  35.9 1.0 %shard_map.52 = (bf16[16,128,128]{2,1,0:T(8,128)(2,1)}, bf16[176,768]{1,0:T(8,128)(2,1)S(1)}) custom-call(bf16[16,64,128]{2,1,0:T(8,128)(2,1)S(1)} %all_to_all.15.refs_0_, f32[48,128]{1,0:T(8,128)S(1)} %get-tuple-element.20.refs_1_, bf16[48,768]{1,0:T(8,128)(2,1)S(1)} %pad_maximum_fusion.refs_2_), custom_call_target="tpu_custom_call" | custom-call | tf_op jit(solution)/shard_map/pallas_call | solution.py:138
  36.8 8.0 %all-to-all-start.1 = ((bf16[16,128,128]{2,1,0:T(8,128)(2,1)}), bf16[16,128,128]{2,1,0:T(8,128)(2,1)S(1)}, u32[]{:S(2)}, u32[]{:S(2)}) async-start(bf16[16,128,128]{2,1,0:T(8,128)(2,1)} %get-tuple-element.22), calls=%async_computation.1 | async-start | bytes 1048576 | tf_op jit(solution)/shard_map/all_to_all | solution.py:430
  44.8 1.4 %collective-permute-start.1 = (bf16[176,768]{1,0:T(8,128)(2,1)S(1)}, bf16[176,768]{1,0:T(8,128)(2,1)S(1)}, u32[]{:S(2)}, u32[]{:S(2)}) collective-permute-start(bf16[176,768]{1,0:T(8,128)(2,1)S(1)} %get-tuple-element.26.refs_1_), channel_id=1, source_target_pairs={{0,32},{16,48},{32,0},{48,16},{64,96},{80,112},{96,64},{112,80},{1... | collective-permute-start | bytes 811016 | tf_op jit(solution)/shard_map/ppermute | solution.py:389
  46.1 1.8 %collective-permute-start.2 = (bf16[176,768]{1,0:T(8,128)(2,1)S(1)}, bf16[176,768]{1,0:T(8,128)(2,1)S(1)}, u32[]{:S(2)}, u32[]{:S(2)}) collective-permute-start(bf16[176,768]{1,0:T(8,128)(2,1)S(1)} %get-tuple-element.26.refs_1_), channel_id=1, source_target_pairs={{0,96},{16,112},{32,64},{48,80},{64,32},{80,48},{96,0},{112,16},{1... | collective-permute-start | bytes 811016 | tf_op jit(solution)/shard_map/ppermute | solution.py:389
  47.9 1.2 %collective-permute-start.3 = (bf16[176,768]{1,0:T(8,128)(2,1)S(1)}, bf16[176,768]{1,0:T(8,128)(2,1)S(1)}, u32[]{:S(2)}, u32[]{:S(2)}) collective-permute-start(bf16[176,768]{1,0:T(8,128)(2,1)S(1)} %get-tuple-element.26.refs_1_), channel_id=1, source_target_pairs={{0,128},{16,144},{32,160},{48,176},{64,192},{80,208},{96,224},{112... | collective-permute-start | bytes 811016 | tf_op jit(solution)/shard_map/ppermute | solution.py:389
  49.7 4.8 %all-to-all-done.1.refs_0_ = bf16[16,128,128]{2,1,0:T(8,128)(2,1)S(1)} async-done(((bf16[16,128,128]{2,1,0:T(8,128)(2,1)}), bf16[16,128,128]{2,1,0:T(8,128)(2,1)S(1)}, u32[]{:S(2)}, u32[]{:S(2)}) %all-to-all-start.1) | async-done | bytes 524320 | tf_op jit(solution)/shard_map/all_to_all | solution.py:430
  54.6 5.9 %shard_map.53.refs_0_ = bf16[192,128]{1,0:T(8,128)(2,1)S(1)} custom-call(bf16[16,128,128]{2,1,0:T(8,128)(2,1)S(1)} %all-to-all-done.1.refs_0_, f32[1,128]{1,0:T(1,128)S(1)} %get-tuple-element.23.refs_1_), custom_call_target="tpu_custom_call" | custom-call | tf_op jit(solution)/shard_map/pallas_call | solution.py:286
  60.6 1.4 %collective-permute-start.4 = (bf16[192,128]{1,0:T(8,128)(2,1)S(1)}, bf16[192,128]{1,0:T(8,128)(2,1)S(1)}, u32[]{:S(2)}, u32[]{:S(2)}) collective-permute-start(bf16[192,128]{1,0:T(8,128)(2,1)S(1)} %shard_map.53.refs_0_), channel_id=1, source_target_pairs={{0,8},{1,9},{2,10},{3,11},{4,12},{5,13},{6,14},{7,15},{8,0},{9,1},... | collective-permute-start | bytes 147464 | tf_op jit(solution)/shard_map/ppermute | solution.py:389
  62.0 3.4 %collective-permute-done.4.refs_1_ = bf16[192,128]{1,0:T(8,128)(2,1)S(1)} collective-permute-done((bf16[192,128]{1,0:T(8,128)(2,1)S(1)}, bf16[192,128]{1,0:T(8,128)(2,1)S(1)}, u32[]{:S(2)}, u32[]{:S(2)}) %collective-permute-start.4) | collective-permute-done | bytes 49184 | tf_op jit(solution)/shard_map/ppermute | solution.py:389
  66.2 3.9 %all-to-all-start.2 = ((bf16[8,240,128]{2,1,0:T(8,128)(2,1)}), bf16[8,240,128]{2,1,0:T(8,128)(2,1)S(1)}, u32[]{:S(2)}, u32[]{:S(2)}) async-start(bf16[8,240,128]{2,1,0:T(8,128)(2,1)} %shard_map.54), calls=%async_computation.2 | async-start | bytes 983040 | tf_op jit(solution)/shard_map/all_to_all | solution.py:449
  70.1 1.3 %collective-permute-start.13 = (bf16[176,768]{1,0:T(8,128)(2,1)S(1)}, bf16[176,768]{1,0:T(8,128)(2,1)S(1)}, u32[]{:S(2)}, u32[]{:S(2)}) collective-permute-start(bf16[176,768]{1,0:T(8,128)(2,1)S(1)} %collective-permute-done.7.refs_5_), channel_id=1, source_target_pairs={{0,128},{16,144},{32,160},{48,176},{64,192},{80,208},{96,224},{112... | collective-permute-start | bytes 811016 | tf_op jit(solution)/shard_map/ppermute | solution.py:389
  71.4 2.1 %collective-permute-start.8 = (bf16[176,768]{1,0:T(8,128)(2,1)S(1)}, bf16[176,768]{1,0:T(8,128)(2,1)S(1)}, u32[]{:S(2)}, u32[]{:S(2)}) collective-permute-start(bf16[176,768]{1,0:T(8,128)(2,1)S(1)} %collective-permute-done.7.refs_5_), channel_id=1, source_target_pairs={{0,16},{16,0},{32,48},{48,32},{64,80},{80,64},{96,112},{112,96},{1... | collective-permute-start | bytes 811016 | tf_op jit(solution)/shard_map/ppermute | solution.py:389
  73.5 1.2 %collective-permute-start.11 = (bf16[176,768]{1,0:T(8,128)(2,1)S(1)}, bf16[176,768]{1,0:T(8,128)(2,1)S(1)}, u32[]{:S(2)}, u32[]{:S(2)}) collective-permute-start(bf16[176,768]{1,0:T(8,128)(2,1)S(1)} %collective-permute-done.1.refs_3_), channel_id=1, source_target_pairs={{0,128},{16,144},{32,160},{48,176},{64,192},{80,208},{96,224},{112... | collective-permute-start | bytes 811016 | tf_op jit(solution)/shard_map/ppermute | solution.py:389
  75.8 6.4 %collective-permute-start.5 = (bf16[176,768]{1,0:T(8,128)(2,1)S(1)}, bf16[176,768]{1,0:T(8,128)(2,1)S(1)}, u32[]{:S(2)}, u32[]{:S(2)}) collective-permute-start(bf16[176,768]{1,0:T(8,128)(2,1)S(1)} %get-tuple-element.26.refs_1_), channel_id=1, source_target_pairs={{0,16},{16,0},{32,48},{48,32},{64,80},{80,64},{96,112},{112,96},{1... | collective-permute-start | bytes 811016 | tf_op jit(solution)/shard_map/ppermute | solution.py:389
  82.5 2.7 %collective-permute-start.9 = (bf16[176,768]{1,0:T(8,128)(2,1)S(1)}, bf16[176,768]{1,0:T(8,128)(2,1)S(1)}, u32[]{:S(2)}, u32[]{:S(2)}) collective-permute-start(bf16[176,768]{1,0:T(8,128)(2,1)S(1)} %collective-permute-done.2.refs_7_), channel_id=1, source_target_pairs={{0,16},{16,0},{32,48},{48,32},{64,80},{80,64},{96,112},{112,96},{1... | collective-permute-start | bytes 811016 | tf_op jit(solution)/shard_map/ppermute | solution.py:389
  89.2 4.9 %shard_map.55 = (f32[1,24,768]{2,1,0:T(8,128)}, f32[1,24,768]{2,1,0:T(8,128)}) custom-call(bf16[8,240,128]{2,1,0:T(8,128)(2,1)} %copy-done.4, bf16[176,768]{1,0:T(8,128)(2,1)} %copy-done.3, bf16[176,768]{1,0:T(8,128)(2,1)} %copy-done.14, bf16[176,768]{1,0:T(8,128)(2,1)} %copy-done.5, bf16[176,768]{1,0:T(8,128)(2,1)} %copy-done.15, ...), custom_call_target="tpu_custom_call" | custom-call | tf_op jit(solution)/shard_map/pallas_call | solution.py:375
  (63 shorter events, 7.2 us)
Async XLA Ops:
  2.0 13.8 %collective-permute-start = (bf16[24,12288]{1,0:T(8,128)(2,1)S(1)}, bf16[24,12288]{1,0:T(8,128)(2,1)S(1)}, u32[]{:S(2)}, u32[]{:S(2)}) collective-permute-start(bf16[24,12288]{1,0:T(8,128)(2,1)S(1)} %broadcast_select_fusion), channel_id=1, source_target_pairs={{0,0},{17,1},{34,2},{51,3},{68,4},{85,5},{102,6},{119,7},{136,8},{... | collective-permute-start | bytes 1769480 | tf_op jit(solution)/shard_map/ppermute | solution.py:415
  36.8 51.5 %copy-start.3 = (bf16[176,768]{1,0:T(8,128)(2,1)}, bf16[176,768]{1,0:T(8,128)(2,1)S(1)}, u32[]{:S(2)}) copy-start(bf16[176,768]{1,0:T(8,128)(2,1)S(1)} %get-tuple-element.26.refs_1_) | copy-start | bytes 811012
  36.8 17.8 %all-to-all-start.1 = ((bf16[16,128,128]{2,1,0:T(8,128)(2,1)}), bf16[16,128,128]{2,1,0:T(8,128)(2,1)S(1)}, u32[]{:S(2)}, u32[]{:S(2)}) async-start(bf16[16,128,128]{2,1,0:T(8,128)(2,1)} %get-tuple-element.22), calls=%async_computation.1 | async-start | bytes 1048576 | tf_op jit(solution)/shard_map/all_to_all | solution.py:430
  44.8 15.7 %collective-permute-start.1 = (bf16[176,768]{1,0:T(8,128)(2,1)S(1)}, bf16[176,768]{1,0:T(8,128)(2,1)S(1)}, u32[]{:S(2)}, u32[]{:S(2)}) collective-permute-start(bf16[176,768]{1,0:T(8,128)(2,1)S(1)} %get-tuple-element.26.refs_1_), channel_id=1, source_target_pairs={{0,32},{16,48},{32,0},{48,16},{64,96},{80,112},{96,64},{112,80},{1... | collective-permute-start | bytes 811016 | tf_op jit(solution)/shard_map/ppermute | solution.py:389
  46.1 14.4 %collective-permute-start.2 = (bf16[176,768]{1,0:T(8,128)(2,1)S(1)}, bf16[176,768]{1,0:T(8,128)(2,1)S(1)}, u32[]{:S(2)}, u32[]{:S(2)}) collective-permute-start(bf16[176,768]{1,0:T(8,128)(2,1)S(1)} %get-tuple-element.26.refs_1_), channel_id=1, source_target_pairs={{0,96},{16,112},{32,64},{48,80},{64,32},{80,48},{96,0},{112,16},{1... | collective-permute-start | bytes 811016 | tf_op jit(solution)/shard_map/ppermute | solution.py:389
  47.9 12.6 %collective-permute-start.3 = (bf16[176,768]{1,0:T(8,128)(2,1)S(1)}, bf16[176,768]{1,0:T(8,128)(2,1)S(1)}, u32[]{:S(2)}, u32[]{:S(2)}) collective-permute-start(bf16[176,768]{1,0:T(8,128)(2,1)S(1)} %get-tuple-element.26.refs_1_), channel_id=1, source_target_pairs={{0,128},{16,144},{32,160},{48,176},{64,192},{80,208},{96,224},{112... | collective-permute-start | bytes 811016 | tf_op jit(solution)/shard_map/ppermute | solution.py:389
  49.1 21.0 %collective-permute-start.7 = (bf16[176,768]{1,0:T(8,128)(2,1)S(1)}, bf16[176,768]{1,0:T(8,128)(2,1)S(1)}, u32[]{:S(2)}, u32[]{:S(2)}) collective-permute-start(bf16[176,768]{1,0:T(8,128)(2,1)S(1)} %get-tuple-element.26.refs_1_), channel_id=1, source_target_pairs={{0,64},{16,80},{32,96},{48,112},{64,0},{80,16},{96,32},{112,48},{1... | collective-permute-start | bytes 811016 | tf_op jit(solution)/shard_map/ppermute | solution.py:389
  60.5 27.8 %copy-start.5 = (bf16[176,768]{1,0:T(8,128)(2,1)}, bf16[176,768]{1,0:T(8,128)(2,1)S(1)}, u32[]{:S(2)}) copy-start(bf16[176,768]{1,0:T(8,128)(2,1)S(1)} %collective-permute-done.1.refs_3_) | copy-start | bytes 811012
  60.5 27.8 %copy-start.6 = (bf16[176,768]{1,0:T(8,128)(2,1)}, bf16[176,768]{1,0:T(8,128)(2,1)S(1)}, u32[]{:S(2)}) copy-start(bf16[176,768]{1,0:T(8,128)(2,1)S(1)} %collective-permute-done.2.refs_7_) | copy-start | bytes 811012
  60.6 27.7 %copy-start.7 = (bf16[176,768]{1,0:T(8,128)(2,1)}, bf16[176,768]{1,0:T(8,128)(2,1)S(1)}, u32[]{:S(2)}) copy-start(bf16[176,768]{1,0:T(8,128)(2,1)S(1)} %collective-permute-done.3.refs_9_) | copy-start | bytes 811012
  60.6 4.8 %collective-permute-start.4 = (bf16[192,128]{1,0:T(8,128)(2,1)S(1)}, bf16[192,128]{1,0:T(8,128)(2,1)S(1)}, u32[]{:S(2)}, u32[]{:S(2)}) collective-permute-start(bf16[192,128]{1,0:T(8,128)(2,1)S(1)} %shard_map.53.refs_0_), channel_id=1, source_target_pairs={{0,8},{1,9},{2,10},{3,11},{4,12},{5,13},{6,14},{7,15},{8,0},{9,1},... | collective-permute-start | bytes 147464 | tf_op jit(solution)/shard_map/ppermute | solution.py:389
  66.2 22.0 %all-to-all-start.2 = ((bf16[8,240,128]{2,1,0:T(8,128)(2,1)}), bf16[8,240,128]{2,1,0:T(8,128)(2,1)S(1)}, u32[]{:S(2)}, u32[]{:S(2)}) async-start(bf16[8,240,128]{2,1,0:T(8,128)(2,1)} %shard_map.54), calls=%async_computation.2 | async-start | bytes 983040 | tf_op jit(solution)/shard_map/all_to_all | solution.py:449
  70.1 18.2 %copy-start.8 = (bf16[176,768]{1,0:T(8,128)(2,1)}, bf16[176,768]{1,0:T(8,128)(2,1)S(1)}, u32[]{:S(2)}) copy-start(bf16[176,768]{1,0:T(8,128)(2,1)S(1)} %collective-permute-done.7.refs_5_) | copy-start | bytes 811012
  70.1 5.7 %collective-permute-start.13 = (bf16[176,768]{1,0:T(8,128)(2,1)S(1)}, bf16[176,768]{1,0:T(8,128)(2,1)S(1)}, u32[]{:S(2)}, u32[]{:S(2)}) collective-permute-start(bf16[176,768]{1,0:T(8,128)(2,1)S(1)} %collective-permute-done.7.refs_5_), channel_id=1, source_target_pairs={{0,128},{16,144},{32,160},{48,176},{64,192},{80,208},{96,224},{112... | collective-permute-start | bytes 811016 | tf_op jit(solution)/shard_map/ppermute | solution.py:389
  71.4 10.8 %collective-permute-start.8 = (bf16[176,768]{1,0:T(8,128)(2,1)S(1)}, bf16[176,768]{1,0:T(8,128)(2,1)S(1)}, u32[]{:S(2)}, u32[]{:S(2)}) collective-permute-start(bf16[176,768]{1,0:T(8,128)(2,1)S(1)} %collective-permute-done.7.refs_5_), channel_id=1, source_target_pairs={{0,16},{16,0},{32,48},{48,32},{64,80},{80,64},{96,112},{112,96},{1... | collective-permute-start | bytes 811016 | tf_op jit(solution)/shard_map/ppermute | solution.py:389
  73.5 9.0 %collective-permute-start.11 = (bf16[176,768]{1,0:T(8,128)(2,1)S(1)}, bf16[176,768]{1,0:T(8,128)(2,1)S(1)}, u32[]{:S(2)}, u32[]{:S(2)}) collective-permute-start(bf16[176,768]{1,0:T(8,128)(2,1)S(1)} %collective-permute-done.1.refs_3_), channel_id=1, source_target_pairs={{0,128},{16,144},{32,160},{48,176},{64,192},{80,208},{96,224},{112... | collective-permute-start | bytes 811016 | tf_op jit(solution)/shard_map/ppermute | solution.py:389
  74.7 10.5 %collective-permute-start.15 = (bf16[176,768]{1,0:T(8,128)(2,1)S(1)}, bf16[176,768]{1,0:T(8,128)(2,1)S(1)}, u32[]{:S(2)}, u32[]{:S(2)}) collective-permute-start(bf16[176,768]{1,0:T(8,128)(2,1)S(1)} %collective-permute-done.3.refs_9_), channel_id=1, source_target_pairs={{0,96},{16,112},{32,64},{48,80},{64,32},{80,48},{96,0},{112,16},{1... | collective-permute-start | bytes 811016 | tf_op jit(solution)/shard_map/ppermute | solution.py:389
  75.3 10.1 %collective-permute-start.10 = (bf16[176,768]{1,0:T(8,128)(2,1)S(1)}, bf16[176,768]{1,0:T(8,128)(2,1)S(1)}, u32[]{:S(2)}, u32[]{:S(2)}) collective-permute-start(bf16[176,768]{1,0:T(8,128)(2,1)S(1)} %collective-permute-done.3.refs_9_), channel_id=1, source_target_pairs={{0,16},{16,0},{32,48},{48,32},{64,80},{80,64},{96,112},{112,96},{1... | collective-permute-start | bytes 811016 | tf_op jit(solution)/shard_map/ppermute | solution.py:389
  75.8 9.9 %collective-permute-start.5 = (bf16[176,768]{1,0:T(8,128)(2,1)S(1)}, bf16[176,768]{1,0:T(8,128)(2,1)S(1)}, u32[]{:S(2)}, u32[]{:S(2)}) collective-permute-start(bf16[176,768]{1,0:T(8,128)(2,1)S(1)} %get-tuple-element.26.refs_1_), channel_id=1, source_target_pairs={{0,16},{16,0},{32,48},{48,32},{64,80},{80,64},{96,112},{112,96},{1... | collective-permute-start | bytes 811016 | tf_op jit(solution)/shard_map/ppermute | solution.py:389
  82.2 3.6 %collective-permute-start.6 = (bf16[176,768]{1,0:T(8,128)(2,1)S(1)}, bf16[176,768]{1,0:T(8,128)(2,1)S(1)}, u32[]{:S(2)}, u32[]{:S(2)}) collective-permute-start(bf16[176,768]{1,0:T(8,128)(2,1)S(1)} %collective-permute-done.1.refs_3_), channel_id=1, source_target_pairs={{0,16},{16,0},{32,48},{48,32},{64,80},{80,64},{96,112},{112,96},{1... | collective-permute-start | bytes 811016 | tf_op jit(solution)/shard_map/ppermute | solution.py:389
  82.5 3.9 %collective-permute-start.9 = (bf16[176,768]{1,0:T(8,128)(2,1)S(1)}, bf16[176,768]{1,0:T(8,128)(2,1)S(1)}, u32[]{:S(2)}, u32[]{:S(2)}) collective-permute-start(bf16[176,768]{1,0:T(8,128)(2,1)S(1)} %collective-permute-done.2.refs_7_), channel_id=1, source_target_pairs={{0,16},{16,0},{32,48},{48,32},{64,80},{80,64},{96,112},{112,96},{1... | collective-permute-start | bytes 811016 | tf_op jit(solution)/shard_map/ppermute | solution.py:389
  85.2 1.6 %collective-permute-start.14 = (bf16[176,768]{1,0:T(8,128)(2,1)S(1)}, bf16[176,768]{1,0:T(8,128)(2,1)S(1)}, u32[]{:S(2)}, u32[]{:S(2)}) collective-permute-start(bf16[176,768]{1,0:T(8,128)(2,1)S(1)} %collective-permute-done.13.refs_13_), channel_id=1, source_target_pairs={{0,16},{16,0},{32,48},{48,32},{64,80},{80,64},{96,112},{112,96},{1... | collective-permute-start | bytes 811016 | tf_op jit(solution)/shard_map/ppermute | solution.py:389
  85.3 2.2 %collective-permute-start.12 = (bf16[176,768]{1,0:T(8,128)(2,1)S(1)}, bf16[176,768]{1,0:T(8,128)(2,1)S(1)}, u32[]{:S(2)}, u32[]{:S(2)}) collective-permute-start(bf16[176,768]{1,0:T(8,128)(2,1)S(1)} %collective-permute-done.11.refs_11_), channel_id=1, source_target_pairs={{0,16},{16,0},{32,48},{48,32},{64,80},{80,64},{96,112},{112,96},{1... | collective-permute-start | bytes 811016 | tf_op jit(solution)/shard_map/ppermute | solution.py:389
  85.7 2.5 %collective-permute-start.16 = (bf16[176,768]{1,0:T(8,128)(2,1)S(1)}, bf16[176,768]{1,0:T(8,128)(2,1)}, u32[]{:S(2)}, u32[]{:S(2)}) collective-permute-start(bf16[176,768]{1,0:T(8,128)(2,1)S(1)} %collective-permute-done.15.refs_15_), channel_id=1, source_target_pairs={{0,16},{16,0},{32,48},{48,32},{64,80},{80,64},{96,112},{112,96},{1... | collective-permute-start | bytes 811016 | tf_op jit(solution)/shard_map/ppermute | solution.py:389
  (14 other events, 42.3 us)

commit v4 on v3

--- a/solution.py
+++ b/solution.py
@@ -314,13 +314,8 @@
 
 
 def finish_kernel(rank, blocks, parts_ref, *refs):
-    down_ref, up_ref, held_ref, copied = refs[blocks:]
-    copies = [
-        pltpu.make_async_copy(ref, held_ref.at[i], copied.at[i])
-        for i, ref in enumerate(refs[:blocks])
-    ]
-    for copy in copies:
-        copy.start()
+    slice_refs = refs[:blocks]
+    down_ref, up_ref = refs[blocks:]
     size = rank * blocks
     tiles = size // LANES
     near = parts_ref.shape[0]
@@ -339,26 +334,27 @@
     place = (lax.broadcasted_iota(jnp.int32, (rank, size), 1) // rank) ^ position
     below = jnp.where(place < position, crossed, 0.0)
     above = jnp.where(place > position, crossed, 0.0)
-    for copy in copies:
-        copy.wait()
-    wide = [held_ref[i].astype(F32) for i in range(blocks)]
+    wide = [ref[...].astype(F32) for ref in slice_refs]
 
     def stacked(first, count):
         return jnp.concatenate([piece[first : first + count] for piece in wide], axis=0).astype(BF16)
 
-    result = jnp.zeros((2 * rank, held_ref.shape[2]), F32)
+    result = jnp.zeros((2 * rank, slice_refs[0].shape[1]), F32)
     for half in range(2):
         start = pl.multiple_of((own_half ^ half) * 2 * rank, 16)
-        for member in range(near):
-            left = parts_ref[member, pl.ds(start, 2 * rank)]
-            result += dot_nn(left, stacked(8 * (half * near + member), 8))
+        for member in range(0, near, 2):
+            pair = [parts_ref[member + i, pl.ds(start, 2 * rank)] for i in range(2)]
+            bands = [stacked(8 * (half * near + member + i), 8) for i in range(2)]
+            result += dot_nn(jnp.concatenate(pair, axis=1), jnp.concatenate(bands, axis=0))
     rows = 16 * near
     all_down = stacked(rows, rank)
     all_up = stacked(rows + rank, rank)
     high, low = split(jnp.concatenate([below, both_up], axis=0))
-    result += dot_nn(high, all_up) + dot_nn(low, all_up)
-    high, low = split(above)
-    cross = dot_nn(high, all_down) + dot_nn(low, all_down)
+    sums = dot_nn(jnp.concatenate([high, low], axis=0), all_up)
+    result += sums[0 : 2 * rank] + sums[2 * rank :]
+    high, low = split(jnp.concatenate([above, jnp.zeros((8, size), F32)], axis=0))
+    sums = dot_nn(jnp.concatenate([high, low], axis=0), all_down)
+    cross = sums[0:rank] + sums[rank + 8 : 2 * rank + 8]
     down_ref[0] = result[0:rank]
     up_ref[0] = result[rank : 2 * rank] + cross
 
@@ -371,17 +367,8 @@
         finish_kernel(rank, blocks, *refs)
 
     shape = jax.ShapeDtypeStruct((1, rank, width), F32)
-    vmem = pl.BlockSpec(memory_space=pltpu.VMEM)
-    return pl.pallas_call(
-        kernel,
-        in_specs=[vmem] + [pl.BlockSpec(memory_space=pl.ANY)] * blocks,
-        out_specs=[vmem, vmem],
-        out_shape=[shape, shape],
-        scratch_shapes=[
-            pltpu.VMEM((blocks,) + slices[0].shape, BF16),
-            pltpu.SemaphoreType.DMA((blocks,)),
-        ],
-        compiler_params=params(60),
+    return pl.pallas_call(
+        kernel, out_shape=[shape, shape], compiler_params=params()
     )(parts, *slices)
 
 
@@ -430,23 +417,30 @@
     grid = lax.all_to_all(grid, "section", 0, 0)
 
     half = sections // 2
-    slices = {0: share}
-    for distance in (2, half - 2, half):
-        slices[distance] = swapped(share, distance, sections)
+    last = half - 2
+    early = (0, 2, last)
+    slices = {d: swapped(share, d, sections) for d in (2, last, half)}
+    later = {d: swapped(share, d, sections) for d in range(4, last, 2)}
     parts = run_chain(grid, square, rank, features, normalizer)
     parts, slices = lax.optimization_barrier((parts, slices))
-    for distance in range(4, half - 2, 2):
-        slices[distance] = swapped(share, distance, sections)
-    last = half - 2
-    slices[half + last] = swapped(slices[half], last, sections)
-    for distance in range(2, last, 2):
-        slices[half + distance] = swapped(slices[distance], half, sections)
-    for distance in range(0, sections, 2):
-        slices[distance + 1] = swapped(slices[distance], 1, sections)
+
     line = members // 2
-    parts = combine(parts, moved(parts, "dp", line, members), rank, line)
+    other = moved(parts, "dp", line, members)
+    parts, other, slices, later = lax.optimization_barrier((parts, other, slices, later))
+    slices = {0: share, **slices, **later}
+    for d in (2, last):
+        slices[half + d] = swapped(slices[half], d, sections)
+    for d in range(4, last, 2):
+        slices[half + d] = swapped(slices[d], half, sections)
+    for d in early:
+        slices[d + 1] = swapped(slices[d], 1, sections)
+    parts = combine(parts, other, rank, line)
     groups = [list(range(start, start + line)) for start in (0, line)]
     parts = lax.all_to_all(parts, "dp", 0, 0, axis_index_groups=groups)
+    parts, slices = lax.optimization_barrier((parts, slices))
+    for d in range(0, sections, 2):
+        if d not in early:
+            slices[d + 1] = swapped(slices[d], 1, sections)
     return finish(parts, [slices[d] for d in range(sections)], rank)
 
 

time: 94.8 us -> 93 us (0.981)
  waiting for transfers between devices: 9.98 us -> 20.4 us
  starting transfers between devices: 40.5 us -> 33.5 us
  Pallas kernels: 15.3 us -> 11.9 us
  local copies, waits for them, and re-layouts: 6.52 us -> 4.97 us
    ppermute x16, waiting for transfers between devices: 5.13 us -> 14.2 us  [moved(): return lax.ppermute(value, axis, [(i, i ^ distance) for i in range(count)])]
    ppermute x16, starting transfers between devices: 22.1 us -> 15.1 us  [moved(): return lax.ppermute(value, axis, [(i, i ^ distance) for i in range(count)])]
    pallas_call x1, Pallas kernels: 4.89 us -> 1.53 us  [finish(): pl.pallas_call(kernel, out_shape=[shape, shape], compiler_params=params())]
    all_to_all x1, waiting for transfers between devices: 0.01 us -> 1.61 us  [shards(): parts = lax.all_to_all(parts, 'dp', 0, 0, axis_index_groups=groups)]
    unnamed x38 -> x6, local copies, waits for them, and re-layouts: 5.55 us -> 4.01 us
  transfers between devices with their start and end apart: 19 -> 19, of which waited for: 5 -> 10; matrix products, arithmetic and copies ran while one was open for 1% -> 1% of each run, Pallas kernels for 10% -> 9%
where the time goes in v4:
time: 93 us; the launch traced here: 92.5 us
  starting transfers between devices  33.5 us (36%)
  waiting for transfers between devices  20.4 us (22%)
  blocking collectives  19.6 us (21%)
  Pallas kernels  11.9 us (13%)
  local copies, waits for them, and re-layouts  4.97 us (5%)
  other arithmetic  1.32 us (1%)
    all_to_all x1, blocking collectives, shards(): lax.all_to_all(pair_products(own_up, other, share, members), 'dp', 0, 0)  19.6 us
    ppermute x16, starting transfers between devices, moved(): return lax.ppermute(value, axis, [(i, i ^ distance) for i in range(count)])  15.1 us
    ppermute x16, waiting for transfers between devices, moved(): return lax.ppermute(value, axis, [(i, i ^ distance) for i in range(count)])  14.2 us
    all_to_all x1, starting transfers between devices, shards(): grid = lax.all_to_all(grid, 'section', 0, 0)  7.95 us
    ppermute x1, starting transfers between devices, shards(): other = lax.ppermute(outgoing, ('section', 'dp'), route)  6.58 us
    pallas_call x1, Pallas kernels, run_chain(): pl.pallas_call(kernel, out_shape=jax.ShapeDtypeStruct((rows, LANES), BF16...  5.94 us
    all_to_all x1, waiting for transfers between devices, shards(): grid = lax.all_to_all(grid, 'section', 0, 0)  4.55 us
    unnamed x6, local copies, waits for them, and re-layouts  4.01 us
  transfers between devices with their start and end apart: 19, of which 10 were waited for; matrix products, arithmetic and copies ran while one was open for 1% of the time, Pallas kernels for 9%

profile of v4, /device:TPU:1, one launch (start us, length us, event | category | flops | bytes accessed | tf_op | source)
XLA Modules:
  0.0 92.5 jit_solution(312389659177126356)
XLA Ops:
  0.6 1.3 %broadcast_select_fusion = bf16[24,12288]{1,0:T(8,128)(2,1)S(1)} fusion(pred[]{:T(512)S(6)} %ge.3, bf16[1,24,12288]{2,1,0:T(8,128)(2,1)} %param.4, bf16[1,24,12288]{2,1,0:T(8,128)(2,1)} %param.5), kind=kLoop, calls=%fused_computation | loop fusion | flops 294912 | bytes 1769473 | tf_op jit(solution)/shard_map/jit(_where)/select_n | solution.py:401
  2.0 6.6 %collective-permute-start = (bf16[24,12288]{1,0:T(8,128)(2,1)S(1)}, bf16[24,12288]{1,0:T(8,128)(2,1)S(1)}, u32[]{:S(2)}, u32[]{:S(2)}) collective-permute-start(bf16[24,12288]{1,0:T(8,128)(2,1)S(1)} %broadcast_select_fusion), channel_id=1, source_target_pairs={{0,0},{17,1},{34,2},{51,3},{68,4},{85,5},{102,6},{119,7},{136,8},{... | collective-permute-start | bytes 1769480 | tf_op jit(solution)/shard_map/ppermute | solution.py:402
  8.5 0.9 %dynamic-slice_bitcast_fusion.share_ref = bf16[8,12288]{1,0:T(8,128)(2,1)S(1)} fusion(bf16[16,8,12288]{2,1,0:T(8,128)(2,1)} %bitcast.14, s32[]{:T(128)S(6)} %select_n.18), kind=kLoop, calls=%fused_computation.1 | loop fusion | bytes 393220 | tf_op jit(solution)/shard_map/jit(dynamic_index_in_dim)/squeeze | solution.py:404
  9.5 1.1 %copy-done = bf16[1,24,12288]{2,1,0:T(8,128)(2,1)S(1)} copy-done((bf16[1,24,12288]{2,1,0:T(8,128)(2,1)S(1)}, bf16[1,24,12288]{2,1,0:T(8,128)(2,1)}, u32[]{:S(2)}) %copy-start) | copy-done | bytes 589848
  10.6 1.9 %copy-done.1 = bf16[2,8,8,12288]{3,2,1,0:T(8,128)(2,1)S(1)} copy-done((bf16[2,8,8,12288]{3,2,1,0:T(8,128)(2,1)S(1)}, bf16[2,8,8,12288]{3,2,1,0:T(8,128)(2,1)}, u32[]{:S(2)}) %copy-start.1) | copy-done | bytes 3145752
  12.4 1.1 %copy-done.2 = bf16[1,24,12288]{2,1,0:T(8,128)(2,1)S(1)} copy-done((bf16[1,24,12288]{2,1,0:T(8,128)(2,1)S(1)}, bf16[1,24,12288]{2,1,0:T(8,128)(2,1)}, u32[]{:S(2)}) %copy-start.2) | copy-done | bytes 589848
  13.5 2.2 %shard_map.50 = (f32[48,128]{1,0:T(8,128)S(1)}, f32[1,128]{1,0:T(1,128)S(1)}) custom-call(bf16[128,12288]{1,0:T(8,128)(2,1)S(1)} %bitcast.15, bf16[24,12288]{1,0:T(8,128)(2,1)S(1)} %bitcast.16, bf16[24,12288]{1,0:T(8,128)(2,1)S(1)} %bitcast.12), custom_call_target="tpu_custom_call" | custom-call | tf_op jit(solution)/shard_map/pallas_call | solution.py:52
  16.2 19.6 %all_to_all.15.refs_0_ = bf16[16,64,128]{2,1,0:T(8,128)(2,1)S(1)} all-to-all(bf16[16,64,128]{2,1,0:T(8,128)(2,1)S(1)} %shard_map.51), channel_id=1, replica_groups=mesh['section'=16,'dp'=16] {'dp'}, dimensions={0} | all-to-all | bytes 524288 | tf_op jit(solution)/shard_map/all_to_all | solution.py:415
  35.9 0.9 %shard_map.52 = (bf16[16,128,128]{2,1,0:T(8,128)(2,1)}, bf16[176,768]{1,0:T(8,128)(2,1)S(1)}) custom-call(bf16[16,64,128]{2,1,0:T(8,128)(2,1)S(1)} %all_to_all.15.refs_0_, f32[48,128]{1,0:T(8,128)S(1)} %get-tuple-element.37.refs_1_, bf16[48,768]{1,0:T(8,128)(2,1)S(1)} %pad_maximum_fusion.refs_2_), custom_call_target="tpu_custom_call" | custom-call | tf_op jit(solution)/shard_map/pallas_call | solution.py:138
  36.8 8.0 %all-to-all-start.1 = ((bf16[16,128,128]{2,1,0:T(8,128)(2,1)}), bf16[16,128,128]{2,1,0:T(8,128)(2,1)S(1)}, u32[]{:S(2)}, u32[]{:S(2)}) async-start(bf16[16,128,128]{2,1,0:T(8,128)(2,1)} %get-tuple-element.39), calls=%async_computation.1 | async-start | bytes 1048576 | tf_op jit(solution)/shard_map/all_to_all | solution.py:417
  44.8 1.4 %collective-permute-start.3 = (bf16[176,768]{1,0:T(8,128)(2,1)S(1)}, bf16[176,768]{1,0:T(8,128)(2,1)S(1)}, u32[]{:S(2)}, u32[]{:S(2)}) collective-permute-start(bf16[176,768]{1,0:T(8,128)(2,1)S(1)} %get-tuple-element.53.refs_1_), channel_id=1, source_target_pairs={{0,128},{16,144},{32,160},{48,176},{64,192},{80,208},{96,224},{112... | collective-permute-start | bytes 811016 | tf_op jit(solution)/shard_map/ppermute | solution.py:376
  46.1 2.4 %collective-permute-start.2 = (bf16[176,768]{1,0:T(8,128)(2,1)S(1)}, bf16[176,768]{1,0:T(8,128)(2,1)S(1)}, u32[]{:S(2)}, u32[]{:S(2)}) collective-permute-start(bf16[176,768]{1,0:T(8,128)(2,1)S(1)} %get-tuple-element.53.refs_1_), channel_id=1, source_target_pairs={{0,96},{16,112},{32,64},{48,80},{64,32},{80,48},{96,0},{112,16},{1... | collective-permute-start | bytes 811016 | tf_op jit(solution)/shard_map/ppermute | solution.py:376
  48.5 1.5 %collective-permute-start.5 = (bf16[176,768]{1,0:T(8,128)(2,1)S(1)}, bf16[176,768]{1,0:T(8,128)(2,1)S(1)}, u32[]{:S(2)}, u32[]{:S(2)}) collective-permute-start(bf16[176,768]{1,0:T(8,128)(2,1)S(1)} %get-tuple-element.53.refs_1_), channel_id=1, source_target_pairs={{0,64},{16,80},{32,96},{48,112},{64,0},{80,16},{96,32},{112,48},{1... | collective-permute-start | bytes 811016 | tf_op jit(solution)/shard_map/ppermute | solution.py:376
  50.0 4.6 %all-to-all-done.1.refs_0_ = bf16[16,128,128]{2,1,0:T(8,128)(2,1)S(1)} async-done(((bf16[16,128,128]{2,1,0:T(8,128)(2,1)}), bf16[16,128,128]{2,1,0:T(8,128)(2,1)S(1)}, u32[]{:S(2)}, u32[]{:S(2)}) %all-to-all-start.1) | async-done | bytes 524320 | tf_op jit(solution)/shard_map/all_to_all | solution.py:417
  54.6 5.9 %shard_map.53.refs_0_ = bf16[192,128]{1,0:T(8,128)(2,1)S(1)} custom-call(bf16[16,128,128]{2,1,0:T(8,128)(2,1)S(1)} %all-to-all-done.1.refs_0_, f32[1,128]{1,0:T(1,128)S(1)} %get-tuple-element.40.refs_1_), custom_call_target="tpu_custom_call" | custom-call | tf_op jit(solution)/shard_map/pallas_call | solution.py:286
  60.5 1.4 %collective-permute-start.4 = (bf16[192,128]{1,0:T(8,128)(2,1)S(1)}, bf16[192,128]{1,0:T(8,128)(2,1)S(1)}, u32[]{:S(2)}, u32[]{:S(2)}) collective-permute-start(bf16[192,128]{1,0:T(8,128)(2,1)S(1)} %shard_map.53.refs_0_), channel_id=1, source_target_pairs={{0,8},{1,9},{2,10},{3,11},{4,12},{5,13},{6,14},{7,15},{8,0},{9,1},... | collective-permute-start | bytes 147464 | tf_op jit(solution)/shard_map/ppermute | solution.py:376
  61.9 3.9 %collective-permute-done.5.refs_5_ = bf16[176,768]{1,0:T(8,128)(2,1)S(1)} collective-permute-done((bf16[176,768]{1,0:T(8,128)(2,1)S(1)}, bf16[176,768]{1,0:T(8,128)(2,1)S(1)}, u32[]{:S(2)}, u32[]{:S(2)}) %collective-permute-start.5) | collective-permute-done | bytes 270368 | tf_op jit(solution)/shard_map/ppermute | solution.py:376
  66.7 3.9 %all-to-all-start.2 = ((bf16[8,240,128]{2,1,0:T(8,128)(2,1)}), bf16[8,240,128]{2,1,0:T(8,128)(2,1)S(1)}, u32[]{:S(2)}, u32[]{:S(2)}) async-start(bf16[8,240,128]{2,1,0:T(8,128)(2,1)} %shard_map.54), calls=%async_computation.2 | async-start | bytes 983040 | tf_op jit(solution)/shard_map/all_to_all | solution.py:439
  70.5 2.3 %collective-permute-start.6 = (bf16[176,768]{1,0:T(8,128)(2,1)S(1)}, bf16[176,768]{1,0:T(8,128)(2,1)S(1)}, u32[]{:S(2)}, u32[]{:S(2)}) collective-permute-start(bf16[176,768]{1,0:T(8,128)(2,1)S(1)} %get-tuple-element.53.refs_1_), channel_id=1, source_target_pairs={{0,16},{16,0},{32,48},{48,32},{64,80},{80,64},{96,112},{112,96},{1... | collective-permute-start | bytes 811016 | tf_op jit(solution)/shard_map/ppermute | solution.py:376
  74.6 6.0 %collective-permute-done.10.refs_13_ = bf16[176,768]{1,0:T(8,128)(2,1)S(1)} collective-permute-done((bf16[176,768]{1,0:T(8,128)(2,1)S(1)}, bf16[176,768]{1,0:T(8,128)(2,1)S(1)}, u32[]{:S(2)}, u32[]{:S(2)}) %collective-permute-start.10) | collective-permute-done | bytes 270368 | tf_op jit(solution)/shard_map/ppermute | solution.py:376
  80.6 2.6 %collective-permute-done.11.refs_15_ = bf16[176,768]{1,0:T(8,128)(2,1)S(1)} collective-permute-done((bf16[176,768]{1,0:T(8,128)(2,1)S(1)}, bf16[176,768]{1,0:T(8,128)(2,1)S(1)}, u32[]{:S(2)}, u32[]{:S(2)}) %collective-permute-start.11) | collective-permute-done | bytes 270368 | tf_op jit(solution)/shard_map/ppermute | solution.py:376
  83.2 1.6 %all-to-all-done.2.refs_0_ = bf16[8,240,128]{2,1,0:T(8,128)(2,1)S(1)} async-done(((bf16[8,240,128]{2,1,0:T(8,128)(2,1)}), bf16[8,240,128]{2,1,0:T(8,128)(2,1)S(1)}, u32[]{:S(2)}, u32[]{:S(2)}) %all-to-all-start.2) | async-done | bytes 491552 | tf_op jit(solution)/shard_map/all_to_all | solution.py:439
  84.8 3.4 %collective-permute-start.12 = (bf16[176,768]{1,0:T(8,128)(2,1)S(1)}, bf16[176,768]{1,0:T(8,128)(2,1)S(1)}, u32[]{:S(2)}, u32[]{:S(2)}) collective-permute-start(bf16[176,768]{1,0:T(8,128)(2,1)S(1)} %collective-permute-done.5.refs_5_), channel_id=1, source_target_pairs={{0,16},{16,0},{32,48},{48,32},{64,80},{80,64},{96,112},{112,96},{1... | collective-permute-start | bytes 811016 | tf_op jit(solution)/shard_map/ppermute | solution.py:376
  91.0 1.5 %shard_map.55 = (f32[1,24,768]{2,1,0:T(8,128)}, f32[1,24,768]{2,1,0:T(8,128)}) custom-call(bf16[8,240,128]{2,1,0:T(8,128)(2,1)S(1)} %all-to-all-done.2.refs_0_, bf16[176,768]{1,0:T(8,128)(2,1)S(1)} %get-tuple-element.53.refs_1_, bf16[176,768]{1,0:T(8,128)(2,1)S(1)} %collective-permute-done.6.refs_2_, bf16[176,768]{1,0:T(8,128)(2,1)S(1)} %collective-permute-done.1.refs_3_, ...), custom_call_target="tpu_custom_call" | custom-call | tf_op jit(solution)/shard_map/pallas_call | solution.py:370
  (31 shorter events, 5.8 us)
Async XLA Ops:
  2.0 13.8 %collective-permute-start = (bf16[24,12288]{1,0:T(8,128)(2,1)S(1)}, bf16[24,12288]{1,0:T(8,128)(2,1)S(1)}, u32[]{:S(2)}, u32[]{:S(2)}) collective-permute-start(bf16[24,12288]{1,0:T(8,128)(2,1)S(1)} %broadcast_select_fusion), channel_id=1, source_target_pairs={{0,0},{17,1},{34,2},{51,3},{68,4},{85,5},{102,6},{119,7},{136,8},{... | collective-permute-start | bytes 1769480 | tf_op jit(solution)/shard_map/ppermute | solution.py:402
  9.5 1.1 %copy-start = (bf16[1,24,12288]{2,1,0:T(8,128)(2,1)S(1)}, bf16[1,24,12288]{2,1,0:T(8,128)(2,1)}, u32[]{:S(2)}) copy-start(bf16[1,24,12288]{2,1,0:T(8,128)(2,1)} %param.5) | copy-start | bytes 1769476
  10.6 1.9 %copy-start.1 = (bf16[2,8,8,12288]{3,2,1,0:T(8,128)(2,1)S(1)}, bf16[2,8,8,12288]{3,2,1,0:T(8,128)(2,1)}, u32[]{:S(2)}) copy-start(bf16[2,8,8,12288]{3,2,1,0:T(8,128)(2,1)} %param.3) | copy-start | bytes 9437188
  12.4 1.1 %copy-start.2 = (bf16[1,24,12288]{2,1,0:T(8,128)(2,1)S(1)}, bf16[1,24,12288]{2,1,0:T(8,128)(2,1)}, u32[]{:S(2)}) copy-start(bf16[1,24,12288]{2,1,0:T(8,128)(2,1)} %param.4) | copy-start | bytes 1769476
  36.8 17.8 %all-to-all-start.1 = ((bf16[16,128,128]{2,1,0:T(8,128)(2,1)}), bf16[16,128,128]{2,1,0:T(8,128)(2,1)S(1)}, u32[]{:S(2)}, u32[]{:S(2)}) async-start(bf16[16,128,128]{2,1,0:T(8,128)(2,1)} %get-tuple-element.39), calls=%async_computation.1 | async-start | bytes 1048576 | tf_op jit(solution)/shard_map/all_to_all | solution.py:417
  44.8 15.7 %collective-permute-start.3 = (bf16[176,768]{1,0:T(8,128)(2,1)S(1)}, bf16[176,768]{1,0:T(8,128)(2,1)S(1)}, u32[]{:S(2)}, u32[]{:S(2)}) collective-permute-start(bf16[176,768]{1,0:T(8,128)(2,1)S(1)} %get-tuple-element.53.refs_1_), channel_id=1, source_target_pairs={{0,128},{16,144},{32,160},{48,176},{64,192},{80,208},{96,224},{112... | collective-permute-start | bytes 811016 | tf_op jit(solution)/shard_map/ppermute | solution.py:376
  46.1 14.4 %collective-permute-start.2 = (bf16[176,768]{1,0:T(8,128)(2,1)S(1)}, bf16[176,768]{1,0:T(8,128)(2,1)S(1)}, u32[]{:S(2)}, u32[]{:S(2)}) collective-permute-start(bf16[176,768]{1,0:T(8,128)(2,1)S(1)} %get-tuple-element.53.refs_1_), channel_id=1, source_target_pairs={{0,96},{16,112},{32,64},{48,80},{64,32},{80,48},{96,0},{112,16},{1... | collective-permute-start | bytes 811016 | tf_op jit(solution)/shard_map/ppermute | solution.py:376
  48.5 12.0 %collective-permute-start.1 = (bf16[176,768]{1,0:T(8,128)(2,1)S(1)}, bf16[176,768]{1,0:T(8,128)(2,1)S(1)}, u32[]{:S(2)}, u32[]{:S(2)}) collective-permute-start(bf16[176,768]{1,0:T(8,128)(2,1)S(1)} %get-tuple-element.53.refs_1_), channel_id=1, source_target_pairs={{0,32},{16,48},{32,0},{48,16},{64,96},{80,112},{96,64},{112,80},{1... | collective-permute-start | bytes 811016 | tf_op jit(solution)/shard_map/ppermute | solution.py:376
  48.5 17.3 %collective-permute-start.5 = (bf16[176,768]{1,0:T(8,128)(2,1)S(1)}, bf16[176,768]{1,0:T(8,128)(2,1)S(1)}, u32[]{:S(2)}, u32[]{:S(2)}) collective-permute-start(bf16[176,768]{1,0:T(8,128)(2,1)S(1)} %get-tuple-element.53.refs_1_), channel_id=1, source_target_pairs={{0,64},{16,80},{32,96},{48,112},{64,0},{80,16},{96,32},{112,48},{1... | collective-permute-start | bytes 811016 | tf_op jit(solution)/shard_map/ppermute | solution.py:376
  60.5 5.3 %collective-permute-start.4 = (bf16[192,128]{1,0:T(8,128)(2,1)S(1)}, bf16[192,128]{1,0:T(8,128)(2,1)S(1)}, u32[]{:S(2)}, u32[]{:S(2)}) collective-permute-start(bf16[192,128]{1,0:T(8,128)(2,1)S(1)} %shard_map.53.refs_0_), channel_id=1, source_target_pairs={{0,8},{1,9},{2,10},{3,11},{4,12},{5,13},{6,14},{7,15},{8,0},{9,1},... | collective-permute-start | bytes 147464 | tf_op jit(solution)/shard_map/ppermute | solution.py:376
  66.7 18.2 %all-to-all-start.2 = ((bf16[8,240,128]{2,1,0:T(8,128)(2,1)}), bf16[8,240,128]{2,1,0:T(8,128)(2,1)S(1)}, u32[]{:S(2)}, u32[]{:S(2)}) async-start(bf16[8,240,128]{2,1,0:T(8,128)(2,1)} %shard_map.54), calls=%async_computation.2 | async-start | bytes 983040 | tf_op jit(solution)/shard_map/all_to_all | solution.py:439
  70.5 4.0 %collective-permute-start.6 = (bf16[176,768]{1,0:T(8,128)(2,1)S(1)}, bf16[176,768]{1,0:T(8,128)(2,1)S(1)}, u32[]{:S(2)}, u32[]{:S(2)}) collective-permute-start(bf16[176,768]{1,0:T(8,128)(2,1)S(1)} %get-tuple-element.53.refs_1_), channel_id=1, source_target_pairs={{0,16},{16,0},{32,48},{48,32},{64,80},{80,64},{96,112},{112,96},{1... | collective-permute-start | bytes 811016 | tf_op jit(solution)/shard_map/ppermute | solution.py:376
  72.8 1.7 %collective-permute-start.7 = (bf16[176,768]{1,0:T(8,128)(2,1)S(1)}, bf16[176,768]{1,0:T(8,128)(2,1)S(1)}, u32[]{:S(2)}, u32[]{:S(2)}) collective-permute-start(bf16[176,768]{1,0:T(8,128)(2,1)S(1)} %collective-permute-done.1.refs_3_), channel_id=1, source_target_pairs={{0,16},{16,0},{32,48},{48,32},{64,80},{80,64},{96,112},{112,96},{1... | collective-permute-start | bytes 811016 | tf_op jit(solution)/shard_map/ppermute | solution.py:376
  72.9 7.6 %collective-permute-start.10 = (bf16[176,768]{1,0:T(8,128)(2,1)S(1)}, bf16[176,768]{1,0:T(8,128)(2,1)S(1)}, u32[]{:S(2)}, u32[]{:S(2)}) collective-permute-start(bf16[176,768]{1,0:T(8,128)(2,1)S(1)} %collective-permute-done.5.refs_5_), channel_id=1, source_target_pairs={{0,128},{16,144},{32,160},{48,176},{64,192},{80,208},{96,224},{112... | collective-permute-start | bytes 811016 | tf_op jit(solution)/shard_map/ppermute | solution.py:376
  73.2 7.4 %collective-permute-start.8 = (bf16[176,768]{1,0:T(8,128)(2,1)S(1)}, bf16[176,768]{1,0:T(8,128)(2,1)S(1)}, u32[]{:S(2)}, u32[]{:S(2)}) collective-permute-start(bf16[176,768]{1,0:T(8,128)(2,1)S(1)} %collective-permute-done.2.refs_7_), channel_id=1, source_target_pairs={{0,16},{16,0},{32,48},{48,32},{64,80},{80,64},{96,112},{112,96},{1... | collective-permute-start | bytes 811016 | tf_op jit(solution)/shard_map/ppermute | solution.py:376
  73.9 9.3 %collective-permute-start.11 = (bf16[176,768]{1,0:T(8,128)(2,1)S(1)}, bf16[176,768]{1,0:T(8,128)(2,1)S(1)}, u32[]{:S(2)}, u32[]{:S(2)}) collective-permute-start(bf16[176,768]{1,0:T(8,128)(2,1)S(1)} %collective-permute-done.3.refs_9_), channel_id=1, source_target_pairs={{0,96},{16,112},{32,64},{48,80},{64,32},{80,48},{96,0},{112,16},{1... | collective-permute-start | bytes 811016 | tf_op jit(solution)/shard_map/ppermute | solution.py:376
  74.5 8.7 %collective-permute-start.9 = (bf16[176,768]{1,0:T(8,128)(2,1)S(1)}, bf16[176,768]{1,0:T(8,128)(2,1)S(1)}, u32[]{:S(2)}, u32[]{:S(2)}) collective-permute-start(bf16[176,768]{1,0:T(8,128)(2,1)S(1)} %collective-permute-done.3.refs_9_), channel_id=1, source_target_pairs={{0,32},{16,48},{32,0},{48,16},{64,96},{80,112},{96,64},{112,80},{1... | collective-permute-start | bytes 811016 | tf_op jit(solution)/shard_map/ppermute | solution.py:376
  84.8 4.6 %collective-permute-start.12 = (bf16[176,768]{1,0:T(8,128)(2,1)S(1)}, bf16[176,768]{1,0:T(8,128)(2,1)S(1)}, u32[]{:S(2)}, u32[]{:S(2)}) collective-permute-start(bf16[176,768]{1,0:T(8,128)(2,1)S(1)} %collective-permute-done.5.refs_5_), channel_id=1, source_target_pairs={{0,16},{16,0},{32,48},{48,32},{64,80},{80,64},{96,112},{112,96},{1... | collective-permute-start | bytes 811016 | tf_op jit(solution)/shard_map/ppermute | solution.py:376
  88.3 1.6 %collective-permute-start.13 = (bf16[176,768]{1,0:T(8,128)(2,1)S(1)}, bf16[176,768]{1,0:T(8,128)(2,1)S(1)}, u32[]{:S(2)}, u32[]{:S(2)}) collective-permute-start(bf16[176,768]{1,0:T(8,128)(2,1)S(1)} %collective-permute-done.3.refs_9_), channel_id=1, source_target_pairs={{0,16},{16,0},{32,48},{48,32},{64,80},{80,64},{96,112},{112,96},{1... | collective-permute-start | bytes 811016 | tf_op jit(solution)/shard_map/ppermute | solution.py:376
  88.3 1.9 %collective-permute-start.14 = (bf16[176,768]{1,0:T(8,128)(2,1)S(1)}, bf16[176,768]{1,0:T(8,128)(2,1)S(1)}, u32[]{:S(2)}, u32[]{:S(2)}) collective-permute-start(bf16[176,768]{1,0:T(8,128)(2,1)S(1)} %collective-permute-done.9.refs_11_), channel_id=1, source_target_pairs={{0,16},{16,0},{32,48},{48,32},{64,80},{80,64},{96,112},{112,96},{1... | collective-permute-start | bytes 811016 | tf_op jit(solution)/shard_map/ppermute | solution.py:376
  88.8 1.8 %collective-permute-start.15 = (bf16[176,768]{1,0:T(8,128)(2,1)S(1)}, bf16[176,768]{1,0:T(8,128)(2,1)S(1)}, u32[]{:S(2)}, u32[]{:S(2)}) collective-permute-start(bf16[176,768]{1,0:T(8,128)(2,1)S(1)} %collective-permute-done.10.refs_13_), channel_id=1, source_target_pairs={{0,16},{16,0},{32,48},{48,32},{64,80},{80,64},{96,112},{112,96},{1... | collective-permute-start | bytes 811016 | tf_op jit(solution)/shard_map/ppermute | solution.py:376
  88.8 2.2 %collective-permute-start.16 = (bf16[176,768]{1,0:T(8,128)(2,1)S(1)}, bf16[176,768]{1,0:T(8,128)(2,1)S(1)}, u32[]{:S(2)}, u32[]{:S(2)}) collective-permute-start(bf16[176,768]{1,0:T(8,128)(2,1)S(1)} %collective-permute-done.11.refs_15_), channel_id=1, source_target_pairs={{0,16},{16,0},{32,48},{48,32},{64,80},{80,64},{96,112},{112,96},{1... | collective-permute-start | bytes 811016 | tf_op jit(solution)/shard_map/ppermute | solution.py:376

commit v5 on v4

--- a/solution.py
+++ b/solution.py
@@ -418,7 +418,7 @@
 
     half = sections // 2
     last = half - 2
-    early = (0, 2, last)
+    early = (0, 2, 4, last)
     slices = {d: swapped(share, d, sections) for d in (2, last, half)}
     later = {d: swapped(share, d, sections) for d in range(4, last, 2)}
     parts = run_chain(grid, square, rank, features, normalizer)

time: 93 us -> 93.6 us (level)
  Pallas kernels: 11.9 us -> 12.9 us
    pallas_call x1, Pallas kernels: 1.53 us -> 2.49 us  [finish(): pl.pallas_call(kernel, out_shape=[shape, shape], compiler_params=params())]
where the time goes in v5:
time: 93.6 us; the launch traced here: 93.1 us
  starting transfers between devices  32.9 us (35%)
  waiting for transfers between devices  20.6 us (22%)
  blocking collectives  19.6 us (21%)
  Pallas kernels  12.9 us (14%)
  local copies, waits for them, and re-layouts  4.97 us (5%)
  other arithmetic  1.32 us (1%)
    all_to_all x1, blocking collectives, shards(): lax.all_to_all(pair_products(own_up, other, share, members), 'dp', 0, 0)  19.6 us
    ppermute x16, starting transfers between devices, moved(): return lax.ppermute(value, axis, [(i, i ^ distance) for i in range(count)])  14.6 us
    ppermute x16, waiting for transfers between devices, moved(): return lax.ppermute(value, axis, [(i, i ^ distance) for i in range(count)])  14.1 us
    all_to_all x1, starting transfers between devices, shards(): grid = lax.all_to_all(grid, 'section', 0, 0)  7.95 us
    ppermute x1, starting transfers between devices, shards(): other = lax.ppermute(outgoing, ('section', 'dp'), route)  6.58 us
    pallas_call x1, Pallas kernels, run_chain(): pl.pallas_call(kernel, out_shape=jax.ShapeDtypeStruct((rows, LANES), BF16...  5.94 us
    all_to_all x1, waiting for transfers between devices, shards(): grid = lax.all_to_all(grid, 'section', 0, 0)  4.55 us
    unnamed x6, local copies, waits for them, and re-layouts  4.01 us
  transfers between devices with their start and end apart: 19, of which 10 were waited for; matrix products, arithmetic and copies ran while one was open for 1% of the time, Pallas kernels for 9%

profile of v5, /device:TPU:1, one launch (start us, length us, event | category | flops | bytes accessed | tf_op | source)
XLA Modules:
  0.0 93.1 jit_solution(14938240763496639273)
XLA Ops:
  0.6 1.3 %broadcast_select_fusion = bf16[24,12288]{1,0:T(8,128)(2,1)S(1)} fusion(pred[]{:T(512)S(6)} %ge.3, bf16[1,24,12288]{2,1,0:T(8,128)(2,1)} %param.4, bf16[1,24,12288]{2,1,0:T(8,128)(2,1)} %param.5), kind=kLoop, calls=%fused_computation | loop fusion | flops 294912 | bytes 1769473 | tf_op jit(solution)/shard_map/jit(_where)/select_n | solution.py:401
  2.0 6.6 %collective-permute-start = (bf16[24,12288]{1,0:T(8,128)(2,1)S(1)}, bf16[24,12288]{1,0:T(8,128)(2,1)S(1)}, u32[]{:S(2)}, u32[]{:S(2)}) collective-permute-start(bf16[24,12288]{1,0:T(8,128)(2,1)S(1)} %broadcast_select_fusion), channel_id=1, source_target_pairs={{0,0},{17,1},{34,2},{51,3},{68,4},{85,5},{102,6},{119,7},{136,8},{... | collective-permute-start | bytes 1769480 | tf_op jit(solution)/shard_map/ppermute | solution.py:402
  8.5 0.9 %dynamic-slice_bitcast_fusion.share_ref = bf16[8,12288]{1,0:T(8,128)(2,1)S(1)} fusion(bf16[16,8,12288]{2,1,0:T(8,128)(2,1)} %bitcast.14, s32[]{:T(128)S(6)} %select_n.18), kind=kLoop, calls=%fused_computation.1 | loop fusion | bytes 393220 | tf_op jit(solution)/shard_map/jit(dynamic_index_in_dim)/squeeze | solution.py:404
  9.5 1.1 %copy-done = bf16[1,24,12288]{2,1,0:T(8,128)(2,1)S(1)} copy-done((bf16[1,24,12288]{2,1,0:T(8,128)(2,1)S(1)}, bf16[1,24,12288]{2,1,0:T(8,128)(2,1)}, u32[]{:S(2)}) %copy-start) | copy-done | bytes 589848
  10.6 1.9 %copy-done.1 = bf16[2,8,8,12288]{3,2,1,0:T(8,128)(2,1)S(1)} copy-done((bf16[2,8,8,12288]{3,2,1,0:T(8,128)(2,1)S(1)}, bf16[2,8,8,12288]{3,2,1,0:T(8,128)(2,1)}, u32[]{:S(2)}) %copy-start.1) | copy-done | bytes 3145752
  12.4 1.1 %copy-done.2 = bf16[1,24,12288]{2,1,0:T(8,128)(2,1)S(1)} copy-done((bf16[1,24,12288]{2,1,0:T(8,128)(2,1)S(1)}, bf16[1,24,12288]{2,1,0:T(8,128)(2,1)}, u32[]{:S(2)}) %copy-start.2) | copy-done | bytes 589848
  13.5 2.2 %shard_map.50 = (f32[48,128]{1,0:T(8,128)S(1)}, f32[1,128]{1,0:T(1,128)S(1)}) custom-call(bf16[128,12288]{1,0:T(8,128)(2,1)S(1)} %bitcast.15, bf16[24,12288]{1,0:T(8,128)(2,1)S(1)} %bitcast.16, bf16[24,12288]{1,0:T(8,128)(2,1)S(1)} %bitcast.12), custom_call_target="tpu_custom_call" | custom-call | tf_op jit(solution)/shard_map/pallas_call | solution.py:52
  16.2 19.6 %all_to_all.15.refs_0_ = bf16[16,64,128]{2,1,0:T(8,128)(2,1)S(1)} all-to-all(bf16[16,64,128]{2,1,0:T(8,128)(2,1)S(1)} %shard_map.51), channel_id=1, replica_groups=mesh['section'=16,'dp'=16] {'dp'}, dimensions={0} | all-to-all | bytes 524288 | tf_op jit(solution)/shard_map/all_to_all | solution.py:415
  36.8 8.0 %all-to-all-start.1 = ((bf16[16,128,128]{2,1,0:T(8,128)(2,1)}), bf16[16,128,128]{2,1,0:T(8,128)(2,1)S(1)}, u32[]{:S(2)}, u32[]{:S(2)}) async-start(bf16[16,128,128]{2,1,0:T(8,128)(2,1)} %get-tuple-element.40), calls=%async_computation.1 | async-start | bytes 1048576 | tf_op jit(solution)/shard_map/all_to_all | solution.py:417
  44.8 1.4 %collective-permute-start.3 = (bf16[176,768]{1,0:T(8,128)(2,1)S(1)}, bf16[176,768]{1,0:T(8,128)(2,1)S(1)}, u32[]{:S(2)}, u32[]{:S(2)}) collective-permute-start(bf16[176,768]{1,0:T(8,128)(2,1)S(1)} %get-tuple-element.54.refs_1_), channel_id=1, source_target_pairs={{0,128},{16,144},{32,160},{48,176},{64,192},{80,208},{96,224},{112... | collective-permute-start | bytes 811016 | tf_op jit(solution)/shard_map/ppermute | solution.py:376
  46.1 2.4 %collective-permute-start.2 = (bf16[176,768]{1,0:T(8,128)(2,1)S(1)}, bf16[176,768]{1,0:T(8,128)(2,1)S(1)}, u32[]{:S(2)}, u32[]{:S(2)}) collective-permute-start(bf16[176,768]{1,0:T(8,128)(2,1)S(1)} %get-tuple-element.54.refs_1_), channel_id=1, source_target_pairs={{0,96},{16,112},{32,64},{48,80},{64,32},{80,48},{96,0},{112,16},{1... | collective-permute-start | bytes 811016 | tf_op jit(solution)/shard_map/ppermute | solution.py:376
  48.5 1.5 %collective-permute-start.5 = (bf16[176,768]{1,0:T(8,128)(2,1)S(1)}, bf16[176,768]{1,0:T(8,128)(2,1)S(1)}, u32[]{:S(2)}, u32[]{:S(2)}) collective-permute-start(bf16[176,768]{1,0:T(8,128)(2,1)S(1)} %get-tuple-element.54.refs_1_), channel_id=1, source_target_pairs={{0,64},{16,80},{32,96},{48,112},{64,0},{80,16},{96,32},{112,48},{1... | collective-permute-start | bytes 811016 | tf_op jit(solution)/shard_map/ppermute | solution.py:376
  50.0 4.6 %all-to-all-done.1.refs_0_ = bf16[16,128,128]{2,1,0:T(8,128)(2,1)S(1)} async-done(((bf16[16,128,128]{2,1,0:T(8,128)(2,1)}), bf16[16,128,128]{2,1,0:T(8,128)(2,1)S(1)}, u32[]{:S(2)}, u32[]{:S(2)}) %all-to-all-start.1) | async-done | bytes 524320 | tf_op jit(solution)/shard_map/all_to_all | solution.py:417
  54.6 5.9 %shard_map.53.refs_0_ = bf16[192,128]{1,0:T(8,128)(2,1)S(1)} custom-call(bf16[16,128,128]{2,1,0:T(8,128)(2,1)S(1)} %all-to-all-done.1.refs_0_, f32[1,128]{1,0:T(1,128)S(1)} %get-tuple-element.41.refs_1_), custom_call_target="tpu_custom_call" | custom-call | tf_op jit(solution)/shard_map/pallas_call | solution.py:286
  60.5 1.4 %collective-permute-start.4 = (bf16[192,128]{1,0:T(8,128)(2,1)S(1)}, bf16[192,128]{1,0:T(8,128)(2,1)S(1)}, u32[]{:S(2)}, u32[]{:S(2)}) collective-permute-start(bf16[192,128]{1,0:T(8,128)(2,1)S(1)} %shard_map.53.refs_0_), channel_id=1, source_target_pairs={{0,8},{1,9},{2,10},{3,11},{4,12},{5,13},{6,14},{7,15},{8,0},{9,1},... | collective-permute-start | bytes 147464 | tf_op jit(solution)/shard_map/ppermute | solution.py:376
  61.9 3.9 %collective-permute-done.5.refs_5_ = bf16[176,768]{1,0:T(8,128)(2,1)S(1)} collective-permute-done((bf16[176,768]{1,0:T(8,128)(2,1)S(1)}, bf16[176,768]{1,0:T(8,128)(2,1)S(1)}, u32[]{:S(2)}, u32[]{:S(2)}) %collective-permute-start.5) | collective-permute-done | bytes 270368 | tf_op jit(solution)/shard_map/ppermute | solution.py:376
  66.7 3.9 %all-to-all-start.2 = ((bf16[8,240,128]{2,1,0:T(8,128)(2,1)}), bf16[8,240,128]{2,1,0:T(8,128)(2,1)S(1)}, u32[]{:S(2)}, u32[]{:S(2)}) async-start(bf16[8,240,128]{2,1,0:T(8,128)(2,1)} %shard_map.54), calls=%async_computation.2 | async-start | bytes 983040 | tf_op jit(solution)/shard_map/all_to_all | solution.py:439
  70.5 2.3 %collective-permute-start.6 = (bf16[176,768]{1,0:T(8,128)(2,1)S(1)}, bf16[176,768]{1,0:T(8,128)(2,1)S(1)}, u32[]{:S(2)}, u32[]{:S(2)}) collective-permute-start(bf16[176,768]{1,0:T(8,128)(2,1)S(1)} %get-tuple-element.54.refs_1_), channel_id=1, source_target_pairs={{0,16},{16,0},{32,48},{48,32},{64,80},{80,64},{96,112},{112,96},{1... | collective-permute-start | bytes 811016 | tf_op jit(solution)/shard_map/ppermute | solution.py:376
  75.5 5.2 %collective-permute-done.11.refs_13_ = bf16[176,768]{1,0:T(8,128)(2,1)S(1)} collective-permute-done((bf16[176,768]{1,0:T(8,128)(2,1)S(1)}, bf16[176,768]{1,0:T(8,128)(2,1)S(1)}, u32[]{:S(2)}, u32[]{:S(2)}) %collective-permute-start.11) | collective-permute-done | bytes 270368 | tf_op jit(solution)/shard_map/ppermute | solution.py:376
  80.7 2.2 %collective-permute-done.12.refs_15_ = bf16[176,768]{1,0:T(8,128)(2,1)S(1)} collective-permute-done((bf16[176,768]{1,0:T(8,128)(2,1)S(1)}, bf16[176,768]{1,0:T(8,128)(2,1)S(1)}, u32[]{:S(2)}, u32[]{:S(2)}) %collective-permute-start.12) | collective-permute-done | bytes 270368 | tf_op jit(solution)/shard_map/ppermute | solution.py:376
  82.9 2.0 %all-to-all-done.2.refs_0_ = bf16[8,240,128]{2,1,0:T(8,128)(2,1)S(1)} async-done(((bf16[8,240,128]{2,1,0:T(8,128)(2,1)}), bf16[8,240,128]{2,1,0:T(8,128)(2,1)S(1)}, u32[]{:S(2)}, u32[]{:S(2)}) %all-to-all-start.2) | async-done | bytes 491552 | tf_op jit(solution)/shard_map/all_to_all | solution.py:439
  84.8 3.4 %collective-permute-start.13 = (bf16[176,768]{1,0:T(8,128)(2,1)S(1)}, bf16[176,768]{1,0:T(8,128)(2,1)S(1)}, u32[]{:S(2)}, u32[]{:S(2)}) collective-permute-start(bf16[176,768]{1,0:T(8,128)(2,1)S(1)} %collective-permute-done.3.refs_9_), channel_id=1, source_target_pairs={{0,16},{16,0},{32,48},{48,32},{64,80},{80,64},{96,112},{112,96},{1... | collective-permute-start | bytes 811016 | tf_op jit(solution)/shard_map/ppermute | solution.py:376
  88.8 1.0 %collective-permute-done.13.refs_10_ = bf16[176,768]{1,0:T(8,128)(2,1)S(1)} collective-permute-done((bf16[176,768]{1,0:T(8,128)(2,1)S(1)}, bf16[176,768]{1,0:T(8,128)(2,1)S(1)}, u32[]{:S(2)}, u32[]{:S(2)}) %collective-permute-start.13) | collective-permute-done | bytes 270368 | tf_op jit(solution)/shard_map/ppermute | solution.py:376
  90.6 2.5 %shard_map.55 = (f32[1,24,768]{2,1,0:T(8,128)}, f32[1,24,768]{2,1,0:T(8,128)}) custom-call(bf16[8,240,128]{2,1,0:T(8,128)(2,1)S(1)} %all-to-all-done.2.refs_0_, bf16[176,768]{1,0:T(8,128)(2,1)S(1)} %get-tuple-element.54.refs_1_, bf16[176,768]{1,0:T(8,128)(2,1)S(1)} %collective-permute-done.6.refs_2_, bf16[176,768]{1,0:T(8,128)(2,1)S(1)} %collective-permute-done.1.refs_3_, ...), custom_call_target="tpu_custom_call" | custom-call | tf_op jit(solution)/shard_map/pallas_call | solution.py:370
  (31 shorter events, 6.2 us)
Async XLA Ops:
  2.0 13.8 %collective-permute-start = (bf16[24,12288]{1,0:T(8,128)(2,1)S(1)}, bf16[24,12288]{1,0:T(8,128)(2,1)S(1)}, u32[]{:S(2)}, u32[]{:S(2)}) collective-permute-start(bf16[24,12288]{1,0:T(8,128)(2,1)S(1)} %broadcast_select_fusion), channel_id=1, source_target_pairs={{0,0},{17,1},{34,2},{51,3},{68,4},{85,5},{102,6},{119,7},{136,8},{... | collective-permute-start | bytes 1769480 | tf_op jit(solution)/shard_map/ppermute | solution.py:402
  9.5 1.1 %copy-start = (bf16[1,24,12288]{2,1,0:T(8,128)(2,1)S(1)}, bf16[1,24,12288]{2,1,0:T(8,128)(2,1)}, u32[]{:S(2)}) copy-start(bf16[1,24,12288]{2,1,0:T(8,128)(2,1)} %param.5) | copy-start | bytes 1769476
  10.6 1.9 %copy-start.1 = (bf16[2,8,8,12288]{3,2,1,0:T(8,128)(2,1)S(1)}, bf16[2,8,8,12288]{3,2,1,0:T(8,128)(2,1)}, u32[]{:S(2)}) copy-start(bf16[2,8,8,12288]{3,2,1,0:T(8,128)(2,1)} %param.3) | copy-start | bytes 9437188
  12.4 1.1 %copy-start.2 = (bf16[1,24,12288]{2,1,0:T(8,128)(2,1)S(1)}, bf16[1,24,12288]{2,1,0:T(8,128)(2,1)}, u32[]{:S(2)}) copy-start(bf16[1,24,12288]{2,1,0:T(8,128)(2,1)} %param.4) | copy-start | bytes 1769476
  36.8 17.8 %all-to-all-start.1 = ((bf16[16,128,128]{2,1,0:T(8,128)(2,1)}), bf16[16,128,128]{2,1,0:T(8,128)(2,1)S(1)}, u32[]{:S(2)}, u32[]{:S(2)}) async-start(bf16[16,128,128]{2,1,0:T(8,128)(2,1)} %get-tuple-element.40), calls=%async_computation.1 | async-start | bytes 1048576 | tf_op jit(solution)/shard_map/all_to_all | solution.py:417
  44.8 15.7 %collective-permute-start.3 = (bf16[176,768]{1,0:T(8,128)(2,1)S(1)}, bf16[176,768]{1,0:T(8,128)(2,1)S(1)}, u32[]{:S(2)}, u32[]{:S(2)}) collective-permute-start(bf16[176,768]{1,0:T(8,128)(2,1)S(1)} %get-tuple-element.54.refs_1_), channel_id=1, source_target_pairs={{0,128},{16,144},{32,160},{48,176},{64,192},{80,208},{96,224},{112... | collective-permute-start | bytes 811016 | tf_op jit(solution)/shard_map/ppermute | solution.py:376
  46.1 14.4 %collective-permute-start.2 = (bf16[176,768]{1,0:T(8,128)(2,1)S(1)}, bf16[176,768]{1,0:T(8,128)(2,1)S(1)}, u32[]{:S(2)}, u32[]{:S(2)}) collective-permute-start(bf16[176,768]{1,0:T(8,128)(2,1)S(1)} %get-tuple-element.54.refs_1_), channel_id=1, source_target_pairs={{0,96},{16,112},{32,64},{48,80},{64,32},{80,48},{96,0},{112,16},{1... | collective-permute-start | bytes 811016 | tf_op jit(solution)/shard_map/ppermute | solution.py:376
  48.5 12.0 %collective-permute-start.1 = (bf16[176,768]{1,0:T(8,128)(2,1)S(1)}, bf16[176,768]{1,0:T(8,128)(2,1)S(1)}, u32[]{:S(2)}, u32[]{:S(2)}) collective-permute-start(bf16[176,768]{1,0:T(8,128)(2,1)S(1)} %get-tuple-element.54.refs_1_), channel_id=1, source_target_pairs={{0,32},{16,48},{32,0},{48,16},{64,96},{80,112},{96,64},{112,80},{1... | collective-permute-start | bytes 811016 | tf_op jit(solution)/shard_map/ppermute | solution.py:376
  48.5 17.3 %collective-permute-start.5 = (bf16[176,768]{1,0:T(8,128)(2,1)S(1)}, bf16[176,768]{1,0:T(8,128)(2,1)S(1)}, u32[]{:S(2)}, u32[]{:S(2)}) collective-permute-start(bf16[176,768]{1,0:T(8,128)(2,1)S(1)} %get-tuple-element.54.refs_1_), channel_id=1, source_target_pairs={{0,64},{16,80},{32,96},{48,112},{64,0},{80,16},{96,32},{112,48},{1... | collective-permute-start | bytes 811016 | tf_op jit(solution)/shard_map/ppermute | solution.py:376
  60.5 5.3 %collective-permute-start.4 = (bf16[192,128]{1,0:T(8,128)(2,1)S(1)}, bf16[192,128]{1,0:T(8,128)(2,1)S(1)}, u32[]{:S(2)}, u32[]{:S(2)}) collective-permute-start(bf16[192,128]{1,0:T(8,128)(2,1)S(1)} %shard_map.53.refs_0_), channel_id=1, source_target_pairs={{0,8},{1,9},{2,10},{3,11},{4,12},{5,13},{6,14},{7,15},{8,0},{9,1},... | collective-permute-start | bytes 147464 | tf_op jit(solution)/shard_map/ppermute | solution.py:376
  66.7 18.2 %all-to-all-start.2 = ((bf16[8,240,128]{2,1,0:T(8,128)(2,1)}), bf16[8,240,128]{2,1,0:T(8,128)(2,1)S(1)}, u32[]{:S(2)}, u32[]{:S(2)}) async-start(bf16[8,240,128]{2,1,0:T(8,128)(2,1)} %shard_map.54), calls=%async_computation.2 | async-start | bytes 983040 | tf_op jit(solution)/shard_map/all_to_all | solution.py:439
  70.5 3.5 %collective-permute-start.6 = (bf16[176,768]{1,0:T(8,128)(2,1)S(1)}, bf16[176,768]{1,0:T(8,128)(2,1)S(1)}, u32[]{:S(2)}, u32[]{:S(2)}) collective-permute-start(bf16[176,768]{1,0:T(8,128)(2,1)S(1)} %get-tuple-element.54.refs_1_), channel_id=1, source_target_pairs={{0,16},{16,0},{32,48},{48,32},{64,80},{80,64},{96,112},{112,96},{1... | collective-permute-start | bytes 811016 | tf_op jit(solution)/shard_map/ppermute | solution.py:376
  72.8 1.7 %collective-permute-start.7 = (bf16[176,768]{1,0:T(8,128)(2,1)S(1)}, bf16[176,768]{1,0:T(8,128)(2,1)S(1)}, u32[]{:S(2)}, u32[]{:S(2)}) collective-permute-start(bf16[176,768]{1,0:T(8,128)(2,1)S(1)} %collective-permute-done.1.refs_3_), channel_id=1, source_target_pairs={{0,16},{16,0},{32,48},{48,32},{64,80},{80,64},{96,112},{112,96},{1... | collective-permute-start | bytes 811016 | tf_op jit(solution)/shard_map/ppermute | solution.py:376
  72.9 7.8 %collective-permute-start.11 = (bf16[176,768]{1,0:T(8,128)(2,1)S(1)}, bf16[176,768]{1,0:T(8,128)(2,1)S(1)}, u32[]{:S(2)}, u32[]{:S(2)}) collective-permute-start(bf16[176,768]{1,0:T(8,128)(2,1)S(1)} %collective-permute-done.5.refs_5_), channel_id=1, source_target_pairs={{0,128},{16,144},{32,160},{48,176},{64,192},{80,208},{96,224},{112... | collective-permute-start | bytes 811016 | tf_op jit(solution)/shard_map/ppermute | solution.py:376
  73.2 7.5 %collective-permute-start.8 = (bf16[176,768]{1,0:T(8,128)(2,1)S(1)}, bf16[176,768]{1,0:T(8,128)(2,1)S(1)}, u32[]{:S(2)}, u32[]{:S(2)}) collective-permute-start(bf16[176,768]{1,0:T(8,128)(2,1)S(1)} %collective-permute-done.5.refs_5_), channel_id=1, source_target_pairs={{0,16},{16,0},{32,48},{48,32},{64,80},{80,64},{96,112},{112,96},{1... | collective-permute-start | bytes 811016 | tf_op jit(solution)/shard_map/ppermute | solution.py:376
  73.9 1.6 %collective-permute-start.9 = (bf16[176,768]{1,0:T(8,128)(2,1)S(1)}, bf16[176,768]{1,0:T(8,128)(2,1)S(1)}, u32[]{:S(2)}, u32[]{:S(2)}) collective-permute-start(bf16[176,768]{1,0:T(8,128)(2,1)S(1)} %collective-permute-done.2.refs_7_), channel_id=1, source_target_pairs={{0,16},{16,0},{32,48},{48,32},{64,80},{80,64},{96,112},{112,96},{1... | collective-permute-start | bytes 811016 | tf_op jit(solution)/shard_map/ppermute | solution.py:376
  74.0 8.9 %collective-permute-start.12 = (bf16[176,768]{1,0:T(8,128)(2,1)S(1)}, bf16[176,768]{1,0:T(8,128)(2,1)S(1)}, u32[]{:S(2)}, u32[]{:S(2)}) collective-permute-start(bf16[176,768]{1,0:T(8,128)(2,1)S(1)} %collective-permute-done.3.refs_9_), channel_id=1, source_target_pairs={{0,96},{16,112},{32,64},{48,80},{64,32},{80,48},{96,0},{112,16},{1... | collective-permute-start | bytes 811016 | tf_op jit(solution)/shard_map/ppermute | solution.py:376
  74.6 8.3 %collective-permute-start.10 = (bf16[176,768]{1,0:T(8,128)(2,1)S(1)}, bf16[176,768]{1,0:T(8,128)(2,1)}, u32[]{:S(2)}, u32[]{:S(2)}) collective-permute-start(bf16[176,768]{1,0:T(8,128)(2,1)S(1)} %collective-permute-done.3.refs_9_), channel_id=1, source_target_pairs={{0,32},{16,48},{32,0},{48,16},{64,96},{80,112},{96,64},{112,80},{1... | collective-permute-start | bytes 811016 | tf_op jit(solution)/shard_map/ppermute | solution.py:376
  84.8 5.0 %collective-permute-start.13 = (bf16[176,768]{1,0:T(8,128)(2,1)S(1)}, bf16[176,768]{1,0:T(8,128)(2,1)S(1)}, u32[]{:S(2)}, u32[]{:S(2)}) collective-permute-start(bf16[176,768]{1,0:T(8,128)(2,1)S(1)} %collective-permute-done.3.refs_9_), channel_id=1, source_target_pairs={{0,16},{16,0},{32,48},{48,32},{64,80},{80,64},{96,112},{112,96},{1... | collective-permute-start | bytes 811016 | tf_op jit(solution)/shard_map/ppermute | solution.py:376
  88.3 2.1 %collective-permute-start.14 = (bf16[176,768]{1,0:T(8,128)(2,1)}, bf16[176,768]{1,0:T(8,128)(2,1)S(1)}, u32[]{:S(2)}, u32[]{:S(2)}) collective-permute-start(bf16[176,768]{1,0:T(8,128)(2,1)} %collective-permute-done.10.refs_11_), channel_id=1, source_target_pairs={{0,16},{16,0},{32,48},{48,32},{64,80},{80,64},{96,112},{112,96},{1... | collective-permute-start | bytes 811016 | tf_op jit(solution)/shard_map/ppermute | solution.py:376
  88.3 2.1 %collective-permute-start.15 = (bf16[176,768]{1,0:T(8,128)(2,1)S(1)}, bf16[176,768]{1,0:T(8,128)(2,1)S(1)}, u32[]{:S(2)}, u32[]{:S(2)}) collective-permute-start(bf16[176,768]{1,0:T(8,128)(2,1)S(1)} %collective-permute-done.11.refs_13_), channel_id=1, source_target_pairs={{0,16},{16,0},{32,48},{48,32},{64,80},{80,64},{96,112},{112,96},{1... | collective-permute-start | bytes 811016 | tf_op jit(solution)/shard_map/ppermute | solution.py:376
  88.8 1.8 %collective-permute-start.16 = (bf16[176,768]{1,0:T(8,128)(2,1)S(1)}, bf16[176,768]{1,0:T(8,128)(2,1)S(1)}, u32[]{:S(2)}, u32[]{:S(2)}) collective-permute-start(bf16[176,768]{1,0:T(8,128)(2,1)S(1)} %collective-permute-done.12.refs_15_), channel_id=1, source_target_pairs={{0,16},{16,0},{32,48},{48,32},{64,80},{80,64},{96,112},{112,96},{1... | collective-permute-start | bytes 811016 | tf_op jit(solution)/shard_map/ppermute | solution.py:376

commit v6 on v4

--- a/solution.py
+++ b/solution.py
@@ -428,9 +428,8 @@
     other = moved(parts, "dp", line, members)
     parts, other, slices, later = lax.optimization_barrier((parts, other, slices, later))
     slices = {0: share, **slices, **later}
-    for d in (2, last):
-        slices[half + d] = swapped(slices[half], d, sections)
-    for d in range(4, last, 2):
+    slices[half + last] = swapped(slices[half], last, sections)
+    for d in range(2, last, 2):
         slices[half + d] = swapped(slices[d], half, sections)
     for d in early:
         slices[d + 1] = swapped(slices[d], 1, sections)

time: 93 us -> 93 us (level)
    ppermute x16, waiting for transfers between devices: 14.2 us -> 16.3 us  [moved(): return lax.ppermute(value, axis, [(i, i ^ distance) for i in range(count)])]
    all_to_all x1, waiting for transfers between devices: 1.61 us -> 0.01 us  [shards(): parts = lax.all_to_all(parts, 'dp', 0, 0, axis_index_groups=groups)]
where the time goes in v6:
time: 93 us; the launch traced here: 92.5 us
  starting transfers between devices  33.1 us (36%)
  waiting for transfers between devices  20.9 us (22%)
  blocking collectives  19.6 us (21%)
  Pallas kernels  11.9 us (13%)
  local copies, waits for them, and re-layouts  4.97 us (5%)
  other arithmetic  1.32 us (1%)
    all_to_all x1, blocking collectives, shards(): lax.all_to_all(pair_products(own_up, other, share, members), 'dp', 0, 0)  19.6 us
    ppermute x16, waiting for transfers between devices, moved(): return lax.ppermute(value, axis, [(i, i ^ distance) for i in range(count)])  16.3 us
    ppermute x16, starting transfers between devices, moved(): return lax.ppermute(value, axis, [(i, i ^ distance) for i in range(count)])  14.7 us
    all_to_all x1, starting transfers between devices, shards(): grid = lax.all_to_all(grid, 'section', 0, 0)  7.95 us
    ppermute x1, starting transfers between devices, shards(): other = lax.ppermute(outgoing, ('section', 'dp'), route)  6.58 us
    pallas_call x1, Pallas kernels, run_chain(): pl.pallas_call(kernel, out_shape=jax.ShapeDtypeStruct((rows, LANES), BF16...  5.94 us
    all_to_all x1, waiting for transfers between devices, shards(): grid = lax.all_to_all(grid, 'section', 0, 0)  4.55 us
    unnamed x6, local copies, waits for them, and re-layouts  4.01 us
  transfers between devices with their start and end apart: 19, of which 10 were waited for; matrix products, arithmetic and copies ran while one was open for 1% of the time, Pallas kernels for 9%

profile of v6, /device:TPU:1, one launch (start us, length us, event | category | flops | bytes accessed | tf_op | source)
XLA Modules:
  0.0 92.5 jit_solution(15795970083081678091)
XLA Ops:
  0.6 1.3 %broadcast_select_fusion = bf16[24,12288]{1,0:T(8,128)(2,1)S(1)} fusion(pred[]{:T(512)S(6)} %ge.3, bf16[1,24,12288]{2,1,0:T(8,128)(2,1)} %param.4, bf16[1,24,12288]{2,1,0:T(8,128)(2,1)} %param.5), kind=kLoop, calls=%fused_computation | loop fusion | flops 294912 | bytes 1769473 | tf_op jit(solution)/shard_map/jit(_where)/select_n | solution.py:401
  2.0 6.6 %collective-permute-start = (bf16[24,12288]{1,0:T(8,128)(2,1)S(1)}, bf16[24,12288]{1,0:T(8,128)(2,1)S(1)}, u32[]{:S(2)}, u32[]{:S(2)}) collective-permute-start(bf16[24,12288]{1,0:T(8,128)(2,1)S(1)} %broadcast_select_fusion), channel_id=1, source_target_pairs={{0,0},{17,1},{34,2},{51,3},{68,4},{85,5},{102,6},{119,7},{136,8},{... | collective-permute-start | bytes 1769480 | tf_op jit(solution)/shard_map/ppermute | solution.py:402
  8.5 0.9 %dynamic-slice_bitcast_fusion.share_ref = bf16[8,12288]{1,0:T(8,128)(2,1)S(1)} fusion(bf16[16,8,12288]{2,1,0:T(8,128)(2,1)} %bitcast.14, s32[]{:T(128)S(6)} %select_n.18), kind=kLoop, calls=%fused_computation.1 | loop fusion | bytes 393220 | tf_op jit(solution)/shard_map/jit(dynamic_index_in_dim)/squeeze | solution.py:404
  9.5 1.1 %copy-done = bf16[1,24,12288]{2,1,0:T(8,128)(2,1)S(1)} copy-done((bf16[1,24,12288]{2,1,0:T(8,128)(2,1)S(1)}, bf16[1,24,12288]{2,1,0:T(8,128)(2,1)}, u32[]{:S(2)}) %copy-start) | copy-done | bytes 589848
  10.6 1.9 %copy-done.1 = bf16[2,8,8,12288]{3,2,1,0:T(8,128)(2,1)S(1)} copy-done((bf16[2,8,8,12288]{3,2,1,0:T(8,128)(2,1)S(1)}, bf16[2,8,8,12288]{3,2,1,0:T(8,128)(2,1)}, u32[]{:S(2)}) %copy-start.1) | copy-done | bytes 3145752
  12.4 1.1 %copy-done.2 = bf16[1,24,12288]{2,1,0:T(8,128)(2,1)S(1)} copy-done((bf16[1,24,12288]{2,1,0:T(8,128)(2,1)S(1)}, bf16[1,24,12288]{2,1,0:T(8,128)(2,1)}, u32[]{:S(2)}) %copy-start.2) | copy-done | bytes 589848
  13.5 2.2 %shard_map.50 = (f32[48,128]{1,0:T(8,128)S(1)}, f32[1,128]{1,0:T(1,128)S(1)}) custom-call(bf16[128,12288]{1,0:T(8,128)(2,1)S(1)} %bitcast.15, bf16[24,12288]{1,0:T(8,128)(2,1)S(1)} %bitcast.16, bf16[24,12288]{1,0:T(8,128)(2,1)S(1)} %bitcast.12), custom_call_target="tpu_custom_call" | custom-call | tf_op jit(solution)/shard_map/pallas_call | solution.py:52
  16.2 19.6 %all_to_all.15.refs_0_ = bf16[16,64,128]{2,1,0:T(8,128)(2,1)S(1)} all-to-all(bf16[16,64,128]{2,1,0:T(8,128)(2,1)S(1)} %shard_map.51), channel_id=1, replica_groups=mesh['section'=16,'dp'=16] {'dp'}, dimensions={0} | all-to-all | bytes 524288 | tf_op jit(solution)/shard_map/all_to_all | solution.py:415
  36.8 8.0 %all-to-all-start.1 = ((bf16[16,128,128]{2,1,0:T(8,128)(2,1)}), bf16[16,128,128]{2,1,0:T(8,128)(2,1)S(1)}, u32[]{:S(2)}, u32[]{:S(2)}) async-start(bf16[16,128,128]{2,1,0:T(8,128)(2,1)} %get-tuple-element.39), calls=%async_computation.1 | async-start | bytes 1048576 | tf_op jit(solution)/shard_map/all_to_all | solution.py:417
  44.8 1.4 %collective-permute-start.3 = (bf16[176,768]{1,0:T(8,128)(2,1)S(1)}, bf16[176,768]{1,0:T(8,128)(2,1)S(1)}, u32[]{:S(2)}, u32[]{:S(2)}) collective-permute-start(bf16[176,768]{1,0:T(8,128)(2,1)S(1)} %get-tuple-element.53.refs_1_), channel_id=1, source_target_pairs={{0,128},{16,144},{32,160},{48,176},{64,192},{80,208},{96,224},{112... | collective-permute-start | bytes 811016 | tf_op jit(solution)/shard_map/ppermute | solution.py:376
  46.1 2.4 %collective-permute-start.2 = (bf16[176,768]{1,0:T(8,128)(2,1)S(1)}, bf16[176,768]{1,0:T(8,128)(2,1)S(1)}, u32[]{:S(2)}, u32[]{:S(2)}) collective-permute-start(bf16[176,768]{1,0:T(8,128)(2,1)S(1)} %get-tuple-element.53.refs_1_), channel_id=1, source_target_pairs={{0,96},{16,112},{32,64},{48,80},{64,32},{80,48},{96,0},{112,16},{1... | collective-permute-start | bytes 811016 | tf_op jit(solution)/shard_map/ppermute | solution.py:376
  48.5 1.5 %collective-permute-start.5 = (bf16[176,768]{1,0:T(8,128)(2,1)S(1)}, bf16[176,768]{1,0:T(8,128)(2,1)S(1)}, u32[]{:S(2)}, u32[]{:S(2)}) collective-permute-start(bf16[176,768]{1,0:T(8,128)(2,1)S(1)} %get-tuple-element.53.refs_1_), channel_id=1, source_target_pairs={{0,64},{16,80},{32,96},{48,112},{64,0},{80,16},{96,32},{112,48},{1... | collective-permute-start | bytes 811016 | tf_op jit(solution)/shard_map/ppermute | solution.py:376
  50.0 4.6 %all-to-all-done.1.refs_0_ = bf16[16,128,128]{2,1,0:T(8,128)(2,1)S(1)} async-done(((bf16[16,128,128]{2,1,0:T(8,128)(2,1)}), bf16[16,128,128]{2,1,0:T(8,128)(2,1)S(1)}, u32[]{:S(2)}, u32[]{:S(2)}) %all-to-all-start.1) | async-done | bytes 524320 | tf_op jit(solution)/shard_map/all_to_all | solution.py:417
  54.6 5.9 %shard_map.53.refs_0_ = bf16[192,128]{1,0:T(8,128)(2,1)S(1)} custom-call(bf16[16,128,128]{2,1,0:T(8,128)(2,1)S(1)} %all-to-all-done.1.refs_0_, f32[1,128]{1,0:T(1,128)S(1)} %get-tuple-element.40.refs_1_), custom_call_target="tpu_custom_call" | custom-call | tf_op jit(solution)/shard_map/pallas_call | solution.py:286
  60.5 1.4 %collective-permute-start.4 = (bf16[192,128]{1,0:T(8,128)(2,1)S(1)}, bf16[192,128]{1,0:T(8,128)(2,1)S(1)}, u32[]{:S(2)}, u32[]{:S(2)}) collective-permute-start(bf16[192,128]{1,0:T(8,128)(2,1)S(1)} %shard_map.53.refs_0_), channel_id=1, source_target_pairs={{0,8},{1,9},{2,10},{3,11},{4,12},{5,13},{6,14},{7,15},{8,0},{9,1},... | collective-permute-start | bytes 147464 | tf_op jit(solution)/shard_map/ppermute | solution.py:376
  61.9 3.9 %collective-permute-done.5.refs_5_ = bf16[176,768]{1,0:T(8,128)(2,1)S(1)} collective-permute-done((bf16[176,768]{1,0:T(8,128)(2,1)S(1)}, bf16[176,768]{1,0:T(8,128)(2,1)S(1)}, u32[]{:S(2)}, u32[]{:S(2)}) %collective-permute-start.5) | collective-permute-done | bytes 270368 | tf_op jit(solution)/shard_map/ppermute | solution.py:376
  66.7 3.9 %all-to-all-start.2 = ((bf16[8,240,128]{2,1,0:T(8,128)(2,1)}), bf16[8,240,128]{2,1,0:T(8,128)(2,1)S(1)}, u32[]{:S(2)}, u32[]{:S(2)}) async-start(bf16[8,240,128]{2,1,0:T(8,128)(2,1)} %shard_map.54), calls=%async_computation.2 | async-start | bytes 983040 | tf_op jit(solution)/shard_map/all_to_all | solution.py:438
  70.5 2.3 %collective-permute-start.6 = (bf16[176,768]{1,0:T(8,128)(2,1)S(1)}, bf16[176,768]{1,0:T(8,128)(2,1)S(1)}, u32[]{:S(2)}, u32[]{:S(2)}) collective-permute-start(bf16[176,768]{1,0:T(8,128)(2,1)S(1)} %get-tuple-element.53.refs_1_), channel_id=1, source_target_pairs={{0,16},{16,0},{32,48},{48,32},{64,80},{80,64},{96,112},{112,96},{1... | collective-permute-start | bytes 811016 | tf_op jit(solution)/shard_map/ppermute | solution.py:376
  74.1 1.1 %collective-permute-start.9 = (bf16[176,768]{1,0:T(8,128)(2,1)S(1)}, bf16[176,768]{1,0:T(8,128)(2,1)S(1)}, u32[]{:S(2)}, u32[]{:S(2)}) collective-permute-start(bf16[176,768]{1,0:T(8,128)(2,1)S(1)} %collective-permute-done.1.refs_3_), channel_id=1, source_target_pairs={{0,128},{16,144},{32,160},{48,176},{64,192},{80,208},{96,224},{112... | collective-permute-start | bytes 811016 | tf_op jit(solution)/shard_map/ppermute | solution.py:376
  76.0 4.9 %collective-permute-done.10.refs_13_ = bf16[176,768]{1,0:T(8,128)(2,1)S(1)} collective-permute-done((bf16[176,768]{1,0:T(8,128)(2,1)S(1)}, bf16[176,768]{1,0:T(8,128)(2,1)S(1)}, u32[]{:S(2)}, u32[]{:S(2)}) %collective-permute-start.10) | collective-permute-done | bytes 270368 | tf_op jit(solution)/shard_map/ppermute | solution.py:376
  80.9 1.7 %collective-permute-done.11.refs_15_ = bf16[176,768]{1,0:T(8,128)(2,1)S(1)} collective-permute-done((bf16[176,768]{1,0:T(8,128)(2,1)S(1)}, bf16[176,768]{1,0:T(8,128)(2,1)S(1)}, u32[]{:S(2)}, u32[]{:S(2)}) %collective-permute-start.11) | collective-permute-done | bytes 270368 | tf_op jit(solution)/shard_map/ppermute | solution.py:376
  82.6 4.0 %collective-permute-done.9.refs_11_ = bf16[176,768]{1,0:T(8,128)(2,1)S(1)} collective-permute-done((bf16[176,768]{1,0:T(8,128)(2,1)S(1)}, bf16[176,768]{1,0:T(8,128)(2,1)S(1)}, u32[]{:S(2)}, u32[]{:S(2)}) %collective-permute-start.9) | collective-permute-done | bytes 270368 | tf_op jit(solution)/shard_map/ppermute | solution.py:376
  86.7 1.6 %collective-permute-start.12 = (bf16[176,768]{1,0:T(8,128)(2,1)S(1)}, bf16[176,768]{1,0:T(8,128)(2,1)S(1)}, u32[]{:S(2)}, u32[]{:S(2)}) collective-permute-start(bf16[176,768]{1,0:T(8,128)(2,1)S(1)} %collective-permute-done.5.refs_5_), channel_id=1, source_target_pairs={{0,16},{16,0},{32,48},{48,32},{64,80},{80,64},{96,112},{112,96},{1... | collective-permute-start | bytes 811016 | tf_op jit(solution)/shard_map/ppermute | solution.py:376
  91.0 1.5 %shard_map.55 = (f32[1,24,768]{2,1,0:T(8,128)}, f32[1,24,768]{2,1,0:T(8,128)}) custom-call(bf16[8,240,128]{2,1,0:T(8,128)(2,1)S(1)} %all-to-all-done.2.refs_0_, bf16[176,768]{1,0:T(8,128)(2,1)S(1)} %get-tuple-element.53.refs_1_, bf16[176,768]{1,0:T(8,128)(2,1)S(1)} %collective-permute-done.6.refs_2_, bf16[176,768]{1,0:T(8,128)(2,1)S(1)} %collective-permute-done.1.refs_3_, ...), custom_call_target="tpu_custom_call" | custom-call | tf_op jit(solution)/shard_map/pallas_call | solution.py:370
  (31 shorter events, 7.0 us)
Async XLA Ops:
  2.0 13.8 %collective-permute-start = (bf16[24,12288]{1,0:T(8,128)(2,1)S(1)}, bf16[24,12288]{1,0:T(8,128)(2,1)S(1)}, u32[]{:S(2)}, u32[]{:S(2)}) collective-permute-start(bf16[24,12288]{1,0:T(8,128)(2,1)S(1)} %broadcast_select_fusion), channel_id=1, source_target_pairs={{0,0},{17,1},{34,2},{51,3},{68,4},{85,5},{102,6},{119,7},{136,8},{... | collective-permute-start | bytes 1769480 | tf_op jit(solution)/shard_map/ppermute | solution.py:402
  9.5 1.1 %copy-start = (bf16[1,24,12288]{2,1,0:T(8,128)(2,1)S(1)}, bf16[1,24,12288]{2,1,0:T(8,128)(2,1)}, u32[]{:S(2)}) copy-start(bf16[1,24,12288]{2,1,0:T(8,128)(2,1)} %param.5) | copy-start | bytes 1769476
  10.6 1.9 %copy-start.1 = (bf16[2,8,8,12288]{3,2,1,0:T(8,128)(2,1)S(1)}, bf16[2,8,8,12288]{3,2,1,0:T(8,128)(2,1)}, u32[]{:S(2)}) copy-start(bf16[2,8,8,12288]{3,2,1,0:T(8,128)(2,1)} %param.3) | copy-start | bytes 9437188
  12.4 1.1 %copy-start.2 = (bf16[1,24,12288]{2,1,0:T(8,128)(2,1)S(1)}, bf16[1,24,12288]{2,1,0:T(8,128)(2,1)}, u32[]{:S(2)}) copy-start(bf16[1,24,12288]{2,1,0:T(8,128)(2,1)} %param.4) | copy-start | bytes 1769476
  36.8 17.8 %all-to-all-start.1 = ((bf16[16,128,128]{2,1,0:T(8,128)(2,1)}), bf16[16,128,128]{2,1,0:T(8,128)(2,1)S(1)}, u32[]{:S(2)}, u32[]{:S(2)}) async-start(bf16[16,128,128]{2,1,0:T(8,128)(2,1)} %get-tuple-element.39), calls=%async_computation.1 | async-start | bytes 1048576 | tf_op jit(solution)/shard_map/all_to_all | solution.py:417
  44.8 15.7 %collective-permute-start.3 = (bf16[176,768]{1,0:T(8,128)(2,1)S(1)}, bf16[176,768]{1,0:T(8,128)(2,1)S(1)}, u32[]{:S(2)}, u32[]{:S(2)}) collective-permute-start(bf16[176,768]{1,0:T(8,128)(2,1)S(1)} %get-tuple-element.53.refs_1_), channel_id=1, source_target_pairs={{0,128},{16,144},{32,160},{48,176},{64,192},{80,208},{96,224},{112... | collective-permute-start | bytes 811016 | tf_op jit(solution)/shard_map/ppermute | solution.py:376
  46.1 14.4 %collective-permute-start.2 = (bf16[176,768]{1,0:T(8,128)(2,1)S(1)}, bf16[176,768]{1,0:T(8,128)(2,1)S(1)}, u32[]{:S(2)}, u32[]{:S(2)}) collective-permute-start(bf16[176,768]{1,0:T(8,128)(2,1)S(1)} %get-tuple-element.53.refs_1_), channel_id=1, source_target_pairs={{0,96},{16,112},{32,64},{48,80},{64,32},{80,48},{96,0},{112,16},{1... | collective-permute-start | bytes 811016 | tf_op jit(solution)/shard_map/ppermute | solution.py:376
  48.5 12.0 %collective-permute-start.1 = (bf16[176,768]{1,0:T(8,128)(2,1)S(1)}, bf16[176,768]{1,0:T(8,128)(2,1)S(1)}, u32[]{:S(2)}, u32[]{:S(2)}) collective-permute-start(bf16[176,768]{1,0:T(8,128)(2,1)S(1)} %get-tuple-element.53.refs_1_), channel_id=1, source_target_pairs={{0,32},{16,48},{32,0},{48,16},{64,96},{80,112},{96,64},{112,80},{1... | collective-permute-start | bytes 811016 | tf_op jit(solution)/shard_map/ppermute | solution.py:376
  48.5 17.3 %collective-permute-start.5 = (bf16[176,768]{1,0:T(8,128)(2,1)S(1)}, bf16[176,768]{1,0:T(8,128)(2,1)S(1)}, u32[]{:S(2)}, u32[]{:S(2)}) collective-permute-start(bf16[176,768]{1,0:T(8,128)(2,1)S(1)} %get-tuple-element.53.refs_1_), channel_id=1, source_target_pairs={{0,64},{16,80},{32,96},{48,112},{64,0},{80,16},{96,32},{112,48},{1... | collective-permute-start | bytes 811016 | tf_op jit(solution)/shard_map/ppermute | solution.py:376
  60.5 5.3 %collective-permute-start.4 = (bf16[192,128]{1,0:T(8,128)(2,1)S(1)}, bf16[192,128]{1,0:T(8,128)(2,1)S(1)}, u32[]{:S(2)}, u32[]{:S(2)}) collective-permute-start(bf16[192,128]{1,0:T(8,128)(2,1)S(1)} %shard_map.53.refs_0_), channel_id=1, source_target_pairs={{0,8},{1,9},{2,10},{3,11},{4,12},{5,13},{6,14},{7,15},{8,0},{9,1},... | collective-permute-start | bytes 147464 | tf_op jit(solution)/shard_map/ppermute | solution.py:376
  66.7 20.0 %all-to-all-start.2 = ((bf16[8,240,128]{2,1,0:T(8,128)(2,1)}), bf16[8,240,128]{2,1,0:T(8,128)(2,1)S(1)}, u32[]{:S(2)}, u32[]{:S(2)}) async-start(bf16[8,240,128]{2,1,0:T(8,128)(2,1)} %shard_map.54), calls=%async_computation.2 | async-start | bytes 983040 | tf_op jit(solution)/shard_map/all_to_all | solution.py:438
  70.5 4.7 %collective-permute-start.6 = (bf16[176,768]{1,0:T(8,128)(2,1)S(1)}, bf16[176,768]{1,0:T(8,128)(2,1)S(1)}, u32[]{:S(2)}, u32[]{:S(2)}) collective-permute-start(bf16[176,768]{1,0:T(8,128)(2,1)S(1)} %get-tuple-element.53.refs_1_), channel_id=1, source_target_pairs={{0,16},{16,0},{32,48},{48,32},{64,80},{80,64},{96,112},{112,96},{1... | collective-permute-start | bytes 811016 | tf_op jit(solution)/shard_map/ppermute | solution.py:376
  72.8 8.0 %collective-permute-start.10 = (bf16[176,768]{1,0:T(8,128)(2,1)S(1)}, bf16[176,768]{1,0:T(8,128)(2,1)S(1)}, u32[]{:S(2)}, u32[]{:S(2)}) collective-permute-start(bf16[176,768]{1,0:T(8,128)(2,1)S(1)} %collective-permute-done.5.refs_5_), channel_id=1, source_target_pairs={{0,128},{16,144},{32,160},{48,176},{64,192},{80,208},{96,224},{112... | collective-permute-start | bytes 811016 | tf_op jit(solution)/shard_map/ppermute | solution.py:376
  73.1 7.8 %collective-permute-start.8 = (bf16[176,768]{1,0:T(8,128)(2,1)S(1)}, bf16[176,768]{1,0:T(8,128)(2,1)S(1)}, u32[]{:S(2)}, u32[]{:S(2)}) collective-permute-start(bf16[176,768]{1,0:T(8,128)(2,1)S(1)} %collective-permute-done.2.refs_7_), channel_id=1, source_target_pairs={{0,16},{16,0},{32,48},{48,32},{64,80},{80,64},{96,112},{112,96},{1... | collective-permute-start | bytes 811016 | tf_op jit(solution)/shard_map/ppermute | solution.py:376
  73.5 9.1 %collective-permute-start.11 = (bf16[176,768]{1,0:T(8,128)(2,1)S(1)}, bf16[176,768]{1,0:T(8,128)(2,1)S(1)}, u32[]{:S(2)}, u32[]{:S(2)}) collective-permute-start(bf16[176,768]{1,0:T(8,128)(2,1)S(1)} %collective-permute-done.3.refs_9_), channel_id=1, source_target_pairs={{0,96},{16,112},{32,64},{48,80},{64,32},{80,48},{96,0},{112,16},{1... | collective-permute-start | bytes 811016 | tf_op jit(solution)/shard_map/ppermute | solution.py:376
  74.1 12.5 %collective-permute-start.9 = (bf16[176,768]{1,0:T(8,128)(2,1)S(1)}, bf16[176,768]{1,0:T(8,128)(2,1)S(1)}, u32[]{:S(2)}, u32[]{:S(2)}) collective-permute-start(bf16[176,768]{1,0:T(8,128)(2,1)S(1)} %collective-permute-done.1.refs_3_), channel_id=1, source_target_pairs={{0,128},{16,144},{32,160},{48,176},{64,192},{80,208},{96,224},{112... | collective-permute-start | bytes 811016 | tf_op jit(solution)/shard_map/ppermute | solution.py:376
  75.2 11.4 %collective-permute-start.7 = (bf16[176,768]{1,0:T(8,128)(2,1)S(1)}, bf16[176,768]{1,0:T(8,128)(2,1)S(1)}, u32[]{:S(2)}, u32[]{:S(2)}) collective-permute-start(bf16[176,768]{1,0:T(8,128)(2,1)S(1)} %collective-permute-done.1.refs_3_), channel_id=1, source_target_pairs={{0,16},{16,0},{32,48},{48,32},{64,80},{80,64},{96,112},{112,96},{1... | collective-permute-start | bytes 811016 | tf_op jit(solution)/shard_map/ppermute | solution.py:376
  86.7 2.8 %collective-permute-start.12 = (bf16[176,768]{1,0:T(8,128)(2,1)S(1)}, bf16[176,768]{1,0:T(8,128)(2,1)S(1)}, u32[]{:S(2)}, u32[]{:S(2)}) collective-permute-start(bf16[176,768]{1,0:T(8,128)(2,1)S(1)} %collective-permute-done.5.refs_5_), channel_id=1, source_target_pairs={{0,16},{16,0},{32,48},{48,32},{64,80},{80,64},{96,112},{112,96},{1... | collective-permute-start | bytes 811016 | tf_op jit(solution)/shard_map/ppermute | solution.py:376
  88.3 1.6 %collective-permute-start.13 = (bf16[176,768]{1,0:T(8,128)(2,1)S(1)}, bf16[176,768]{1,0:T(8,128)(2,1)S(1)}, u32[]{:S(2)}, u32[]{:S(2)}) collective-permute-start(bf16[176,768]{1,0:T(8,128)(2,1)S(1)} %collective-permute-done.3.refs_9_), channel_id=1, source_target_pairs={{0,16},{16,0},{32,48},{48,32},{64,80},{80,64},{96,112},{112,96},{1... | collective-permute-start | bytes 811016 | tf_op jit(solution)/shard_map/ppermute | solution.py:376
  88.3 1.9 %collective-permute-start.14 = (bf16[176,768]{1,0:T(8,128)(2,1)S(1)}, bf16[176,768]{1,0:T(8,128)(2,1)S(1)}, u32[]{:S(2)}, u32[]{:S(2)}) collective-permute-start(bf16[176,768]{1,0:T(8,128)(2,1)S(1)} %collective-permute-done.9.refs_11_), channel_id=1, source_target_pairs={{0,16},{16,0},{32,48},{48,32},{64,80},{80,64},{96,112},{112,96},{1... | collective-permute-start | bytes 811016 | tf_op jit(solution)/shard_map/ppermute | solution.py:376
  88.8 1.8 %collective-permute-start.15 = (bf16[176,768]{1,0:T(8,128)(2,1)S(1)}, bf16[176,768]{1,0:T(8,128)(2,1)S(1)}, u32[]{:S(2)}, u32[]{:S(2)}) collective-permute-start(bf16[176,768]{1,0:T(8,128)(2,1)S(1)} %collective-permute-done.10.refs_13_), channel_id=1, source_target_pairs={{0,16},{16,0},{32,48},{48,32},{64,80},{80,64},{96,112},{112,96},{1... | collective-permute-start | bytes 811016 | tf_op jit(solution)/shard_map/ppermute | solution.py:376
  88.8 2.2 %collective-permute-start.16 = (bf16[176,768]{1,0:T(8,128)(2,1)S(1)}, bf16[176,768]{1,0:T(8,128)(2,1)S(1)}, u32[]{:S(2)}, u32[]{:S(2)}) collective-permute-start(bf16[176,768]{1,0:T(8,128)(2,1)S(1)} %collective-permute-done.11.refs_15_), channel_id=1, source_target_pairs={{0,16},{16,0},{32,48},{48,32},{64,80},{80,64},{96,112},{112,96},{1... | collective-permute-start | bytes 811016 | tf_op jit(solution)/shard_map/ppermute | solution.py:376
